TPU v7x, 512 devices: a whole 4x4x16 slice. The times are simulated.
512 devices in a mesh: aper: 32 (over z_lo, x), band: 16 (over z_hi, y, core).
Axes of the slice: x: 4, y: 4, z: 16 (z_hi: 2, z_lo: 8; z = z_hi * 8 + z_lo), core: 2. Of those that a mesh axis runs over, the one named last changes fastest.
Arguments:
- pulse_data: bfloat16 [2, 4096, 8192], P(None, ('aper', 'band')), may hold values from -6 to 6
- window_start: int32 [4096, 16], P(('aper', 'band')), may hold values from 0 to 7680
- footprint: int32 [4096, 8], P(('aper', 'band')), may hold values from 0 to 15, all different within a row
- range_to_row_weight: bfloat16 [1024, 512], P('band'), may hold values from -0.25 to 0.25
- slow_taps: float32 [5], replicated, may hold values from 0.2 to 1
- ramp_rate: float32 [4096], replicated, may hold values from -0.5 to 0.5
- image_now: float32 [2, 1024, 8192], P(None, 'band', 'aper'), may hold values from -6 to 6
- step_and_variation_weight: float32 [2], replicated, may hold values from 0.5 to 1.5
Outputs:
- updated_image: float32 [2, 1024, 8192], P(None, 'band', 'aper')
Inputs may be any that keep to these rules, and one draw needn't show every extreme that they name: `window_start`: each pulse's window of 512 bins lies inside its 8192 range bins. `footprint`: each row lists 8 distinct bands; every band is lit by some pulse.
All inputs are finite; a program needn't handle non-finite values.
Results may differ from a plain program's by a relative error of at most 0.0031.
Values may be sent and summed in bfloat16 or wider, within the bound.
No kernel may reach another device: no remote copies, remote signals or barrier semaphores. Data moves between devices by JAX's collectives and lax.ppermute only.
A program may use at most 128 MiB of HBM per device.

v0:
```python
import math

import jax
import jax.numpy as jnp
from jax import lax
from jax.sharding import PartitionSpec as P

TAPS_K = 2


smooth_eps = 0.05


def extended(value, sides, width, wrap):
    for axis, dim in sides:
        size, length = (lax.axis_size(axis), value.shape[dim])
        up = [(i, (i + 1) % size) for i in range(size if wrap else size - 1)]
        down = [(j, i) for i, j in up]
        last = lax.slice_in_dim(value, length - width, length, axis=dim)
        leading = lax.slice_in_dim(value, 0, width, axis=dim)
        before = lax.ppermute(last, axis, up)
        after = lax.ppermute(leading, axis, down)
        value = jnp.concatenate([before, value, after], axis=dim)
    return value


def variation_term(padded):
    row_step = padded[:, 1:, :-1] - padded[:, :-1, :-1]
    col_step = padded[:, :-1, 1:] - padded[:, :-1, :-1]
    magnitude = jnp.sqrt(jnp.sum(row_step * row_step + col_step * col_step, axis=0) + smooth_eps)
    row_flow = row_step / magnitude
    col_flow = col_step / magnitude
    return -(
        row_flow[:, 1:, 1:] - row_flow[:, :-1, 1:] + col_flow[:, 1:, 1:] - col_flow[:, 1:, :-1]
    )


def column_products(blend_part, ramp_part, columns, band_rows):
    phase_angle = ramp_part[:, None] * columns[None, :]
    cos_table = jnp.cos(phase_angle).astype(jnp.bfloat16)
    sin_table = jnp.sin(phase_angle).astype(jnp.bfloat16)
    dims = (((0,), (0,)), ((), ()))
    cos_sum = lax.dot_general(cos_table, blend_part, dims, preferred_element_type=jnp.float32)
    sin_sum = lax.dot_general(sin_table, blend_part, dims, preferred_element_type=jnp.float32)
    real_part = cos_sum[:, :band_rows] - sin_sum[:, band_rows:]
    imag_part = sin_sum[:, :band_rows] + cos_sum[:, band_rows:]
    return jnp.concatenate([real_part, imag_part], axis=1)


def local(
    pulse_data,
    window_start,
    footprint,
    range_to_row_weight,
    slow_taps,
    ramp_rate,
    image_now,
    step_and_variation_weight,
):
    band_count = lax.axis_size("band")
    groups = lax.axis_size("aper")
    band_rows = range_to_row_weight.shape[0]
    window_len = range_to_row_weight.shape[1]
    band_ids = jnp.arange(band_count, dtype=jnp.int32)
    lit_mask = jnp.any(footprint[:, :, None] == band_ids[None, None, :], axis=1)

    def cut_pulse(pulse_rows, starts):
        return jax.vmap(
            lambda start_bin: lax.dynamic_slice_in_dim(pulse_rows, start_bin, window_len, 1)
        )(starts)

    fragment_list = jax.vmap(cut_pulse, in_axes=(1, 0))(pulse_data, window_start)
    fragment_list = (
        fragment_list * jnp.where(lit_mask, 1.0, 0.0).astype(jnp.bfloat16)[:, :, None, None]
    )
    incoming_block = lax.all_to_all(fragment_list, "band", split_axis=1, concat_axis=0, tiled=True)
    raised_output = jnp.einsum(
        "lfw,ew->lfe", incoming_block[:, 0], range_to_row_weight, preferred_element_type=jnp.float32
    ).astype(jnp.bfloat16)
    raised_output = raised_output.reshape(raised_output.shape[0], 2 * band_rows)
    group_pulses = raised_output.shape[0]
    padded = extended(raised_output, (("aper", 0),), TAPS_K, True)
    blended = jnp.zeros(raised_output.shape, jnp.float32)
    for offset in range(2 * TAPS_K + 1):
        blended = blended + slow_taps[offset] * padded[offset : offset + group_pulses].astype(
            jnp.float32
        )
    blended = blended.astype(jnp.bfloat16)
    cols_dev = image_now.shape[2]
    my_group = lax.axis_index("aper")
    columns = (my_group * cols_dev + jnp.arange(cols_dev, dtype=jnp.int32)).astype(jnp.float32)
    gradient = column_products(
        lax.all_gather(blended, "aper", axis=0, tiled=True), ramp_rate, columns, band_rows
    )
    gradient = gradient * (1.0 / math.sqrt(group_pulses * groups))
    gradient = gradient.reshape(cols_dev, 2, band_rows).transpose(1, 2, 0)
    padded_image = extended(image_now, (("band", 1), ("aper", 2)), 1, False)
    return image_now - step_and_variation_weight[0] * (
        gradient + step_and_variation_weight[1] * variation_term(padded_image)
    )


def solution(mesh):
    return jax.shard_map(
        local,
        mesh=mesh,
        in_specs=(
            P(None, ("aper", "band"), None),
            P(("aper", "band"), None),
            P(("aper", "band"), None),
            P("band", None),
            P(),
            P(),
            P(None, "band", "aper"),
            P(),
        ),
        out_specs=P(None, "band", "aper"),
        check_vma=False,
    )
```

profile of v0, /device:TPU:16, one launch (start us, length us, event | category | flops | bytes accessed | tf_op | source)
XLA Modules:
  0.0 364.2 jit_solution(5612659424560549962)
XLA Ops:
  6.5 0.0 copy-start
  6.5 0.0 copy-start.4
  6.5 0.0 all-gather.2.cloned.1.call-start
  6.5 14.0 %copy.14 = bf16[2,8,8192]{0,1,2:T(8,128)(2,1)} copy(bf16[2,8,8192]{2,1,0:T(8,128)(2,1)} %param.8) | data formatting | bytes 524288 | tf_op args[0]
  20.5 0.0 copy-done.4
  20.6 0.1 reshape.25
  20.6 48.7 %gather_fusion = bf16[128,2,512]{1,0,2:T(8,128)(2,1)} fusion(bf16[8,2,8192]{1,0,2:T(8,128)(2,1)} %bitcast.40, s32[128]{0:T(128)S(1)} %reshape.25), kind=kCustom, calls=%fused_computation | custom fusion | bytes 525824 | tf_op jit(solution)/shard_map/vmap(vmap())/gather | solution.py:69
  69.3 0.0 copy-start.3
  69.3 0.0 copy-start.2
  69.3 0.0 copy-start.1
  69.3 0.0 copy-start.5
  69.3 21.6 %copy.16 = bf16[8,16,2,512]{3,0,2,1:T(8,128)(2,1)S(1)} copy(bf16[8,16,2,512]{2,1,0,3:T(8,128)(2,1)} %bitcast.41) | data formatting | bytes 524288 | tf_op jit(solution)/shard_map/vmap(vmap())/gather | solution.py:69
  90.9 0.0 copy-done.3
  90.9 0.0 copy-start.6
  90.9 0.1 fusion.24
  91.0 0.1 copy.15
  91.1 0.1 broadcast_multiply_fusion
  91.2 32.2 %all_to_all.15 = bf16[8,16,2,512]{3,0,2,1:T(8,128)(2,1)S(1)} all-to-all(bf16[8,16,2,512]{3,0,2,1:T(8,128)(2,1)S(1)} %broadcast_multiply_fusion), channel_id=1, replica_groups=mesh['aper'=32,'band'=16] {'band'}, dimensions={1} | all-to-all | bytes 524288 | tf_op jit(solution)/shard_map/all_to_all | solution.py:76
  123.4 0.0 copy-done
  123.4 0.2 convolution_convert_fusion
  123.6 0.1 fusion.31
  123.7 7.6 %collective-permute-start.1 = (bf16[2,128]{0,1:T(8,128)(2,1)S(1)}, bf16[2,128]{0,1:T(8,128)(2,1)S(1)}, u32[]{:S(2)}, u32[]{:S(2)}) collective-permute-start(bf16[2,128]{0,1:T(8,128)(2,1)S(1)} %bitcast.44), channel_id=1, source_target_pairs={{16,0},{32,16},{48,32},{64,48},{80,64},{96,80},{112,96},{128,112},... | collective-permute-start | bytes 1544 | tf_op jit(solution)/shard_map/ppermute | solution.py:22
  131.3 1.9 collective-permute-start
  133.3 0.0 copy-done.2
  133.3 0.7 fusion.33
  133.9 0.0 collective-permute-done.1
  133.9 11.9 %collective-permute-done = bf16[2,128]{0,1:T(8,128)(2,1)S(1)} collective-permute-done((bf16[2,128]{0,1:T(8,128)(2,1)S(1)}, bf16[2,128]{0,1:T(8,128)(2,1)S(1)}, u32[]{:S(2)}, u32[]{:S(2)}) %collective-permute-start) | collective-permute-done | bytes 544 | tf_op jit(solution)/shard_map/ppermute | solution.py:21
  145.8 3.9 %add_convert_fusion = bf16[128,128]{0,1:T(8,128)(2,1)} fusion(bf16[128,128]{0,1:T(8,128)(2,1)S(1)} %bitcast.42, bf16[2,128]{0,1:T(8,128)(2,1)S(1)} %collective-permute-done.1, bf16[2,128]{0,1:T(8,128)(2,1)S(1)} %collective-permute-done, f32[]{:T(128)} %bitcast.15, f32[]{:T(128)} %bitcast.13, f32[]{:T(128)} %bitcast.12, f32[]{:T(128)} %bitcast.11, f32[]{:T(128)} %bitcast.1), kind=kLoop, calls=%fused_computation.45 | loop fusion | flops 442368 | bytes 66580 | tf_op jit(solution)/shard_map/convert_element_type | solution.py:88
  149.7 0.0 all-gather.2.cloned.1.call-update
  149.7 0.0 copy-done.1
  149.7 1.9 collective-permute-start.3
  151.7 2.4 collective-permute-start.2
  154.1 0.0 copy-done.5
  154.1 0.6 fusion.32
  154.7 0.0 collective-permute-done.3
  154.7 1.9 collective-permute-done.2
  156.6 0.1 fusion.29
  156.7 1.3 collective-permute-start.4
  158.0 1.5 collective-permute-start.5
  159.5 0.5 collective-permute-done.4
  159.9 0.1 maximum_maximum_fusion
  160.1 4.2 %collective-permute-done.5 = f32[2,66,1]{2,1,0:T(8,128)S(1)} collective-permute-done((f32[2,66,1]{2,1,0:T(8,128)S(1)}, f32[2,66,1]{2,1,0:T(8,128)S(1)}, u32[]{:S(2)}, u32[]{:S(2)}) %collective-permute-start.5) | collective-permute-done | bytes 560 | tf_op jit(solution)/shard_map/ppermute | solution.py:22
  164.2 0.1 add_reduce_fusion
  164.4 0.1 broadcast_divide_fusion.1
  164.5 154.1 %all-gather.2.cloned.1.call-done = bf16[4096,128]{0,1:T(8,128)(2,1)} async-done(((bf16[128,128]{0,1:T(8,128)(2,1)}), bf16[4096,128]{0,1:T(8,128)(2,1)}) %all-gather.2.cloned.1.call-update) | async-done | bytes 1048592 | tf_op jit(solution)/shard_map/all_gather | solution.py:93
  318.5 0.0 copy-done.6
  318.6 18.6 %fusion.2 = f32[256,128]{0,1:T(8,128)S(1)} fusion(bf16[4096,128]{0,1:T(8,128)(2,1)} %all-gather.2.cloned.1.call-done, f32[256]{0:T(256)S(1)} %add_convert_fusion.1, f32[4096]{0:T(1024)S(1)} %copy-done.6), kind=kOutput, calls=%fused_computation.5 | convolution fusion | flops 270532608 | bytes 1197056 | tf_op jit(solution)/shard_map/dot_general | solution.py:44
  337.2 18.1 %fusion.4 = f32[256,128]{0,1:T(8,128)S(1)} fusion(bf16[4096,128]{0,1:T(8,128)(2,1)} %all-gather.2.cloned.1.call-done, f32[256]{0:T(256)S(1)} %add_convert_fusion.1, f32[4096]{0:T(1024)S(1)} %copy-done.6), kind=kOutput, calls=%fused_computation.6 | convolution fusion | flops 270532608 | bytes 1197056 | tf_op jit(solution)/shard_map/dot_general | solution.py:43
  355.3 2.1 fusion.17
  (7 shorter events, 0.1 us)
Async XLA Ops:
  6.5 116.9 %copy-start = (bf16[64,512]{1,0:T(8,128)(2,1)S(1)}, bf16[64,512]{1,0:T(8,128)(2,1)}, u32[]{:S(2)}) copy-start(bf16[64,512]{1,0:T(8,128)(2,1)} %param.11) | copy-start | bytes 196612
  6.5 14.0 %copy-start.4 = (s32[8,16]{1,0:T(8,128)S(1)}, s32[8,16]{1,0:T(8,128)}, u32[]{:S(2)}) copy-start(s32[8,16]{1,0:T(8,128)} %param.9) | copy-start | bytes 1540
  6.5 312.0 %all-gather.2.cloned.1.call-start = ((), (), s32[]{:S(2)}) async-start(), calls=%async_computation.1 | async-start | bytes 1081344 | tf_op jit(solution)/shard_map/all_gather | solution.py:93
  69.3 21.6 %copy-start.3 = (s32[8,8]{1,0:T(8,128)S(1)}, s32[8,8]{1,0:T(8,128)}, u32[]{:S(2)}) copy-start(s32[8,8]{1,0:T(8,128)} %param.10) | copy-start | bytes 772
  69.3 64.0 %copy-start.2 = (f32[5]{0:T(128)S(1)}, f32[5]{0:T(128)}, u32[]{:S(2)}) copy-start(f32[5]{0:T(128)} %param.12) | copy-start | bytes 64
  69.3 80.4 %copy-start.1 = (f32[2,64,256]{2,1,0:T(8,128)S(1)}, f32[2,64,256]{2,1,0:T(8,128)}, u32[]{:S(2)}) copy-start(f32[2,64,256]{2,1,0:T(8,128)} %param.14) | copy-start | bytes 393220
  69.3 84.8 %copy-start.5 = (f32[2]{0:T(128)S(1)}, f32[2]{0:T(128)}, u32[]{:S(2)}) copy-start(f32[2]{0:T(128)} %param.15) | copy-start | bytes 28
  90.9 227.6 %copy-start.6 = (f32[4096]{0:T(1024)S(1)}, f32[4096]{0:T(1024)}, u32[]{:S(2)}) copy-start(f32[4096]{0:T(1024)} %param.13) | copy-start | bytes 49156
  123.7 10.2 %collective-permute-start.1 = (bf16[2,128]{0,1:T(8,128)(2,1)S(1)}, bf16[2,128]{0,1:T(8,128)(2,1)S(1)}, u32[]{:S(2)}, u32[]{:S(2)}) collective-permute-start(bf16[2,128]{0,1:T(8,128)(2,1)S(1)} %bitcast.44), channel_id=1, source_target_pairs={{16,0},{32,16},{48,32},{64,48},{80,64},{96,80},{112,96},{128,112},... | collective-permute-start | bytes 1544 | tf_op jit(solution)/shard_map/ppermute | solution.py:22
  131.3 14.5 %collective-permute-start = (bf16[2,128]{0,1:T(8,128)(2,1)S(1)}, bf16[2,128]{0,1:T(8,128)(2,1)S(1)}, u32[]{:S(2)}, u32[]{:S(2)}) collective-permute-start(bf16[2,128]{0,1:T(8,128)(2,1)S(1)} %bitcast.43), channel_id=1, source_target_pairs={{0,16},{16,32},{32,48},{48,64},{64,80},{80,96},{96,112},{112,128},... | collective-permute-start | bytes 1544 | tf_op jit(solution)/shard_map/ppermute | solution.py:21
  149.7 4.9 %collective-permute-start.3 = (f32[2,1,256]{2,1,0:T(1,128)S(1)}, f32[2,1,256]{2,1,0:T(1,128)S(1)}, u32[]{:S(2)}, u32[]{:S(2)}) collective-permute-start(f32[2,1,256]{2,1,0:T(1,128)S(1)} %get-tuple-element.12), channel_id=1, source_target_pairs={{1,0},{2,1},{3,2},{4,3},{5,4},{6,5},{7,6},{8,7},{9,8},{10,9},{11,1... | collective-permute-start | bytes 6152 | tf_op jit(solution)/shard_map/ppermute | solution.py:22
  151.7 4.9 %collective-permute-start.2 = (f32[2,1,256]{2,1,0:T(1,128)S(1)}, f32[2,1,256]{2,1,0:T(1,128)S(1)}, u32[]{:S(2)}, u32[]{:S(2)}) collective-permute-start(f32[2,1,256]{2,1,0:T(1,128)S(1)} %get-tuple-element.11), channel_id=1, source_target_pairs={{0,1},{1,2},{2,3},{3,4},{4,5},{5,6},{6,7},{7,8},{8,9},{9,10},{10,1... | collective-permute-start | bytes 6152 | tf_op jit(solution)/shard_map/ppermute | solution.py:21
  156.7 3.3 collective-permute-start.4
  158.0 6.2 %collective-permute-start.5 = (f32[2,66,1]{2,1,0:T(8,128)S(1)}, f32[2,66,1]{2,1,0:T(8,128)S(1)}, u32[]{:S(2)}, u32[]{:S(2)}) collective-permute-start(f32[2,66,1]{2,1,0:T(8,128)S(1)} %get-tuple-element.9), channel_id=1, source_target_pairs={{16,0},{32,16},{48,32},{64,48},{80,64},{96,80},{112,96},{128,112},... | collective-permute-start | bytes 1592 | tf_op jit(solution)/shard_map/ppermute | solution.py:22
Sparse Core Ops, SparseCore 0:
  149.8 168.6 all-gather.1
where the time goes:
time: 365 us; the launch traced here: 364 us
  waiting for transfers between devices  173 us (47%)
  local copies, waits for them, and re-layouts  85.9 us (24%)
  matrix products  36.9 us (10%)
  blocking collectives  32.2 us (9%)
  starting transfers between devices  16.6 us (5%)
  between operations  13.6 us (4%)
  other arithmetic  6.51 us (2%)
    all_gather x1, waiting for transfers between devices, local(): lax.all_gather(blended, 'aper', axis=0, tiled=True)  154 us
    gather x3, local copies, waits for them, and re-layouts, cut_pulse(): lax.dynamic_slice_in_dim(pulse_rows, start_bin, window_len, 1)  70.3 us
    all_to_all x1, blocking collectives, local(): lax.all_to_all(fragment_list, 'band', split_axis=1, concat_axis=0, tiled=...  32.2 us
    dot_general x1, matrix products, column_products(): lax.dot_general(sin_table, blend_part, dims, preferred_element_type=jnp.f...  18.6 us
    dot_general x1, matrix products, column_products(): lax.dot_general(cos_table, blend_part, dims, preferred_element_type=jnp.f...  18.1 us
    ppermute x3, waiting for transfers between devices, extended(): before = lax.ppermute(last, axis, up)  14.3 us
    unnamed x15, local copies, waits for them, and re-layouts  14 us
    ppermute x3, starting transfers between devices, extended(): after = lax.ppermute(leading, axis, down)  11 us
  transfers between devices with their start and end apart: 7, of which 5 were waited for; matrix products, arithmetic and copies ran while one was open for 0% of the time, Pallas kernels for 0%

commit v1 on v0

v1 whole, which is shorter than its diff:
```python
import math

import jax
import jax.numpy as jnp
from jax import lax
from jax.experimental import pallas as pl
from jax.experimental.pallas import tpu as pltpu
from jax.sharding import PartitionSpec as P

TAPS_K = 2
LANES = 128
EDGE = 8
Z_HI, Z_LO, N_X, N_YC = 2, 8, 4, 8
N_Z = Z_HI * Z_LO
smooth_eps = 0.05
BF16, F32 = jnp.bfloat16, jnp.float32
VMEM = pl.BlockSpec(memory_space=pltpu.VMEM)
SMEM = pl.BlockSpec(memory_space=pltpu.SMEM)


def device_index(z_hi, z_lo, x, yc):
    return ((z_lo * N_X + x) * Z_HI + z_hi) * N_YC + yc


def z_rings():
    return [
        [device_index(z // Z_LO, z % Z_LO, x, yc) for z in range(N_Z)]
        for x in range(N_X)
        for yc in range(N_YC)
    ]


def mirrored():
    return [
        (device_index(h, z, x, yc), device_index(1 - h, Z_LO - 1 - z, x, yc))
        for h in range(Z_HI)
        for z in range(Z_LO)
        for x in range(N_X)
        for yc in range(N_YC)
    ]


def extended(value, sides, width, wrap):
    for axis, dim in sides:
        size, length = (lax.axis_size(axis), value.shape[dim])
        up = [(i, (i + 1) % size) for i in range(size if wrap else size - 1)]
        down = [(j, i) for i, j in up]
        last = lax.slice_in_dim(value, length - width, length, axis=dim)
        leading = lax.slice_in_dim(value, 0, width, axis=dim)
        before = lax.ppermute(last, axis, up)
        after = lax.ppermute(leading, axis, down)
        value = jnp.concatenate([before, value, after], axis=dim)
    return value


def variation_term(padded):
    row_step = padded[:, 1:, :-1] - padded[:, :-1, :-1]
    col_step = padded[:, :-1, 1:] - padded[:, :-1, :-1]
    magnitude = jnp.sqrt(jnp.sum(row_step * row_step + col_step * col_step, axis=0) + smooth_eps)
    row_flow = row_step / magnitude
    col_flow = col_step / magnitude
    return -(
        row_flow[:, 1:, 1:] - row_flow[:, :-1, 1:] + col_flow[:, 1:, 1:] - col_flow[:, 1:, :-1]
    )


def cut_windows(start_ref, foot_ref, pulse_ref, out_ref, flat_ref, window_ref):
    comps, pulses, bins = pulse_ref.shape
    parts = bins // LANES
    pitch = comps * (parts + 1)
    block = out_ref.shape[0] * out_ref.shape[1] // (Z_HI * N_YC)
    for part in range(parts):
        for comp in range(comps):
            flat_ref[pl.ds(part * comps + comp, pulses, stride=pitch), :] = pulse_ref[
                comp, :, part * LANES : (part + 1) * LANES
            ].astype(F32)
    window_ref[...] = jnp.zeros_like(window_ref)
    lane = lax.broadcasted_iota(jnp.int32, (block // pulses, LANES), 1)
    for pulse in range(pulses):
        for k in range(foot_ref.shape[1]):
            band = foot_ref[pulse, k]
            start = start_ref[pulse, band]
            row = pulse * pitch + comps * (start // LANES)
            shift = start % LANES
            here = flat_ref[pl.ds(row, block // pulses), :]
            following = flat_ref[pl.ds(row + comps, block // pulses), :]
            both = jnp.where(lane >= shift, here, following)
            both = pltpu.roll(both, (LANES - shift) % LANES, 1)
            place = ((band % N_YC) * Z_HI + band // N_YC) * block + pulse
            window_ref[pl.ds(place, block // pulses, stride=pulses), :] = both
    out_ref[...] = window_ref[...].astype(BF16).reshape(out_ref.shape)


def lift_windows(where_ref, window_ref, own_ref, other_ref, out_ref):
    sources, height = window_ref.shape[:2]
    half = height // Z_HI
    parts = own_ref.shape[1] // LANES
    rows = half // parts
    band_rows = own_ref.shape[0]
    my_half = where_ref[0]
    dims = (((1,), (1,)), ((), ()))
    for weight_ref, z_half in ((own_ref, my_half), (other_ref, 1 - my_half)):
        lifted = jnp.zeros((sources * rows, band_rows), F32)
        for part in range(parts):
            first = pl.multiple_of(z_half * half + part * rows, rows)
            piece = window_ref[:, pl.ds(first, rows), :].reshape(sources * rows, LANES)
            lifted = lifted + lax.dot_general(
                piece,
                weight_ref[:, part * LANES : (part + 1) * LANES],
                dims,
                preferred_element_type=F32,
            )
        lifted = lifted.reshape(sources, 2, rows // 2, band_rows)
        both = jnp.concatenate([lifted[:, 0], lifted[:, 1]], axis=-1)
        both = both.reshape(sources * rows // 2, 2 * band_rows).astype(BF16)
        for z in range(Z_LO):
            out_ref[z_half * Z_LO + z] = both


def sin_cos(angle):
    turns = jnp.round(angle * (2.0 / math.pi))
    rest = angle - turns * 1.5703125
    rest = rest - turns * 4.837512969970703125e-4
    rest = rest - turns * 7.54978995489188216e-8
    square = rest * rest
    sine = -1.9515295891e-4 * square + 8.3321608736e-3
    sine = (sine * square - 1.6666654611e-1) * square * rest + rest
    cosine = 2.443315711809948e-5 * square - 1.388731625493765e-3
    cosine = (cosine * square + 4.166664568298827e-2) * square * square - 0.5 * square + 1.0
    quarter = turns.astype(jnp.int32) & 3
    swap = (quarter & 1) == 1
    sin_out = jnp.where(swap, cosine, sine)
    cos_out = jnp.where(swap, sine, cosine)
    sin_out = jnp.where(quarter >= 2, -sin_out, sin_out)
    cos_out = jnp.where((quarter == 1) | (quarter == 2), -cos_out, cos_out)
    return sin_out, cos_out


FINE = 16


def sum_pulses(
    where_ref, taps_ref, ramp_ref, lifted_ref, out_ref, table_ref, rate_ref, pad_ref, blend_ref, fine_ref, coarse_ref
):
    z_lo, x = where_ref[1], where_ref[2]
    n_groups = ramp_ref.shape[0]
    half_pulses, width = lifted_ref.shape[1:]
    main = Z_LO * LANES
    depth = main + LANES
    blocks, columns = out_ref.shape[:2]

    lane = lax.broadcasted_iota(jnp.int32, (1, LANES), 1)
    ends = jnp.zeros((1, LANES), F32)
    for i in range(Z_LO):
        group = i * N_X + x
        rate_ref[i : i + 1, :] = ramp_ref[pl.ds(group, 1), :]
        before = ramp_ref[pl.ds((group + n_groups - 1) % n_groups, 1), :]
        after = ramp_ref[pl.ds((group + 1) % n_groups, 1), :]
        place = 2 * EDGE * i
        move = (place + EDGE) % LANES
        before = pltpu.roll(before, move, 1) if move else before
        after = pltpu.roll(after, move, 1) if move else after
        ends = jnp.where((lane >= place) & (lane < place + EDGE), before, ends)
        ends = jnp.where((lane >= place + EDGE) & (lane < place + 2 * EDGE), after, ends)
    rate_ref[Z_LO : Z_LO + 1, :] = ends

    zero = jnp.zeros((2 * EDGE, width), F32)
    pad_ref[: 2 * EDGE] = zero
    pad_ref[2 * EDGE + LANES :] = zero
    for i in range(Z_LO):
        for h in range(Z_HI):
            pad_ref[pl.ds(2 * EDGE + h * half_pulses, half_pulses), :] = lifted_ref[
                h * Z_LO + i
            ].astype(F32)
        blended = jnp.zeros((LANES + 2 * EDGE, width), F32)
        for t in range(2 * TAPS_K + 1):
            blended = blended + taps_ref[t] * pad_ref[pl.ds(EDGE - TAPS_K + t, LANES + 2 * EDGE), :]
        turned = pltpu.roll(blended, width // 2, 1)
        lane_full = lax.broadcasted_iota(jnp.int32, blended.shape, 1)
        turned = jnp.where(lane_full < width // 2, -turned, turned)
        for k, value in enumerate((blended, turned)):
            value = value.astype(BF16)
            blend_ref[pl.ds(k * depth + i * LANES, LANES), :] = value[EDGE : EDGE + LANES]
            outside = jnp.concatenate([value[:EDGE], value[EDGE + LANES :]], axis=0)
            blend_ref[pl.ds(k * depth + main + i * 2 * EDGE, 2 * EDGE), :] = outside

    n_coarse = blocks * columns // FINE
    first = z_lo * (blocks * columns)
    fine_step = lax.broadcasted_iota(jnp.int32, (FINE, LANES), 0).astype(F32)
    coarse_step = (
        first + FINE * lax.broadcasted_iota(jnp.int32, (n_coarse, LANES), 0)
    ).astype(F32)
    for i in range(Z_LO + 1):
        rate = rate_ref[i : i + 1, :]
        fine_sin, fine_cos = sin_cos(rate * fine_step)
        coarse_sin, coarse_cos = sin_cos(rate * coarse_step)
        coarse_ref[0] = coarse_sin
        coarse_ref[1] = coarse_cos
        for a in range(n_coarse):
            s = coarse_ref[0, a : a + 1, :]
            c = coarse_ref[1, a : a + 1, :]
            table_ref[a * FINE : (a + 1) * FINE, i * LANES : (i + 1) * LANES] = (
                c * fine_cos - s * fine_sin
            ).astype(BF16)
            table_ref[a * FINE : (a + 1) * FINE, depth + i * LANES : depth + (i + 1) * LANES] = (
                s * fine_cos + c * fine_sin
            ).astype(BF16)

    for block in range(blocks):
        out_ref[block] = jnp.dot(
            table_ref[block * columns : (block + 1) * columns, :],
            blend_ref[...],
            preferred_element_type=F32,
        )


def finish(scale, step_ref, sums_ref, base_ref, out_ref):
    total = sums_ref[0]
    for k in range(1, sums_ref.shape[0]):
        total = total + sums_ref[k]
    total = total.T * (step_ref[0] * scale)
    out_ref[...] = base_ref[...] - total.reshape(out_ref.shape)


def call(kernel, out_shape, in_specs, args, scratch=(), out_specs=VMEM):
    return pl.pallas_call(
        kernel,
        out_shape=out_shape,
        in_specs=in_specs,
        out_specs=out_specs,
        scratch_shapes=scratch,
        compiler_params=pltpu.CompilerParams(vmem_limit_bytes=40 * 1024 * 1024),
    )(*args)


def local(
    pulse_data,
    window_start,
    footprint,
    range_to_row_weight,
    slow_taps,
    ramp_rate,
    image_now,
    step_and_variation_weight,
):
    band_count = lax.axis_size("band")
    groups = lax.axis_size("aper")
    comps, pulses, bins = pulse_data.shape
    band_rows, window_len = range_to_row_weight.shape
    columns = image_now.shape[2]
    group = lax.axis_index("aper")
    z_hi = lax.axis_index("band") // N_YC
    where = jnp.stack([z_hi, group // N_X, group % N_X]).astype(jnp.int32)

    other_weight = lax.ppermute(range_to_row_weight, ("aper", "band"), mirrored())
    parts = window_len // LANES
    block = parts * comps * pulses
    windows = call(
        cut_windows,
        jax.ShapeDtypeStruct((N_YC, Z_HI * block, LANES), BF16),
        [SMEM, SMEM, VMEM],
        (window_start, footprint, pulse_data),
        [
            pltpu.VMEM((pulses * comps * (bins // LANES + 1), LANES), F32),
            pltpu.VMEM((band_count * block, LANES), F32),
        ],
    )
    in_plane = [[h * N_YC + i for i in range(N_YC)] for h in range(Z_HI)]
    windows = lax.all_to_all(windows, "band", 0, 0, axis_index_groups=in_plane, tiled=True)
    width = comps * band_rows
    lifted = call(
        lift_windows,
        jax.ShapeDtypeStruct((N_Z, N_YC * pulses, width), BF16),
        [SMEM, VMEM, VMEM, VMEM],
        (where, windows, range_to_row_weight, other_weight),
    )
    lifted = lax.all_to_all(lifted, ("aper", "band"), 0, 0, axis_index_groups=z_rings(), tiled=True)
    depth = (Z_LO + 1) * LANES
    sums = call(
        sum_pulses,
        jax.ShapeDtypeStruct((N_X, columns, width), F32),
        [SMEM, SMEM, VMEM, VMEM],
        (where, slow_taps, ramp_rate.reshape(groups, LANES), lifted),
        [
            pltpu.VMEM((N_X * columns, 2 * depth), BF16),
            pltpu.VMEM((2 * EDGE, LANES), F32),
            pltpu.VMEM((LANES + 4 * EDGE, width), F32),
            pltpu.VMEM((2 * depth, width), BF16),
            pltpu.VMEM((FINE, LANES), F32),
            pltpu.VMEM((2, N_X * columns // FINE, LANES), F32),
        ],
    )
    along_x = [[z * N_X + x for x in range(N_X)] for z in range(Z_LO)]
    sums = lax.all_to_all(sums, "aper", 0, 0, axis_index_groups=along_x, tiled=True)

    padded_image = extended(image_now, (("band", 1), ("aper", 2)), 1, False)
    base = image_now - step_and_variation_weight[0] * (
        step_and_variation_weight[1] * variation_term(padded_image)
    )
    scale = 1.0 / math.sqrt(groups * LANES)
    return call(
        lambda *refs: finish(scale, *refs),
        jax.ShapeDtypeStruct(image_now.shape, F32),
        [SMEM, VMEM, VMEM],
        (step_and_variation_weight, sums, base),
    )


def solution(mesh):
    return jax.shard_map(
        local,
        mesh=mesh,
        in_specs=(
            P(None, ("aper", "band"), None),
            P(("aper", "band"), None),
            P(("aper", "band"), None),
            P("band", None),
            P(),
            P(),
            P(None, "band", "aper"),
            P(),
        ),
        out_specs=P(None, "band", "aper"),
        check_vma=False,
    )
```

time: 365 us -> 94.9 us (0.26)
  the two profiles are of different devices: /device:TPU:16 before, /device:TPU:25 now
where the time goes in v1:
time: 94.9 us; the launch traced here: 94.3 us
  starting transfers between devices  49.1 us (52%)
  waiting for transfers between devices  29.1 us (31%)
  Pallas kernels  10.3 us (11%)
  local copies, waits for them, and re-layouts  3.71 us (4%)
  other arithmetic  1.87 us (2%)
    ppermute x2, waiting for transfers between devices, extended(): after = lax.ppermute(leading, axis, down)  17.4 us
    ppermute x2, starting transfers between devices, extended(): before = lax.ppermute(last, axis, up)  16.9 us
    pallas_call x4, Pallas kernels, call(): pl.pallas_call(kernel, out_shape=out_shape, in_specs=in_specs, out_specs=...  10.3 us
    all_to_all x1, starting transfers between devices, local(): lax.all_to_all(windows, 'band', 0, 0, axis_index_groups=in_plane, tiled=T...  9.39 us
    all_to_all x1, starting transfers between devices, local(): lax.all_to_all(lifted, ('aper', 'band'), 0, 0, axis_index_groups=z_rings(...  7.97 us
    ppermute x1, starting transfers between devices, local(): lax.ppermute(range_to_row_weight, ('aper', 'band'), mirrored())  6.86 us
    ppermute x1, waiting for transfers between devices, local(): lax.ppermute(range_to_row_weight, ('aper', 'band'), mirrored())  6.28 us
    all_to_all x1, waiting for transfers between devices, local(): lax.all_to_all(sums, 'aper', 0, 0, axis_index_groups=along_x, tiled=True)  5.4 us
  transfers between devices with their start and end apart: 8, of which 4 were waited for; matrix products, arithmetic and copies ran while one was open for 3% of the time, Pallas kernels for 0%

profile of v1, /device:TPU:25, one launch (start us, length us, event | category | flops | bytes accessed | tf_op | source)
XLA Modules:
  0.0 94.3 jit_solution(2175137805744560476)
XLA Ops:
  0.0 0.0 copy-start
  0.0 0.9 %copy-done = bf16[2,8,8192]{2,1,0:T(8,128)(2,1)S(1)} copy-done((bf16[2,8,8192]{2,1,0:T(8,128)(2,1)S(1)}, bf16[2,8,8192]{2,1,0:T(8,128)(2,1)}, u32[]{:S(2)}) %copy-start) | copy-done | bytes 262168
  1.0 0.0 copy-start.4
  1.0 0.7 copy-done.4
  1.6 0.0 copy-start.5
  1.6 0.7 copy-done.5
  2.3 2.5 %shard_map.82 = bf16[8,128,128]{2,1,0:T(8,128)(2,1)} custom-call(s32[8,16]{1,0:T(8,128)S(1)} %copy-done.4, s32[8,8]{1,0:T(8,128)S(1)} %copy-done.5, bf16[2,8,8192]{2,1,0:T(8,128)(2,1)S(1)} %copy-done), custom_call_target="tpu_custom_call" | custom-call | tf_op jit(solution)/shard_map/pallas_call | solution.py:226
  4.9 0.0 copy-start.1
  4.9 9.4 %all-to-all-start = ((bf16[8,128,128]{2,1,0:T(8,128)(2,1)}), bf16[8,128,128]{2,1,0:T(8,128)(2,1)S(1)}, u32[]{:S(2)}, u32[]{:S(2)}) async-start(bf16[8,128,128]{2,1,0:T(8,128)(2,1)} %shard_map.82), calls=%async_computation | async-start | bytes 524288 | tf_op jit(solution)/shard_map/all_to_all | solution.py:269
  14.2 0.0 copy-done.1
  14.2 6.9 %collective-permute-start = (bf16[64,512]{1,0:T(8,128)(2,1)S(1)}, bf16[64,512]{1,0:T(8,128)(2,1)S(1)}, u32[]{:S(2)}, u32[]{:S(2)}) collective-permute-start(bf16[64,512]{1,0:T(8,128)(2,1)S(1)} %copy-done.1), channel_id=1, source_target_pairs={{0,456},{1,457},{2,458},{3,459},{4,460},{5,461},{6,462},{7,463},{1... | collective-permute-start | bytes 196616 | tf_op jit(solution)/shard_map/ppermute | solution.py:255
  21.1 0.1 pad_add_fusion.where_ref
  21.2 6.3 %collective-permute-done.other_ref = bf16[64,512]{1,0:T(8,128)(2,1)S(1)} collective-permute-done((bf16[64,512]{1,0:T(8,128)(2,1)S(1)}, bf16[64,512]{1,0:T(8,128)(2,1)S(1)}, u32[]{:S(2)}, u32[]{:S(2)}) %collective-permute-start) | collective-permute-done | bytes 65568 | tf_op jit(solution)/shard_map/ppermute | solution.py:255
  27.5 0.0 all-to-all-done.window_ref
  27.5 1.5 %shard_map.83 = bf16[16,64,128]{2,1,0:T(8,128)(2,1)} custom-call(s32[3]{0:T(128)S(1)} %pad_add_fusion.where_ref, bf16[8,128,128]{2,1,0:T(8,128)(2,1)S(1)} %all-to-all-done.window_ref, bf16[64,512]{1,0:T(8,128)(2,1)S(1)} %copy-done.1, bf16[64,512]{1,0:T(8,128)(2,1)S(1)} %collective-permute-done.other_ref), custom_call_target="tpu_custom_call" | custom-call | tf_op jit(solution)/shard_map/pallas_call | solution.py:226
  29.0 0.0 copy-start.7
  29.0 8.0 %all-to-all-start.1 = ((bf16[16,64,128]{2,1,0:T(8,128)(2,1)}), bf16[16,64,128]{2,1,0:T(8,128)(2,1)S(1)}, u32[]{:S(2)}, u32[]{:S(2)}) async-start(bf16[16,64,128]{2,1,0:T(8,128)(2,1)} %shard_map.83), calls=%async_computation.1 | async-start | bytes 524288 | tf_op jit(solution)/shard_map/all_to_all | solution.py:277
  37.0 0.0 copy-done.7
  37.0 13.6 %collective-permute-start.1 = (f32[2,1,256]{2,1,0:T(1,128)S(1)}, f32[2,1,256]{2,1,0:T(1,128)S(1)}, u32[]{:S(2)}, u32[]{:S(2)}) collective-permute-start(f32[2,1,256]{2,1,0:T(1,128)S(1)} %get-tuple-element.9), channel_id=1, source_target_pairs={{0,1},{1,2},{2,3},{3,4},{4,5},{5,6},{6,7},{7,8},{8,9},{9,10},{10,1... | collective-permute-start | bytes 6152 | tf_op jit(solution)/shard_map/ppermute | solution.py:50
  50.7 1.9 %collective-permute-start.2 = (f32[2,1,256]{2,1,0:T(1,128)S(1)}, f32[2,1,256]{2,1,0:T(1,128)S(1)}, u32[]{:S(2)}, u32[]{:S(2)}) collective-permute-start(f32[2,1,256]{2,1,0:T(1,128)S(1)} %get-tuple-element.10), channel_id=1, source_target_pairs={{1,0},{2,1},{3,2},{4,3},{5,4},{6,5},{7,6},{8,7},{9,8},{10,9},{11,1... | collective-permute-start | bytes 6152 | tf_op jit(solution)/shard_map/ppermute | solution.py:51
  52.6 0.0 collective-permute-done.1
  52.6 13.8 %collective-permute-done.2 = f32[2,1,256]{2,1,0:T(1,128)S(1)} collective-permute-done((f32[2,1,256]{2,1,0:T(1,128)S(1)}, f32[2,1,256]{2,1,0:T(1,128)S(1)}, u32[]{:S(2)}, u32[]{:S(2)}) %collective-permute-start.2) | collective-permute-done | bytes 2080 | tf_op jit(solution)/shard_map/ppermute | solution.py:51
  66.4 0.1 fusion.5
  66.5 0.0 copy-start.3
  66.5 3.2 %collective-permute-start.3 = (f32[2,66,1]{2,1,0:T(8,128)S(1)}, f32[2,66,1]{2,1,0:T(8,128)S(1)}, u32[]{:S(2)}, u32[]{:S(2)}) collective-permute-start(f32[2,66,1]{2,1,0:T(8,128)S(1)} %get-tuple-element.8), channel_id=1, source_target_pairs={{0,16},{16,32},{32,48},{48,64},{64,80},{80,96},{96,112},{112,128},... | collective-permute-start | bytes 1592 | tf_op jit(solution)/shard_map/ppermute | solution.py:50
  69.8 0.0 copy-done.3
  69.8 0.6 fusion.7
  70.4 1.3 %collective-permute-start.4 = (f32[2,66,1]{2,1,0:T(8,128)S(1)}, f32[2,66,1]{2,1,0:T(8,128)S(1)}, u32[]{:S(2)}, u32[]{:S(2)}) collective-permute-start(f32[2,66,1]{2,1,0:T(8,128)S(1)} %get-tuple-element.7), channel_id=1, source_target_pairs={{16,0},{32,16},{48,32},{64,48},{80,64},{96,80},{112,96},{128,112},... | collective-permute-start | bytes 1592 | tf_op jit(solution)/shard_map/ppermute | solution.py:51
  71.7 0.0 collective-permute-done.3
  71.7 0.1 maximum_maximum_fusion
  71.8 3.6 %collective-permute-done.4 = f32[2,66,1]{2,1,0:T(8,128)S(1)} collective-permute-done((f32[2,66,1]{2,1,0:T(8,128)S(1)}, f32[2,66,1]{2,1,0:T(8,128)S(1)}, u32[]{:S(2)}, u32[]{:S(2)}) %collective-permute-start.4) | collective-permute-done | bytes 560 | tf_op jit(solution)/shard_map/ppermute | solution.py:51
  75.5 0.1 add_reduce_fusion
  75.6 0.0 copy-start.2
  75.6 0.0 copy-start.6
  75.6 0.0 all-to-all-done.1.lifted_ref
  75.7 0.6 copy-done.2
  76.3 0.0 copy-done.6
  76.3 4.9 %shard_map.84 = f32[4,256,128]{2,1,0:T(8,128)} custom-call(s32[3]{0:T(128)S(1)} %pad_add_fusion.where_ref, f32[5]{0:T(128)S(1)} %copy-done.6, f32[32,128]{1,0:T(8,128)S(1)} %bitcast.6, bf16[16,64,128]{2,1,0:T(8,128)(2,1)S(1)} %all-to-all-done.1.lifted_ref), custom_call_target="tpu_custom_call" | custom-call | tf_op jit(solution)/shard_map/pallas_call | solution.py:226
  81.2 4.9 %all-to-all-start.2 = ((f32[4,256,128]{2,1,0:T(8,128)}), f32[4,256,128]{2,1,0:T(8,128)S(1)}, u32[]{:S(2)}, u32[]{:S(2)}) async-start(f32[4,256,128]{2,1,0:T(8,128)} %shard_map.84), calls=%async_computation.2 | async-start | bytes 1048576 | tf_op jit(solution)/shard_map/all_to_all | solution.py:294
  86.0 0.1 broadcast_divide_fusion.1
  86.1 1.4 %fusion.4.refs_2_ = f32[2,64,256]{2,1,0:T(8,128)S(1)} fusion(f32[2,64,256]{2,1,0:T(8,128)S(1)} %copy-done.7, f32[2,65,257]{2,1,0:T(8,128)S(1)} %get-tuple-element.6, f32[2,65,257]{2,1,0:T(8,128)S(1)} %get-tuple-element.5, f32[]{:T(128)} %bitcast.5, f32[]{:T(128)} %bitcast.4), kind=kLoop, calls=%fused_computation.12 | loop fusion | flops 229376 | bytes 786440 | tf_op jit(solution)/shard_map/sub | solution.py:297
  87.6 5.4 %all-to-all-done.2.refs_1_ = f32[4,256,128]{2,1,0:T(8,128)S(1)} async-done(((f32[4,256,128]{2,1,0:T(8,128)}), f32[4,256,128]{2,1,0:T(8,128)S(1)}, u32[]{:S(2)}, u32[]{:S(2)}) %all-to-all-start.2) | async-done | bytes 524320 | tf_op jit(solution)/shard_map/all_to_all | solution.py:294
  93.0 1.3 %shard_map.85 = f32[2,64,256]{2,1,0:T(8,128)} custom-call(f32[2]{0:T(128)S(1)} %copy-done.3, f32[4,256,128]{2,1,0:T(8,128)S(1)} %all-to-all-done.2.refs_1_, f32[2,64,256]{2,1,0:T(8,128)S(1)} %fusion.4.refs_2_), custom_call_target="tpu_custom_call" | custom-call | tf_op jit(solution)/shard_map/pallas_call | solution.py:226
  (3 shorter events, 0.1 us)
Async XLA Ops:
  0.0 0.9 %copy-start = (bf16[2,8,8192]{2,1,0:T(8,128)(2,1)S(1)}, bf16[2,8,8192]{2,1,0:T(8,128)(2,1)}, u32[]{:S(2)}) copy-start(bf16[2,8,8192]{2,1,0:T(8,128)(2,1)} %pulse_ref.1) | copy-start | bytes 786436
  1.0 0.7 copy-start.4
  1.6 0.7 copy-start.5
  4.9 9.4 %copy-start.1 = (bf16[64,512]{1,0:T(8,128)(2,1)S(1)}, bf16[64,512]{1,0:T(8,128)(2,1)}, u32[]{:S(2)}) copy-start(bf16[64,512]{1,0:T(8,128)(2,1)} %own_ref.1) | copy-start | bytes 196612
  4.9 22.6 %all-to-all-start = ((bf16[8,128,128]{2,1,0:T(8,128)(2,1)}), bf16[8,128,128]{2,1,0:T(8,128)(2,1)S(1)}, u32[]{:S(2)}, u32[]{:S(2)}) async-start(bf16[8,128,128]{2,1,0:T(8,128)(2,1)} %shard_map.82), calls=%async_computation | async-start | bytes 524288 | tf_op jit(solution)/shard_map/all_to_all | solution.py:269
  14.2 13.3 %collective-permute-start = (bf16[64,512]{1,0:T(8,128)(2,1)S(1)}, bf16[64,512]{1,0:T(8,128)(2,1)S(1)}, u32[]{:S(2)}, u32[]{:S(2)}) collective-permute-start(bf16[64,512]{1,0:T(8,128)(2,1)S(1)} %copy-done.1), channel_id=1, source_target_pairs={{0,456},{1,457},{2,458},{3,459},{4,460},{5,461},{6,462},{7,463},{1... | collective-permute-start | bytes 196616 | tf_op jit(solution)/shard_map/ppermute | solution.py:255
  29.0 8.0 %copy-start.7 = (f32[2,64,256]{2,1,0:T(8,128)S(1)}, f32[2,64,256]{2,1,0:T(8,128)}, u32[]{:S(2)}) copy-start(f32[2,64,256]{2,1,0:T(8,128)} %param.14) | copy-start | bytes 393220
  29.0 46.6 %all-to-all-start.1 = ((bf16[16,64,128]{2,1,0:T(8,128)(2,1)}), bf16[16,64,128]{2,1,0:T(8,128)(2,1)S(1)}, u32[]{:S(2)}, u32[]{:S(2)}) async-start(bf16[16,64,128]{2,1,0:T(8,128)(2,1)} %shard_map.83), calls=%async_computation.1 | async-start | bytes 524288 | tf_op jit(solution)/shard_map/all_to_all | solution.py:277
  37.0 15.6 %collective-permute-start.1 = (f32[2,1,256]{2,1,0:T(1,128)S(1)}, f32[2,1,256]{2,1,0:T(1,128)S(1)}, u32[]{:S(2)}, u32[]{:S(2)}) collective-permute-start(f32[2,1,256]{2,1,0:T(1,128)S(1)} %get-tuple-element.9), channel_id=1, source_target_pairs={{0,1},{1,2},{2,3},{3,4},{4,5},{5,6},{6,7},{7,8},{8,9},{9,10},{10,1... | collective-permute-start | bytes 6152 | tf_op jit(solution)/shard_map/ppermute | solution.py:50
  50.7 15.7 %collective-permute-start.2 = (f32[2,1,256]{2,1,0:T(1,128)S(1)}, f32[2,1,256]{2,1,0:T(1,128)S(1)}, u32[]{:S(2)}, u32[]{:S(2)}) collective-permute-start(f32[2,1,256]{2,1,0:T(1,128)S(1)} %get-tuple-element.10), channel_id=1, source_target_pairs={{1,0},{2,1},{3,2},{4,3},{5,4},{6,5},{7,6},{8,7},{9,8},{10,9},{11,1... | collective-permute-start | bytes 6152 | tf_op jit(solution)/shard_map/ppermute | solution.py:51
  66.5 3.3 %copy-start.3 = (f32[2]{0:T(128)S(1)}, f32[2]{0:T(128)}, u32[]{:S(2)}) copy-start(f32[2]{0:T(128)} %refs_0_.1) | copy-start | bytes 28
  66.5 5.2 %collective-permute-start.3 = (f32[2,66,1]{2,1,0:T(8,128)S(1)}, f32[2,66,1]{2,1,0:T(8,128)S(1)}, u32[]{:S(2)}, u32[]{:S(2)}) collective-permute-start(f32[2,66,1]{2,1,0:T(8,128)S(1)} %get-tuple-element.8), channel_id=1, source_target_pairs={{0,16},{16,32},{32,48},{48,64},{64,80},{80,96},{96,112},{112,128},... | collective-permute-start | bytes 1592 | tf_op jit(solution)/shard_map/ppermute | solution.py:50
  70.4 5.1 %collective-permute-start.4 = (f32[2,66,1]{2,1,0:T(8,128)S(1)}, f32[2,66,1]{2,1,0:T(8,128)S(1)}, u32[]{:S(2)}, u32[]{:S(2)}) collective-permute-start(f32[2,66,1]{2,1,0:T(8,128)S(1)} %get-tuple-element.7), channel_id=1, source_target_pairs={{16,0},{32,16},{48,32},{64,48},{80,64},{96,80},{112,96},{128,112},... | collective-permute-start | bytes 1592 | tf_op jit(solution)/shard_map/ppermute | solution.py:51
  75.6 0.7 copy-start.2
  75.6 0.7 copy-start.6
  81.2 11.8 %all-to-all-start.2 = ((f32[4,256,128]{2,1,0:T(8,128)}), f32[4,256,128]{2,1,0:T(8,128)S(1)}, u32[]{:S(2)}, u32[]{:S(2)}) async-start(f32[4,256,128]{2,1,0:T(8,128)} %shard_map.84), calls=%async_computation.2 | async-start | bytes 1048576 | tf_op jit(solution)/shard_map/all_to_all | solution.py:294

commit v2 on v1

v2 whole, which is shorter than its diff:
```python
import math

import jax
import jax.numpy as jnp
from jax import lax
from jax.experimental import pallas as pl
from jax.experimental.pallas import tpu as pltpu
from jax.sharding import PartitionSpec as P

TAPS_K = 2
LANES = 128
EDGE = 8
Z_HI, Z_LO, N_X, N_YC = 2, 8, 4, 8
N_Z = Z_HI * Z_LO
smooth_eps = 0.05
BF16, F32 = jnp.bfloat16, jnp.float32
VMEM = pl.BlockSpec(memory_space=pltpu.VMEM)
SMEM = pl.BlockSpec(memory_space=pltpu.SMEM)
ANY = pl.BlockSpec(memory_space=pl.ANY)


def device_index(z_hi, z_lo, x, yc):
    return ((z_lo * N_X + x) * Z_HI + z_hi) * N_YC + yc


def z_rings():
    return [
        [device_index(z // Z_LO, z % Z_LO, x, yc) for z in range(N_Z)]
        for x in range(N_X)
        for yc in range(N_YC)
    ]


def halves_swapped():
    return [
        (device_index(h, z, x, yc), device_index(1 - h, (z + Z_LO // 2) % Z_LO, x, yc))
        for h in range(Z_HI)
        for z in range(Z_LO)
        for x in range(N_X)
        for yc in range(N_YC)
    ]


def place_of():
    group, band = lax.axis_index("aper"), lax.axis_index("band")
    return band // N_YC, group // N_X, group % N_X, band % N_YC


def three_parts(value, spare_ref):
    first = value.astype(BF16).astype(F32)
    second = (value - first).astype(BF16).astype(F32)
    spare_ref[0:4] = first
    spare_ref[4:8] = second
    spare_ref[8:12] = value - first - second
    spare_ref[12:16] = jnp.zeros_like(value)
    return spare_ref[...].astype(BF16)


def joined(rows):
    rows = rows.astype(F32)
    return rows[0:4] + rows[4:8] + rows[8:12]


TOP, LOW = EDGE - 1, EDGE + 64


def with_corners(columns, above, below):
    lane = lax.broadcasted_iota(jnp.int32, columns.shape, 1)
    row = lax.broadcasted_iota(jnp.int32, columns.shape, 0)
    above = pltpu.roll(above, TOP, 1)
    below = pltpu.roll(below, (LOW + 1) % LANES, 1)
    for comp in range(2):
        columns = jnp.where((lane == TOP) & (row == comp), above[2 * comp : 2 * comp + 1], columns)
        columns = jnp.where(
            (lane == LOW) & (row == 2 + comp), below[2 * comp + 1 : 2 * comp + 2], columns
        )
    return columns


def cut_windows(
    start_hbm,
    foot_hbm,
    pulse_hbm,
    image_hbm,
    out_ref,
    start_ref,
    foot_ref,
    pulse_ref,
    edge_ref,
    flat_ref,
    window_ref,
    spare_ref,
    sem,
):
    rows = image_hbm.shape[1]
    copies = [
        pltpu.make_async_copy(pulse_hbm, pulse_ref, sem.at[0]),
        pltpu.make_async_copy(start_hbm, start_ref, sem.at[1]),
        pltpu.make_async_copy(foot_hbm, foot_ref, sem.at[2]),
        pltpu.make_async_copy(image_hbm.at[:, pl.ds(0, EDGE), :], edge_ref.at[0], sem.at[3]),
        pltpu.make_async_copy(image_hbm.at[:, pl.ds(rows - EDGE, EDGE), :], edge_ref.at[1], sem.at[4]),
    ]
    for copy in copies:
        copy.start()
    window_ref[...] = jnp.zeros_like(window_ref)
    comps, pulses, bins = pulse_ref.shape
    parts = bins // LANES
    pitch = comps * (parts + 1)
    block = window_ref.shape[0] // (Z_HI * N_YC)
    for copy in copies:
        copy.wait()
    for part in range(parts):
        for comp in range(comps):
            flat_ref[pl.ds(part * comps + comp, pulses, stride=pitch), :] = pulse_ref[
                comp, :, part * LANES : (part + 1) * LANES
            ].astype(F32)
    lane = lax.broadcasted_iota(jnp.int32, (block // pulses, LANES), 1)
    for pulse in range(pulses):
        for k in range(foot_ref.shape[1]):
            band = foot_ref[pulse, k]
            start = start_ref[pulse, band]
            row = pulse * pitch + comps * (start >> 7)
            shift = start & (LANES - 1)
            here = flat_ref[pl.ds(row, block // pulses), :]
            following = flat_ref[pl.ds(row + comps, block // pulses), :]
            both = jnp.where(lane >= shift, here, following)
            both = pltpu.roll(both, (LANES - shift) & (LANES - 1), 1)
            place = ((band & (N_YC - 1)) * Z_HI + (band >> 3)) * block + pulse
            window_ref[pl.ds(place, block // pulses, stride=pulses), :] = both
    tall = Z_HI * block
    out_ref[:, :tall, :] = window_ref[...].astype(BF16).reshape(N_YC, tall, LANES)
    out_ref[:, tall:, :] = jnp.zeros((N_YC, 2 * EDGE, LANES), BF16)
    yc = place_of()[3]
    for side, line, to in ((0, 0, yc + N_YC - 1), (1, EDGE - 1, yc + 1)):
        edge = [edge_ref[side, comp, line : line + 1, :] for comp in range(comps)]
        edge = [e[:, i * LANES : (i + 1) * LANES] for e in edge for i in range(2)]
        out_ref[to % N_YC, tall:, :] = three_parts(jnp.concatenate(edge, axis=0), spare_ref)


def side_columns(image_ref, out_ref, pad_ref):
    rows, columns = image_ref.shape[1:]
    pad_ref[...] = jnp.zeros_like(pad_ref)
    out_ref[...] = jnp.zeros_like(out_ref)
    for comp in range(2):
        for side, line in ((0, 0), (1, LANES - 1)):
            pad_ref[EDGE : EDGE + rows, :] = image_ref[
                comp, :, side * (columns - LANES) : side * (columns - LANES) + LANES
            ]
            out_ref[2 * side + comp : 2 * side + comp + 1, :] = pad_ref[...].T[line : line + 1, :]


def lift_windows(
    window_ref, own_ref, other_ref, column_ref, out_ref, edge_ref, spare_ref
):
    z_hi, _, _, yc = place_of()
    sources, height = window_ref.shape[0], window_ref.shape[1] - 2 * EDGE
    half = height // Z_HI
    parts = own_ref.shape[1] // LANES
    rows = half // parts
    band_rows = own_ref.shape[0]
    tall = sources * rows // 2

    above = joined(window_ref[(yc + N_YC - 1) % N_YC, height:, :])
    below = joined(window_ref[(yc + 1) % N_YC, height:, :])
    foreign = jnp.where(yc == 0, above, below)
    above = jnp.where(yc > 0, above, jnp.zeros_like(above))
    below = jnp.where(yc < N_YC - 1, below, jnp.zeros_like(below))
    edge_ref[0:4] = above
    edge_ref[4:8] = below
    columns = with_corners(column_ref[0:4], above, below)

    dims = (((1,), (1,)), ((), ()))
    for weight_ref, z_half, extra in ((own_ref, z_hi, columns), (other_ref, 1 - z_hi, foreign)):
        lifted = jnp.zeros((sources * rows, band_rows), F32)
        for part in range(parts):
            first = pl.multiple_of(z_half * half + part * rows, rows)
            piece = window_ref[:, pl.ds(first, rows), :].reshape(sources * rows, LANES)
            lifted = lifted + lax.dot_general(
                piece,
                weight_ref[:, part * LANES : (part + 1) * LANES],
                dims,
                preferred_element_type=F32,
            )
        lifted = lifted.reshape(sources, 2, rows // 2, band_rows)
        both = jnp.concatenate([lifted[:, 0], lifted[:, 1]], axis=-1)
        both = both.reshape(tall, 2 * band_rows).astype(BF16)
        extra = three_parts(extra, spare_ref)
        for z in range(Z_LO):
            out_ref[z_half * Z_LO + z, :tall, :] = both
            out_ref[z_half * Z_LO + z, tall:, :] = extra


def sin_cos(angle):
    turns = jnp.round(angle * (2.0 / math.pi))
    rest = angle - turns * 1.5703125
    rest = rest - turns * 4.837512969970703125e-4
    rest = rest - turns * 7.54978995489188216e-8
    square = rest * rest
    sine = -1.9515295891e-4 * square + 8.3321608736e-3
    sine = (sine * square - 1.6666654611e-1) * square * rest + rest
    cosine = 2.443315711809948e-5 * square - 1.388731625493765e-3
    cosine = (cosine * square + 4.166664568298827e-2) * square * square - 0.5 * square + 1.0
    quarter = turns.astype(jnp.int32) & 3
    swap = (quarter & 1) == 1
    sin_out = jnp.where(swap, cosine, sine)
    cos_out = jnp.where(swap, sine, cosine)
    sin_out = jnp.where(quarter >= 2, -sin_out, sin_out)
    cos_out = jnp.where((quarter == 1) | (quarter == 2), -cos_out, cos_out)
    return sin_out, cos_out


FINE = 16


def make_table(after_ref, ramp_ref, taps_ref, table_ref, tap_rows_ref, rate_ref, coarse_ref):
    del after_ref
    _, z_lo, x, _ = place_of()
    n_groups = ramp_ref.shape[0]
    depth = table_ref.shape[1] // 2
    for t in range(2 * TAPS_K + 1):
        tap_rows_ref[t : t + 1, :] = jnp.full((1, LANES), taps_ref[t], F32)

    lane = lax.broadcasted_iota(jnp.int32, (1, LANES), 1)
    ends = jnp.zeros((1, LANES), F32)
    for i in range(Z_LO):
        group = i * N_X + x
        rate_ref[i : i + 1, :] = ramp_ref[pl.ds(group, 1), :]
        before = ramp_ref[pl.ds((group + n_groups - 1) % n_groups, 1), :]
        after = ramp_ref[pl.ds((group + 1) % n_groups, 1), :]
        place = 2 * EDGE * i
        move = (place + EDGE) % LANES
        before = pltpu.roll(before, move, 1) if move else before
        after = pltpu.roll(after, move, 1) if move else after
        ends = jnp.where((lane >= place) & (lane < place + EDGE), before, ends)
        ends = jnp.where((lane >= place + EDGE) & (lane < place + 2 * EDGE), after, ends)
    rate_ref[Z_LO : Z_LO + 1, :] = ends

    n_coarse = table_ref.shape[0] // FINE
    first = z_lo * table_ref.shape[0]
    fine_step = lax.broadcasted_iota(jnp.int32, (FINE, LANES), 0).astype(F32)
    coarse_step = (
        first + FINE * lax.broadcasted_iota(jnp.int32, (n_coarse, LANES), 0)
    ).astype(F32)
    for i in range(Z_LO + 1):
        rate = rate_ref[i : i + 1, :]
        fine_sin, fine_cos = sin_cos(rate * fine_step)
        coarse_sin, coarse_cos = sin_cos(rate * coarse_step)
        coarse_ref[0] = coarse_sin
        coarse_ref[1] = coarse_cos
        for a in range(n_coarse):
            s = coarse_ref[0, a : a + 1, :]
            c = coarse_ref[1, a : a + 1, :]
            table_ref[a * FINE : (a + 1) * FINE, i * LANES : (i + 1) * LANES] = (
                c * fine_cos - s * fine_sin
            ).astype(BF16)
            table_ref[a * FINE : (a + 1) * FINE, depth + i * LANES : depth + (i + 1) * LANES] = (
                s * fine_cos + c * fine_sin
            ).astype(BF16)


def sum_pulses(
    tap_rows_ref, table_ref, lifted_ref, column_ref, edge_ref, out_ref, edge_out_ref, pad_ref, blend_ref
):
    z_hi, z_lo, x, yc = place_of()
    width = lifted_ref.shape[2]
    half_pulses = LANES // Z_HI
    main = Z_LO * LANES
    depth = main + LANES
    blocks, columns = out_ref.shape[0], out_ref.shape[1] - EDGE

    zero = jnp.zeros((2 * EDGE, width), F32)
    pad_ref[: 2 * EDGE] = zero
    pad_ref[2 * EDGE + LANES :] = zero
    for i in range(Z_LO):
        for h in range(Z_HI):
            pad_ref[pl.ds(2 * EDGE + h * half_pulses, half_pulses), :] = lifted_ref[
                h * Z_LO + i, :half_pulses, :
            ].astype(F32)
        blended = jnp.zeros((LANES + 2 * EDGE, width), F32)
        for t in range(2 * TAPS_K + 1):
            blended = blended + tap_rows_ref[t : t + 1, :] * pad_ref[
                pl.ds(EDGE - TAPS_K + t, LANES + 2 * EDGE), :
            ]
        turned = pltpu.roll(blended, width // 2, 1)
        lane_full = lax.broadcasted_iota(jnp.int32, blended.shape, 1)
        turned = jnp.where(lane_full < width // 2, -turned, turned)
        for k, value in enumerate((blended, turned)):
            value = value.astype(BF16)
            blend_ref[pl.ds(k * depth + i * LANES, LANES), :] = value[EDGE : EDGE + LANES]
            outside = jnp.concatenate([value[:EDGE], value[EDGE + LANES :]], axis=0)
            blend_ref[pl.ds(k * depth + main + i * 2 * EDGE, 2 * EDGE), :] = outside

    for block in range(blocks):
        out_ref[block, :columns, :] = jnp.dot(
            table_ref[block * columns : (block + 1) * columns, :],
            blend_ref[...],
            preferred_element_type=F32,
        )

    def came(half, z):
        return joined(lifted_ref[half * Z_LO + z % Z_LO, half_pulses:, :])

    first_band = (z_hi == 1) & (yc == 0)
    last_band = (z_hi == 0) & (yc == N_YC - 1)
    foreign = came(1 - z_hi, z_lo)
    above = jnp.where(first_band, foreign, edge_ref[0:4])
    below = jnp.where(last_band, foreign, edge_ref[4:8])
    edge_out_ref[0:4] = above
    edge_out_ref[4:8] = below
    own = with_corners(column_ref[0:4], above, below)
    left = came(z_hi, z_lo + Z_LO - 1)
    left_fixed = with_corners(left, above, came(1 - z_hi, z_lo + Z_LO - 1))
    left = jnp.where(last_band, left_fixed, left)
    right = came(z_hi, z_lo + 1)
    right_fixed = with_corners(right, came(1 - z_hi, z_lo + 1), below)
    right = jnp.where(first_band, right_fixed, right)
    out_ref[:, columns:, :] = jnp.zeros((blocks, EDGE, LANES), F32)
    out_ref[(x + 1) % N_X, columns : columns + 2, :] = jnp.where(x < N_X - 1, own, left)[2:4]
    out_ref[(x + N_X - 1) % N_X, columns : columns + 2, :] = jnp.where(x > 0, own, right)[0:2]


def finish(scale, step_ref, sums_ref, edge_ref, image_ref, out_ref, pad_ref, side_ref, flow_ref):
    _, z_lo, x, _ = place_of()
    group = z_lo * N_X + x
    comps, rows, columns = image_ref.shape
    tall = pad_ref.shape[1]
    total = sums_ref[0, :columns, :]
    for k in range(1, N_X):
        total = total + sums_ref[k, :columns, :]
    total = total.T.reshape(image_ref.shape) * scale

    zero = jnp.zeros((2, LANES), F32)
    left = sums_ref[(x + N_X - 1) % N_X, columns : columns + 2, :]
    right = sums_ref[(x + 1) % N_X, columns : columns + 2, :]
    side_ref[...] = jnp.zeros_like(side_ref)
    side_ref[0:2, :] = jnp.where(group > 0, left, zero)
    side_ref[2:4, :] = jnp.where(group < Z_LO * N_X - 1, right, zero)
    sides = side_ref[...].T[:tall]
    lane = lax.broadcasted_iota(jnp.int32, (tall, LANES), 1)
    blank = jnp.zeros((tall, LANES), F32)
    pad_ref[...] = jnp.zeros_like(pad_ref)
    for comp in range(comps):
        pad_ref[comp, EDGE : EDGE + rows, LANES : LANES + columns] = image_ref[comp]
        for half in range(2):
            span = pl.ds((1 + half) * LANES, LANES)
            pad_ref[comp, TOP : TOP + 1, span] = edge_ref[2 * comp + half : 2 * comp + half + 1, :]
            pad_ref[comp, LOW : LOW + 1, span] = edge_ref[4 + 2 * comp + half : 5 + 2 * comp + half, :]
        pad_ref[comp, :, :LANES] = jnp.where(lane == LANES - 1, sides[:, comp : comp + 1], blank)
        pad_ref[comp, :, LANES + columns :] = jnp.where(
            lane == 0, sides[:, 2 + comp : 3 + comp], blank
        )

    high, wide = rows + EDGE, columns + LANES
    row_step, col_step = [], []
    square = jnp.zeros((high, wide), F32) + smooth_eps
    for comp in range(comps):
        here = pad_ref[comp, :high, :]
        following = pltpu.roll(here, here.shape[1] - 1, 1)[:, :wide]
        here = here[:, :wide]
        row_step.append(pad_ref[comp, 1 : high + 1, :wide] - here)
        col_step.append(following - here)
        square = square + row_step[-1] * row_step[-1] + col_step[-1] * col_step[-1]
    inverse = lax.rsqrt(square)
    step, weight = step_ref[0], step_ref[1]
    for comp in range(comps):
        row_flow = row_step[comp] * inverse
        col_flow = col_step[comp] * inverse
        flow_ref[...] = row_flow
        across = col_flow - pltpu.roll(col_flow, 1, 1)
        down = row_flow[EDGE:, LANES:] - flow_ref[EDGE - 1 : high - 1, LANES:]
        variation = -(down + across[EDGE:, LANES:])
        out_ref[comp] = image_ref[comp] - step * (total[comp] + weight * variation)


def call(kernel, out_shape, in_specs, args, scratch=(), cost=None):
    out_specs = jax.tree.map(lambda _: VMEM, out_shape)
    return pl.pallas_call(
        kernel,
        out_shape=out_shape,
        in_specs=in_specs,
        out_specs=out_specs,
        scratch_shapes=scratch,
        cost_estimate=cost,
        compiler_params=pltpu.CompilerParams(vmem_limit_bytes=16 * 1024 * 1024),
    )(*args)


def local(
    pulse_data,
    window_start,
    footprint,
    range_to_row_weight,
    slow_taps,
    ramp_rate,
    image_now,
    step_and_variation_weight,
):
    band_count = lax.axis_size("band")
    groups = lax.axis_size("aper")
    comps, pulses, bins = pulse_data.shape
    band_rows, window_len = range_to_row_weight.shape
    columns = image_now.shape[2]
    shape = jax.ShapeDtypeStruct

    other_weight = lax.ppermute(range_to_row_weight, ("aper", "band"), halves_swapped())
    block = window_len // LANES * comps * pulses
    windows = call(
        cut_windows,
        shape((N_YC, Z_HI * block + 2 * EDGE, LANES), BF16),
        [ANY, ANY, ANY, ANY],
        (window_start, footprint, pulse_data, image_now),
        [
            pltpu.SMEM(window_start.shape, jnp.int32),
            pltpu.SMEM(footprint.shape, jnp.int32),
            pltpu.VMEM(pulse_data.shape, BF16),
            pltpu.VMEM((2, comps, EDGE, columns), F32),
            pltpu.VMEM((pulses * comps * (bins // LANES + 1), LANES), F32),
            pltpu.VMEM((band_count * block, LANES), F32),
            pltpu.VMEM((2 * EDGE, LANES), F32),
            pltpu.SemaphoreType.DMA((5,)),
        ],
    )
    in_plane = [[h * N_YC + i for i in range(N_YC)] for h in range(Z_HI)]
    windows = lax.all_to_all(windows, "band", 0, 0, axis_index_groups=in_plane, tiled=True)
    side = call(
        side_columns,
        shape((EDGE, LANES), F32),
        [VMEM],
        (image_now,),
        [pltpu.VMEM((LANES, LANES), F32)],
        pl.CostEstimate(flops=1 << 20, bytes_accessed=1 << 17, transcendentals=0),
    )
    width = comps * band_rows
    lifted, edges = call(
        lift_windows,
        (
            shape((N_Z, N_YC * pulses + 2 * EDGE, width), BF16),
            shape((EDGE, LANES), F32),
        ),
        [VMEM, VMEM, VMEM, VMEM],
        (windows, range_to_row_weight, other_weight, side),
        [pltpu.VMEM((2 * EDGE, LANES), F32)],
    )
    lifted = lax.all_to_all(lifted, ("aper", "band"), 0, 0, axis_index_groups=z_rings(), tiled=True)
    depth = (Z_LO + 1) * LANES
    table, tap_rows = call(
        make_table,
        (shape((N_X * columns, 2 * depth), BF16), shape((EDGE, LANES), F32)),
        [ANY, VMEM, SMEM],
        (edges, ramp_rate.reshape(groups, LANES), slow_taps),
        [
            pltpu.VMEM((2 * EDGE, LANES), F32),
            pltpu.VMEM((2, N_X * columns // FINE, LANES), F32),
        ],
        pl.CostEstimate(flops=1 << 24, bytes_accessed=1 << 23, transcendentals=0),
    )
    sums, edges = call(
        sum_pulses,
        (shape((N_X, columns + EDGE, width), F32), shape((EDGE, LANES), F32)),
        [VMEM, VMEM, VMEM, VMEM, VMEM],
        (tap_rows, table, lifted, side, edges),
        [
            pltpu.VMEM((LANES + 4 * EDGE, width), F32),
            pltpu.VMEM((2 * depth, width), BF16),
        ],
    )
    along_x = [[z * N_X + x for x in range(N_X)] for z in range(Z_LO)]
    sums = lax.all_to_all(sums, "aper", 0, 0, axis_index_groups=along_x, tiled=True)
    scale = 1.0 / math.sqrt(groups * LANES)
    return call(
        lambda *refs: finish(scale, *refs),
        shape(image_now.shape, F32),
        [SMEM, VMEM, VMEM, VMEM],
        (step_and_variation_weight, sums, edges, image_now),
        [
            pltpu.VMEM((comps, band_rows + 2 * EDGE, columns + 2 * LANES), F32),
            pltpu.VMEM((LANES, LANES), F32),
            pltpu.VMEM((band_rows + EDGE, columns + LANES), F32),
        ],
    )


def solution(mesh):
    return jax.shard_map(
        local,
        mesh=mesh,
        in_specs=(
            P(None, ("aper", "band"), None),
            P(("aper", "band"), None),
            P(("aper", "band"), None),
            P("band", None),
            P(),
            P(),
            P(None, "band", "aper"),
            P(),
        ),
        out_specs=P(None, "band", "aper"),
        check_vma=False,
    )
```

time: 94.9 us -> 79.2 us (0.83)
  the two profiles are of different devices: /device:TPU:25 before, /device:TPU:8 now
where the time goes in v2:
time: 79.2 us; the launch traced here: 78.6 us
  starting transfers between devices  26.9 us (34%)
  waiting for transfers between devices  19.6 us (25%)
  blocking collectives  12.3 us (16%)
  local copies, waits for them, and re-layouts  10.8 us (14%)
  Pallas kernels  8.82 us (11%)
    all_to_all x1, waiting for transfers between devices, local(): lax.all_to_all(lifted, ('aper', 'band'), 0, 0, axis_index_groups=z_rings(...  14.4 us
    all_to_all x1, blocking collectives, local(): lax.all_to_all(sums, 'aper', 0, 0, axis_index_groups=along_x, tiled=True)  12.3 us
    unnamed x24, local copies, waits for them, and re-layouts  10.8 us
    all_to_all x1, starting transfers between devices, local(): lax.all_to_all(lifted, ('aper', 'band'), 0, 0, axis_index_groups=z_rings(...  9.3 us
    all_to_all x1, starting transfers between devices, local(): lax.all_to_all(windows, 'band', 0, 0, axis_index_groups=in_plane, tiled=T...  9.16 us
    pallas_call x6, Pallas kernels, call(): pl.pallas_call(kernel, out_shape=out_shape, in_specs=in_specs, out_specs=...  8.82 us
    ppermute x1, starting transfers between devices, local(): lax.ppermute(range_to_row_weight, ('aper', 'band'), halves_swapped())  8.49 us
    ppermute x1, waiting for transfers between devices, local(): lax.ppermute(range_to_row_weight, ('aper', 'band'), halves_swapped())  5.2 us
  transfers between devices with their start and end apart: 3, of which 2 were waited for; matrix products, arithmetic and copies ran while one was open for 0% of the time, Pallas kernels for 3%

profile of v2, /device:TPU:8, one launch (start us, length us, event | category | flops | bytes accessed | tf_op | source)
XLA Modules:
  0.0 78.6 jit_solution(16741855531513977928)
XLA Ops:
  0.0 0.0 copy-start.2
  0.0 0.9 %copy-done.2 = f32[2,64,256]{2,1,0:T(8,128)S(1)} copy-done((f32[2,64,256]{2,1,0:T(8,128)S(1)}, f32[2,64,256]{2,1,0:T(8,128)}, u32[]{:S(2)}) %copy-start.2) | copy-done | bytes 131096
  0.9 0.0 copy-start.5
  0.9 0.9 %copy-done.5 = bf16[2,8,8192]{2,1,0:T(8,128)(2,1)S(1)} copy-done((bf16[2,8,8192]{2,1,0:T(8,128)(2,1)S(1)}, bf16[2,8,8192]{2,1,0:T(8,128)(2,1)}, u32[]{:S(2)}) %copy-start.5) | copy-done | bytes 262168
  1.9 0.0 copy-start.7
  1.9 0.7 copy-done.7
  2.5 0.0 copy-start.8
  2.5 0.7 copy-done.8
  3.2 0.0 copy-start.4
  3.2 0.0 copy-start.9
  3.2 1.9 %shard_map.82 = bf16[8,144,128]{2,1,0:T(8,128)(2,1)} custom-call(s32[8,16]{1,0:T(8,128)S(1)} %copy-done.7, s32[8,8]{1,0:T(8,128)S(1)} %copy-done.8, bf16[2,8,8192]{2,1,0:T(8,128)(2,1)S(1)} %copy-done.5, f32[2,64,256]{2,1,0:T(8,128)S(1)} %copy-done.2), custom_call_target="tpu_custom_call" | custom-call | tf_op jit(solution)/shard_map/pallas_call | solution.py:377
  5.1 9.2 %all-to-all-start = ((bf16[8,144,128]{2,1,0:T(8,128)(2,1)}), bf16[8,144,128]{2,1,0:T(8,128)(2,1)S(1)}, u32[]{:S(2)}, u32[]{:S(2)}) async-start(bf16[8,144,128]{2,1,0:T(8,128)(2,1)} %shard_map.82), calls=%async_computation | async-start | bytes 589824 | tf_op jit(solution)/shard_map/all_to_all | solution.py:424
  14.3 8.5 %collective-permute-start = (bf16[64,512]{1,0:T(8,128)(2,1)}, bf16[64,512]{1,0:T(8,128)(2,1)S(1)}, u32[]{:S(2)}, u32[]{:S(2)}) collective-permute-start(bf16[64,512]{1,0:T(8,128)(2,1)} %own_ref.1), channel_id=1, source_target_pairs={{0,264},{1,265},{2,266},{3,267},{4,268},{5,269},{6,270},{7,271},{1... | collective-permute-start | bytes 196616 | tf_op jit(solution)/shard_map/ppermute | solution.py:405
  22.8 0.0 copy-start.3
  22.8 0.9 %copy-done.3 = f32[2,64,256]{2,1,0:T(8,128)S(1)} copy-done((f32[2,64,256]{2,1,0:T(8,128)S(1)}, f32[2,64,256]{2,1,0:T(8,128)}, u32[]{:S(2)}) %copy-start.3) | copy-done | bytes 131096
  23.7 0.1 shard_map.83.column_ref
  23.8 5.2 %collective-permute-done.other_ref = bf16[64,512]{1,0:T(8,128)(2,1)S(1)} collective-permute-done((bf16[64,512]{1,0:T(8,128)(2,1)}, bf16[64,512]{1,0:T(8,128)(2,1)S(1)}, u32[]{:S(2)}, u32[]{:S(2)}) %collective-permute-start) | collective-permute-done | bytes 65568 | tf_op jit(solution)/shard_map/ppermute | solution.py:405
  29.0 0.0 all-to-all-done.window_ref
  29.0 0.0 copy-start.6
  29.0 0.8 %copy-done.6 = bf16[64,512]{1,0:T(8,128)(2,1)S(1)} copy-done((bf16[64,512]{1,0:T(8,128)(2,1)S(1)}, bf16[64,512]{1,0:T(8,128)(2,1)}, u32[]{:S(2)}) %copy-start.6) | copy-done | bytes 65560
  29.9 1.0 %shard_map.84 = (bf16[16,80,128]{2,1,0:T(8,128)(2,1)}, f32[8,128]{1,0:T(8,128)S(1)}) custom-call(bf16[8,144,128]{2,1,0:T(8,128)(2,1)S(1)} %all-to-all-done.window_ref, bf16[64,512]{1,0:T(8,128)(2,1)S(1)} %copy-done.6, bf16[64,512]{1,0:T(8,128)(2,1)S(1)} %collective-permute-done.other_ref, f32[8,128]{1,0:T(8,128)S(1)} %shard_map.83.column_ref), custom_call_target="tpu_custom_call" | custom-call | tf_op jit(solution)/shard_map/pallas_call | solution.py:377
  30.9 9.3 %all-to-all-start.1 = ((bf16[16,80,128]{2,1,0:T(8,128)(2,1)}), bf16[16,80,128]{2,1,0:T(8,128)(2,1)S(1)}, u32[]{:S(2)}, u32[]{:S(2)}) async-start(bf16[16,80,128]{2,1,0:T(8,128)(2,1)} %get-tuple-element.14), calls=%async_computation.1 | async-start | bytes 655360 | tf_op jit(solution)/shard_map/all_to_all | solution.py:444
  40.2 0.0 copy-start.10
  40.2 0.7 copy-done.10
  40.9 0.0 copy-start.11
  40.9 0.7 copy-done.11
  41.6 2.4 %shard_map.85 = (bf16[1024,2304]{1,0:T(8,128)(2,1)S(1)}, f32[8,128]{1,0:T(8,128)S(1)}) custom-call(f32[8,128]{1,0:T(8,128)S(1)} %get-tuple-element.11.after_ref.edge_ref, f32[32,128]{1,0:T(8,128)S(1)} %bitcast.1, f32[5]{0:T(128)S(1)} %copy-done.11), custom_call_target="tpu_custom_call" | custom-call | flops 16777216 | bytes 8388608 | tf_op jit(solution)/shard_map/pallas_call | solution.py:377
  44.0 0.0 copy-start
  44.0 2.1 %copy-done = bf16[1024,2304]{1,0:T(8,128)(2,1)} copy-done((bf16[1024,2304]{1,0:T(8,128)(2,1)}, bf16[1024,2304]{1,0:T(8,128)(2,1)S(1)}, u32[]{:S(2)}) %copy-start) | copy-done | bytes 4718616
  46.1 14.4 %all-to-all-done.1.lifted_ref = bf16[16,80,128]{2,1,0:T(8,128)(2,1)S(1)} async-done(((bf16[16,80,128]{2,1,0:T(8,128)(2,1)}), bf16[16,80,128]{2,1,0:T(8,128)(2,1)S(1)}, u32[]{:S(2)}, u32[]{:S(2)}) %all-to-all-start.1) | async-done | bytes 327712 | tf_op jit(solution)/shard_map/all_to_all | solution.py:444
  60.6 0.0 copy-start.1
  60.6 2.3 %copy-done.1 = bf16[1024,2304]{1,0:T(8,128)(2,1)S(1)} copy-done((bf16[1024,2304]{1,0:T(8,128)(2,1)S(1)}, bf16[1024,2304]{1,0:T(8,128)(2,1)}, u32[]{:S(2)}) %copy-start.1) | copy-done | bytes 4718616
  62.9 1.7 %shard_map.86 = (f32[4,264,128]{2,1,0:T(8,128)S(1)}, f32[8,128]{1,0:T(8,128)S(1)}) custom-call(f32[8,128]{1,0:T(8,128)S(1)} %get-tuple-element.12.tap_rows_ref, bf16[1024,2304]{1,0:T(8,128)(2,1)S(1)} %copy-done.1, bf16[16,80,128]{2,1,0:T(8,128)(2,1)S(1)} %all-to-all-done.1.lifted_ref, f32[8,128]{1,0:T(8,128)S(1)} %shard_map.83.column_ref, ...), custom_call_target="tpu_custom_call" | custom-call | tf_op jit(solution)/shard_map/pallas_call | solution.py:377
  64.6 12.3 %all_to_all.15.refs_1_ = f32[4,264,128]{2,1,0:T(8,128)S(1)} all-to-all(f32[4,264,128]{2,1,0:T(8,128)S(1)} %get-tuple-element.15), channel_id=1, replica_groups={{0,16,32,48},{64,80,96,112},{128,144,160,176},{192,208,224,240},{256,27..., dimensions={0} | all-to-all | bytes 1081344 | tf_op jit(solution)/shard_map/all_to_all | solution.py:468
  76.9 0.0 copy-done.4
  76.9 0.0 copy-done.9
  76.9 1.7 %shard_map.87 = f32[2,64,256]{2,1,0:T(8,128)} custom-call(f32[2]{0:T(128)S(1)} %copy-done.9, f32[4,264,128]{2,1,0:T(8,128)S(1)} %all_to_all.15.refs_1_, f32[8,128]{1,0:T(8,128)S(1)} %get-tuple-element.16.refs_2_, f32[2,64,256]{2,1,0:T(8,128)S(1)} %copy-done.4), custom_call_target="tpu_custom_call" | custom-call | tf_op jit(solution)/shard_map/pallas_call | solution.py:377
Async XLA Ops:
  0.0 0.9 %copy-start.2 = (f32[2,64,256]{2,1,0:T(8,128)S(1)}, f32[2,64,256]{2,1,0:T(8,128)}, u32[]{:S(2)}) copy-start(f32[2,64,256]{2,1,0:T(8,128)} %refs_3_.1) | copy-start | bytes 393220
  0.9 0.9 %copy-start.5 = (bf16[2,8,8192]{2,1,0:T(8,128)(2,1)S(1)}, bf16[2,8,8192]{2,1,0:T(8,128)(2,1)}, u32[]{:S(2)}) copy-start(bf16[2,8,8192]{2,1,0:T(8,128)(2,1)} %pulse_hbm.1) | copy-start | bytes 786436
  1.9 0.7 copy-start.7
  2.5 0.7 copy-start.8
  3.2 73.7 %copy-start.4 = (f32[2,64,256]{2,1,0:T(8,128)S(1)}, f32[2,64,256]{2,1,0:T(8,128)}, u32[]{:S(2)}) copy-start(f32[2,64,256]{2,1,0:T(8,128)} %refs_3_.1) | copy-start | bytes 393220
  3.2 73.7 %copy-start.9 = (f32[2]{0:T(128)S(1)}, f32[2]{0:T(128)}, u32[]{:S(2)}) copy-start(f32[2]{0:T(128)} %refs_0_.1) | copy-start | bytes 28
  5.1 23.9 %all-to-all-start = ((bf16[8,144,128]{2,1,0:T(8,128)(2,1)}), bf16[8,144,128]{2,1,0:T(8,128)(2,1)S(1)}, u32[]{:S(2)}, u32[]{:S(2)}) async-start(bf16[8,144,128]{2,1,0:T(8,128)(2,1)} %shard_map.82), calls=%async_computation | async-start | bytes 589824 | tf_op jit(solution)/shard_map/all_to_all | solution.py:424
  14.3 14.7 %collective-permute-start = (bf16[64,512]{1,0:T(8,128)(2,1)}, bf16[64,512]{1,0:T(8,128)(2,1)S(1)}, u32[]{:S(2)}, u32[]{:S(2)}) collective-permute-start(bf16[64,512]{1,0:T(8,128)(2,1)} %own_ref.1), channel_id=1, source_target_pairs={{0,264},{1,265},{2,266},{3,267},{4,268},{5,269},{6,270},{7,271},{1... | collective-permute-start | bytes 196616 | tf_op jit(solution)/shard_map/ppermute | solution.py:405
  22.8 0.9 %copy-start.3 = (f32[2,64,256]{2,1,0:T(8,128)S(1)}, f32[2,64,256]{2,1,0:T(8,128)}, u32[]{:S(2)}) copy-start(f32[2,64,256]{2,1,0:T(8,128)} %refs_3_.1) | copy-start | bytes 393220
  29.0 0.8 %copy-start.6 = (bf16[64,512]{1,0:T(8,128)(2,1)S(1)}, bf16[64,512]{1,0:T(8,128)(2,1)}, u32[]{:S(2)}) copy-start(bf16[64,512]{1,0:T(8,128)(2,1)} %own_ref.1) | copy-start | bytes 196612
  30.9 29.7 %all-to-all-start.1 = ((bf16[16,80,128]{2,1,0:T(8,128)(2,1)}), bf16[16,80,128]{2,1,0:T(8,128)(2,1)S(1)}, u32[]{:S(2)}, u32[]{:S(2)}) async-start(bf16[16,80,128]{2,1,0:T(8,128)(2,1)} %get-tuple-element.14), calls=%async_computation.1 | async-start | bytes 655360 | tf_op jit(solution)/shard_map/all_to_all | solution.py:444
  40.2 0.7 copy-start.10
  40.9 0.7 copy-start.11
  44.0 2.1 %copy-start = (bf16[1024,2304]{1,0:T(8,128)(2,1)}, bf16[1024,2304]{1,0:T(8,128)(2,1)S(1)}, u32[]{:S(2)}) copy-start(bf16[1024,2304]{1,0:T(8,128)(2,1)S(1)} %get-tuple-element.13.table_ref) | copy-start | bytes 14155780
  60.6 2.3 %copy-start.1 = (bf16[1024,2304]{1,0:T(8,128)(2,1)S(1)}, bf16[1024,2304]{1,0:T(8,128)(2,1)}, u32[]{:S(2)}) copy-start(bf16[1024,2304]{1,0:T(8,128)(2,1)} %copy-done) | copy-start | bytes 14155780

commit v3 on v2

--- a/solution.py
+++ b/solution.py
@@ -17,6 +17,7 @@
 VMEM = pl.BlockSpec(memory_space=pltpu.VMEM)
 SMEM = pl.BlockSpec(memory_space=pltpu.SMEM)
 ANY = pl.BlockSpec(memory_space=pl.ANY)
+HBM = pl.BlockSpec(memory_space=pltpu.HBM)
 
 
 def device_index(z_hi, z_lo, x, yc):
@@ -46,19 +47,16 @@
     return band // N_YC, group // N_X, group % N_X, band % N_YC
 
 
-def three_parts(value, spare_ref):
+def two_parts(value, spare_ref):
     first = value.astype(BF16).astype(F32)
-    second = (value - first).astype(BF16).astype(F32)
     spare_ref[0:4] = first
-    spare_ref[4:8] = second
-    spare_ref[8:12] = value - first - second
-    spare_ref[12:16] = jnp.zeros_like(value)
+    spare_ref[4:8] = value - first
     return spare_ref[...].astype(BF16)
 
 
 def joined(rows):
     rows = rows.astype(F32)
-    return rows[0:4] + rows[4:8] + rows[8:12]
+    return rows[0:4] + rows[4:8]
 
 
 TOP, LOW = EDGE - 1, EDGE + 64
@@ -129,35 +127,46 @@
             window_ref[pl.ds(place, block // pulses, stride=pulses), :] = both
     tall = Z_HI * block
     out_ref[:, :tall, :] = window_ref[...].astype(BF16).reshape(N_YC, tall, LANES)
-    out_ref[:, tall:, :] = jnp.zeros((N_YC, 2 * EDGE, LANES), BF16)
+    out_ref[:, tall:, :] = jnp.zeros((N_YC, EDGE, LANES), BF16)
     yc = place_of()[3]
     for side, line, to in ((0, 0, yc + N_YC - 1), (1, EDGE - 1, yc + 1)):
         edge = [edge_ref[side, comp, line : line + 1, :] for comp in range(comps)]
         edge = [e[:, i * LANES : (i + 1) * LANES] for e in edge for i in range(2)]
-        out_ref[to % N_YC, tall:, :] = three_parts(jnp.concatenate(edge, axis=0), spare_ref)
-
-
-def side_columns(image_ref, out_ref, pad_ref):
-    rows, columns = image_ref.shape[1:]
+        out_ref[to % N_YC, tall:, :] = two_parts(jnp.concatenate(edge, axis=0), spare_ref)
+
+
+def side_columns(image_hbm, weight_hbm, other_ref, out_ref, weight_ref, pad_ref, block_ref, sem):
+    z_hi = place_of()[0]
+    rows, columns = image_hbm.shape[1:]
+    copies = [
+        pltpu.make_async_copy(weight_hbm, weight_ref.at[z_hi], sem.at[0]),
+        pltpu.make_async_copy(image_hbm.at[:, :, pl.ds(0, LANES)], block_ref.at[0], sem.at[1]),
+        pltpu.make_async_copy(
+            image_hbm.at[:, :, pl.ds(columns - LANES, LANES)], block_ref.at[1], sem.at[2]
+        ),
+    ]
+    for copy in copies:
+        copy.start()
+    weight_ref[1 - z_hi] = other_ref[...]
     pad_ref[...] = jnp.zeros_like(pad_ref)
     out_ref[...] = jnp.zeros_like(out_ref)
+    for copy in copies:
+        copy.wait()
     for comp in range(2):
         for side, line in ((0, 0), (1, LANES - 1)):
-            pad_ref[EDGE : EDGE + rows, :] = image_ref[
-                comp, :, side * (columns - LANES) : side * (columns - LANES) + LANES
-            ]
+            pad_ref[EDGE : EDGE + rows, :] = block_ref[side, comp]
             out_ref[2 * side + comp : 2 * side + comp + 1, :] = pad_ref[...].T[line : line + 1, :]
 
 
 def lift_windows(
-    window_ref, own_ref, other_ref, column_ref, out_ref, edge_ref, spare_ref
+    window_ref, weight_ref, column_ref, out_ref, edge_ref, spare_ref
 ):
     z_hi, _, _, yc = place_of()
-    sources, height = window_ref.shape[0], window_ref.shape[1] - 2 * EDGE
+    sources, height = window_ref.shape[0], window_ref.shape[1] - EDGE
     half = height // Z_HI
-    parts = own_ref.shape[1] // LANES
+    band_rows, window_len = weight_ref.shape[1:]
+    parts = window_len // LANES
     rows = half // parts
-    band_rows = own_ref.shape[0]
     tall = sources * rows // 2
 
     above = joined(window_ref[(yc + N_YC - 1) % N_YC, height:, :])
@@ -170,21 +179,22 @@
     columns = with_corners(column_ref[0:4], above, below)
 
     dims = (((1,), (1,)), ((), ()))
-    for weight_ref, z_half, extra in ((own_ref, z_hi, columns), (other_ref, 1 - z_hi, foreign)):
+    for z_half in range(Z_HI):
+        extra = jnp.where(z_half == z_hi, columns, foreign)
         lifted = jnp.zeros((sources * rows, band_rows), F32)
         for part in range(parts):
-            first = pl.multiple_of(z_half * half + part * rows, rows)
+            first = z_half * half + part * rows
             piece = window_ref[:, pl.ds(first, rows), :].reshape(sources * rows, LANES)
             lifted = lifted + lax.dot_general(
                 piece,
-                weight_ref[:, part * LANES : (part + 1) * LANES],
+                weight_ref[z_half, :, part * LANES : (part + 1) * LANES],
                 dims,
                 preferred_element_type=F32,
             )
         lifted = lifted.reshape(sources, 2, rows // 2, band_rows)
         both = jnp.concatenate([lifted[:, 0], lifted[:, 1]], axis=-1)
         both = both.reshape(tall, 2 * band_rows).astype(BF16)
-        extra = three_parts(extra, spare_ref)
+        extra = two_parts(extra, spare_ref)
         for z in range(Z_LO):
             out_ref[z_half * Z_LO + z, :tall, :] = both
             out_ref[z_half * Z_LO + z, tall:, :] = extra
@@ -212,11 +222,32 @@
 FINE = 16
 
 
-def make_table(after_ref, ramp_ref, taps_ref, table_ref, tap_rows_ref, rate_ref, coarse_ref):
+def make_table(
+    after_ref,
+    ramp_hbm,
+    taps_hbm,
+    near_ref,
+    far_hbm,
+    tap_rows_ref,
+    ramp_ref,
+    taps_ref,
+    far_ref,
+    rate_ref,
+    coarse_ref,
+    sem,
+):
     del after_ref
+    copies = [
+        pltpu.make_async_copy(ramp_hbm, ramp_ref, sem.at[0]),
+        pltpu.make_async_copy(taps_hbm, taps_ref, sem.at[1]),
+    ]
+    for copy in copies:
+        copy.start()
     _, z_lo, x, _ = place_of()
     n_groups = ramp_ref.shape[0]
-    depth = table_ref.shape[1] // 2
+    half, depth = near_ref.shape[0], near_ref.shape[1] // 2
+    for copy in copies:
+        copy.wait()
     for t in range(2 * TAPS_K + 1):
         tap_rows_ref[t : t + 1, :] = jnp.full((1, LANES), taps_ref[t], F32)
 
@@ -235,8 +266,8 @@
         ends = jnp.where((lane >= place + EDGE) & (lane < place + 2 * EDGE), after, ends)
     rate_ref[Z_LO : Z_LO + 1, :] = ends
 
-    n_coarse = table_ref.shape[0] // FINE
-    first = z_lo * table_ref.shape[0]
+    n_coarse = 2 * half // FINE
+    first = z_lo * 2 * half
     fine_step = lax.broadcasted_iota(jnp.int32, (FINE, LANES), 0).astype(F32)
     coarse_step = (
         first + FINE * lax.broadcasted_iota(jnp.int32, (n_coarse, LANES), 0)
@@ -250,17 +281,35 @@
         for a in range(n_coarse):
             s = coarse_ref[0, a : a + 1, :]
             c = coarse_ref[1, a : a + 1, :]
-            table_ref[a * FINE : (a + 1) * FINE, i * LANES : (i + 1) * LANES] = (
+            table_ref = near_ref if a < n_coarse // 2 else far_ref
+            row = a % (n_coarse // 2) * FINE
+            table_ref[row : row + FINE, i * LANES : (i + 1) * LANES] = (
                 c * fine_cos - s * fine_sin
             ).astype(BF16)
-            table_ref[a * FINE : (a + 1) * FINE, depth + i * LANES : depth + (i + 1) * LANES] = (
+            table_ref[row : row + FINE, depth + i * LANES : depth + (i + 1) * LANES] = (
                 s * fine_cos + c * fine_sin
             ).astype(BF16)
+    copy = pltpu.make_async_copy(far_ref, far_hbm, sem.at[2])
+    copy.start()
+    copy.wait()
 
 
 def sum_pulses(
-    tap_rows_ref, table_ref, lifted_ref, column_ref, edge_ref, out_ref, edge_out_ref, pad_ref, blend_ref
+    tap_rows_ref,
+    near_ref,
+    far_hbm,
+    lifted_ref,
+    column_ref,
+    edge_ref,
+    out_ref,
+    edge_out_ref,
+    pad_ref,
+    blend_ref,
+    far_ref,
+    sem,
 ):
+    copy = pltpu.make_async_copy(far_hbm, far_ref, sem)
+    copy.start()
     z_hi, z_lo, x, yc = place_of()
     width = lifted_ref.shape[2]
     half_pulses = LANES // Z_HI
@@ -291,8 +340,12 @@
             blend_ref[pl.ds(k * depth + main + i * 2 * EDGE, 2 * EDGE), :] = outside
 
     for block in range(blocks):
+        if block == blocks // 2:
+            copy.wait()
+        table_ref = near_ref if block < blocks // 2 else far_ref
+        row = block % (blocks // 2) * columns
         out_ref[block, :columns, :] = jnp.dot(
-            table_ref[block * columns : (block + 1) * columns, :],
+            table_ref[row : row + columns, :],
             blend_ref[...],
             preferred_element_type=F32,
         )
@@ -319,49 +372,47 @@
     out_ref[(x + N_X - 1) % N_X, columns : columns + 2, :] = jnp.where(x > 0, own, right)[0:2]
 
 
-def finish(scale, step_ref, sums_ref, edge_ref, image_ref, out_ref, pad_ref, side_ref, flow_ref):
-    _, z_lo, x, _ = place_of()
-    group = z_lo * N_X + x
-    comps, rows, columns = image_ref.shape
-    tall = pad_ref.shape[1]
-    total = sums_ref[0, :columns, :]
-    for k in range(1, N_X):
-        total = total + sums_ref[k, :columns, :]
-    total = total.T.reshape(image_ref.shape) * scale
-
-    zero = jnp.zeros((2, LANES), F32)
-    left = sums_ref[(x + N_X - 1) % N_X, columns : columns + 2, :]
-    right = sums_ref[(x + 1) % N_X, columns : columns + 2, :]
-    side_ref[...] = jnp.zeros_like(side_ref)
-    side_ref[0:2, :] = jnp.where(group > 0, left, zero)
-    side_ref[2:4, :] = jnp.where(group < Z_LO * N_X - 1, right, zero)
-    sides = side_ref[...].T[:tall]
-    lane = lax.broadcasted_iota(jnp.int32, (tall, LANES), 1)
-    blank = jnp.zeros((tall, LANES), F32)
-    pad_ref[...] = jnp.zeros_like(pad_ref)
+def variation_inside(step_ref, image_hbm, edge_ref, out_ref, line_ref, pad_ref, flow_ref, sem):
+    comps, rows, columns = image_hbm.shape
+    copies = [
+        pltpu.make_async_copy(
+            image_hbm.at[comp],
+            pad_ref.at[comp, pl.ds(EDGE, rows), pl.ds(LANES, columns)],
+            sem.at[comp],
+        )
+        for comp in range(comps)
+    ]
+    for copy in copies:
+        copy.start()
     for comp in range(comps):
-        pad_ref[comp, EDGE : EDGE + rows, LANES : LANES + columns] = image_ref[comp]
+        pad_ref[comp, :, :LANES] = jnp.zeros((LANES, LANES), F32)
+        pad_ref[comp, :EDGE, LANES:] = jnp.zeros((EDGE, columns), F32)
+        pad_ref[comp, LOW:, LANES:] = jnp.zeros((LANES - LOW, columns), F32)
         for half in range(2):
             span = pl.ds((1 + half) * LANES, LANES)
             pad_ref[comp, TOP : TOP + 1, span] = edge_ref[2 * comp + half : 2 * comp + half + 1, :]
             pad_ref[comp, LOW : LOW + 1, span] = edge_ref[4 + 2 * comp + half : 5 + 2 * comp + half, :]
-        pad_ref[comp, :, :LANES] = jnp.where(lane == LANES - 1, sides[:, comp : comp + 1], blank)
-        pad_ref[comp, :, LANES + columns :] = jnp.where(
-            lane == 0, sides[:, 2 + comp : 3 + comp], blank
-        )
+    for copy in copies:
+        copy.wait()
+    line_ref[...] = jnp.zeros_like(line_ref)
+    for comp in range(comps):
+        first = pad_ref[comp, :, LANES : 2 * LANES].T
+        last = pad_ref[comp, :, columns : columns + LANES].T
+        line_ref[comp : comp + 1, :] = first[0:1]
+        line_ref[2 + comp : 3 + comp, :] = last[LANES - 1 : LANES]
 
     high, wide = rows + EDGE, columns + LANES
+    lane = lax.broadcasted_iota(jnp.int32, (high, wide), 1)
+    whole = (lane >= LANES) & (lane < wide - 1)
     row_step, col_step = [], []
     square = jnp.zeros((high, wide), F32) + smooth_eps
     for comp in range(comps):
         here = pad_ref[comp, :high, :]
-        following = pltpu.roll(here, here.shape[1] - 1, 1)[:, :wide]
-        here = here[:, :wide]
-        row_step.append(pad_ref[comp, 1 : high + 1, :wide] - here)
-        col_step.append(following - here)
+        row_step.append(pad_ref[comp, 1 : high + 1, :] - here)
+        col_step.append(pltpu.roll(here, wide - 1, 1) - here)
         square = square + row_step[-1] * row_step[-1] + col_step[-1] * col_step[-1]
-    inverse = lax.rsqrt(square)
-    step, weight = step_ref[0], step_ref[1]
+    inverse = jnp.where(whole, lax.rsqrt(square), jnp.zeros_like(square))
+    weight = step_ref[0] * step_ref[1]
     for comp in range(comps):
         row_flow = row_step[comp] * inverse
         col_flow = col_step[comp] * inverse
@@ -369,11 +420,53 @@
         across = col_flow - pltpu.roll(col_flow, 1, 1)
         down = row_flow[EDGE:, LANES:] - flow_ref[EDGE - 1 : high - 1, LANES:]
         variation = -(down + across[EDGE:, LANES:])
-        out_ref[comp] = image_ref[comp] - step * (total[comp] + weight * variation)
-
-
-def call(kernel, out_shape, in_specs, args, scratch=(), cost=None):
-    out_specs = jax.tree.map(lambda _: VMEM, out_shape)
+        out_ref[comp] = pad_ref[comp, EDGE:high, LANES:] - weight * variation
+
+
+def finish(scale, step_ref, sums_ref, base_ref, line_ref, out_ref, side_ref):
+    _, z_lo, x, _ = place_of()
+    group = z_lo * N_X + x
+    comps, rows, columns = base_ref.shape
+    total = sums_ref[0, :columns, :]
+    for k in range(1, N_X):
+        total = total + sums_ref[k, :columns, :]
+    total = total.T.reshape(base_ref.shape) * (scale * step_ref[0])
+
+    zero = jnp.zeros((comps, LANES), F32)
+    left = jnp.where(group > 0, sums_ref[(x + N_X - 1) % N_X, columns : columns + comps, :], zero)
+    right = jnp.where(
+        group < Z_LO * N_X - 1, sums_ref[(x + 1) % N_X, columns : columns + comps, :], zero
+    )
+    first, last = line_ref[0:comps, :], line_ref[comps : 2 * comps, :]
+
+    def flows(here, beside):
+        down = pltpu.roll(here, LANES - 1, 1) - here
+        across = beside - here
+        inverse = lax.rsqrt(jnp.sum(down * down + across * across, axis=0, keepdims=True) + smooth_eps)
+        return down * inverse, across * inverse
+
+    side_ref[...] = jnp.zeros_like(side_ref)
+    side_ref[0:comps, :] = flows(left, first)[1]
+    down, across = flows(last, right)
+    side_ref[comps : 2 * comps, :] = pltpu.roll(down, 1, 1) - down - across
+    sides = side_ref[...].T[EDGE : EDGE + rows] * (step_ref[0] * step_ref[1])
+    lane = lax.broadcasted_iota(jnp.int32, (rows, LANES), 1)
+    blank = jnp.zeros((rows, LANES), F32)
+    for comp in range(comps):
+        added = jnp.where(lane == 0, sides[:, comp : comp + 1], blank)
+        out_ref[comp, :, :LANES] = base_ref[comp, :, :LANES] - total[comp, :, :LANES] - added
+        added = jnp.where(lane == LANES - 1, sides[:, comps + comp : comps + comp + 1], blank)
+        tail = columns - LANES
+        out_ref[comp, :, tail:] = base_ref[comp, :, tail:] - total[comp, :, tail:] - added
+
+
+def in_hbm(*values):
+    return tuple(pltpu.with_memory_space_constraint(value, pltpu.HBM) for value in values)
+
+
+def call(kernel, out_shape, in_specs, args, scratch=(), cost=None, out_specs=None):
+    if out_specs is None:
+        out_specs = jax.tree.map(lambda _: VMEM, out_shape)
     return pl.pallas_call(
         kernel,
         out_shape=out_shape,
@@ -406,9 +499,9 @@
     block = window_len // LANES * comps * pulses
     windows = call(
         cut_windows,
-        shape((N_YC, Z_HI * block + 2 * EDGE, LANES), BF16),
-        [ANY, ANY, ANY, ANY],
-        (window_start, footprint, pulse_data, image_now),
+        shape((N_YC, Z_HI * block + EDGE, LANES), BF16),
+        [HBM, HBM, HBM, HBM],
+        in_hbm(window_start, footprint, pulse_data, image_now),
         [
             pltpu.SMEM(window_start.shape, jnp.int32),
             pltpu.SMEM(footprint.shape, jnp.int32),
@@ -416,67 +509,91 @@
             pltpu.VMEM((2, comps, EDGE, columns), F32),
             pltpu.VMEM((pulses * comps * (bins // LANES + 1), LANES), F32),
             pltpu.VMEM((band_count * block, LANES), F32),
-            pltpu.VMEM((2 * EDGE, LANES), F32),
+            pltpu.VMEM((EDGE, LANES), F32),
             pltpu.SemaphoreType.DMA((5,)),
         ],
     )
     in_plane = [[h * N_YC + i for i in range(N_YC)] for h in range(Z_HI)]
     windows = lax.all_to_all(windows, "band", 0, 0, axis_index_groups=in_plane, tiled=True)
-    side = call(
+    side, weights = call(
         side_columns,
-        shape((EDGE, LANES), F32),
-        [VMEM],
-        (image_now,),
-        [pltpu.VMEM((LANES, LANES), F32)],
-        pl.CostEstimate(flops=1 << 20, bytes_accessed=1 << 17, transcendentals=0),
+        (shape((EDGE, LANES), F32), shape((Z_HI, band_rows, window_len), BF16)),
+        [HBM, HBM, VMEM],
+        (*in_hbm(image_now, range_to_row_weight), other_weight),
+        [
+            pltpu.VMEM((LANES, LANES), F32),
+            pltpu.VMEM((2, comps, band_rows, LANES), F32),
+            pltpu.SemaphoreType.DMA((3,)),
+        ],
+        pl.CostEstimate(flops=1 << 34, bytes_accessed=1 << 27, transcendentals=0),
     )
     width = comps * band_rows
     lifted, edges = call(
         lift_windows,
         (
-            shape((N_Z, N_YC * pulses + 2 * EDGE, width), BF16),
+            shape((N_Z, N_YC * pulses + EDGE, width), BF16),
             shape((EDGE, LANES), F32),
         ),
-        [VMEM, VMEM, VMEM, VMEM],
-        (windows, range_to_row_weight, other_weight, side),
-        [pltpu.VMEM((2 * EDGE, LANES), F32)],
+        [VMEM] * 3,
+        (windows, weights, side),
+        [pltpu.VMEM((EDGE, LANES), F32)],
     )
     lifted = lax.all_to_all(lifted, ("aper", "band"), 0, 0, axis_index_groups=z_rings(), tiled=True)
     depth = (Z_LO + 1) * LANES
-    table, tap_rows = call(
+    half = N_X * columns // 2
+    near, far, tap_rows = call(
         make_table,
-        (shape((N_X * columns, 2 * depth), BF16), shape((EDGE, LANES), F32)),
-        [ANY, VMEM, SMEM],
-        (edges, ramp_rate.reshape(groups, LANES), slow_taps),
+        (
+            shape((half, 2 * depth), BF16),
+            pltpu.HBM((half, 2 * depth), BF16),
+            shape((EDGE, LANES), F32),
+        ),
+        [ANY, HBM, HBM],
+        (edges, *in_hbm(ramp_rate.reshape(groups, LANES), slow_taps)),
         [
+            pltpu.VMEM((groups, LANES), F32),
+            pltpu.SMEM(slow_taps.shape, F32),
+            pltpu.VMEM((half, 2 * depth), BF16),
             pltpu.VMEM((2 * EDGE, LANES), F32),
-            pltpu.VMEM((2, N_X * columns // FINE, LANES), F32),
+            pltpu.VMEM((2, 2 * half // FINE, LANES), F32),
+            pltpu.SemaphoreType.DMA((3,)),
         ],
         pl.CostEstimate(flops=1 << 24, bytes_accessed=1 << 23, transcendentals=0),
+        [VMEM, HBM, VMEM],
     )
     sums, edges = call(
         sum_pulses,
         (shape((N_X, columns + EDGE, width), F32), shape((EDGE, LANES), F32)),
-        [VMEM, VMEM, VMEM, VMEM, VMEM],
-        (tap_rows, table, lifted, side, edges),
+        [VMEM, VMEM, HBM, VMEM, VMEM, VMEM],
+        (tap_rows, near, *in_hbm(far), lifted, side, edges),
         [
             pltpu.VMEM((LANES + 4 * EDGE, width), F32),
             pltpu.VMEM((2 * depth, width), BF16),
+            pltpu.VMEM((half, 2 * depth), BF16),
+            pltpu.SemaphoreType.DMA,
         ],
     )
     along_x = [[z * N_X + x for x in range(N_X)] for z in range(Z_LO)]
     sums = lax.all_to_all(sums, "aper", 0, 0, axis_index_groups=along_x, tiled=True)
+    base, lines = call(
+        variation_inside,
+        (shape(image_now.shape, F32), shape((EDGE, LANES), F32)),
+        [SMEM, HBM, VMEM],
+        (step_and_variation_weight, *in_hbm(image_now), edges),
+        [
+            pltpu.VMEM((comps, LANES, columns + LANES), F32),
+            pltpu.VMEM((band_rows + EDGE, columns + LANES), F32),
+            pltpu.SemaphoreType.DMA((comps,)),
+        ],
+        pl.CostEstimate(flops=1 << 24, bytes_accessed=1 << 23, transcendentals=0),
+    )
     scale = 1.0 / math.sqrt(groups * LANES)
     return call(
         lambda *refs: finish(scale, *refs),
         shape(image_now.shape, F32),
         [SMEM, VMEM, VMEM, VMEM],
-        (step_and_variation_weight, sums, edges, image_now),
-        [
-            pltpu.VMEM((comps, band_rows + 2 * EDGE, columns + 2 * LANES), F32),
-            pltpu.VMEM((LANES, LANES), F32),
-            pltpu.VMEM((band_rows + EDGE, columns + LANES), F32),
-        ],
+        (step_and_variation_weight, sums, base, lines),
+        [pltpu.VMEM((LANES, LANES), F32)],
     )
 
 

time: 79.2 us -> 72.1 us (0.910)
  the two profiles are of different devices: /device:TPU:8 before, /device:TPU:32 now
where the time goes in v3:
time: 72.1 us; the launch traced here: 71.5 us
  starting transfers between devices  27.8 us (39%)
  waiting for transfers between devices  27.7 us (38%)
  Pallas kernels  15.9 us (22%)
    pallas_call x7, Pallas kernels, call(): pl.pallas_call(kernel, out_shape=out_shape, in_specs=in_specs, out_specs=...  15.9 us
    all_to_all x1, waiting for transfers between devices, local(): lax.all_to_all(lifted, ('aper', 'band'), 0, 0, axis_index_groups=z_rings(...  14.4 us
    ppermute x1, starting transfers between devices, local(): lax.ppermute(range_to_row_weight, ('aper', 'band'), halves_swapped())  11.8 us
    all_to_all x1, starting transfers between devices, local(): lax.all_to_all(lifted, ('aper', 'band'), 0, 0, axis_index_groups=z_rings(...  7.21 us
    all_to_all x1, waiting for transfers between devices, local(): lax.all_to_all(sums, 'aper', 0, 0, axis_index_groups=along_x, tiled=True)  6.68 us
    all_to_all x1, waiting for transfers between devices, local(): lax.all_to_all(windows, 'band', 0, 0, axis_index_groups=in_plane, tiled=T...  6.64 us
    all_to_all x1, starting transfers between devices, local(): lax.all_to_all(windows, 'band', 0, 0, axis_index_groups=in_plane, tiled=T...  4.48 us
    all_to_all x1, starting transfers between devices, local(): lax.all_to_all(sums, 'aper', 0, 0, axis_index_groups=along_x, tiled=True)  4.32 us
  transfers between devices with their start and end apart: 4, of which 3 were waited for; matrix products, arithmetic and copies ran while one was open for 0% of the time, Pallas kernels for 13%

profile of v3, /device:TPU:32, one launch (start us, length us, event | category | flops | bytes accessed | tf_op | source)
XLA Modules:
  0.0 71.5 jit_solution(14923608987838453529)
XLA Ops:
  0.0 11.8 %collective-permute-start = (bf16[64,512]{1,0:T(8,128)(2,1)}, bf16[64,512]{1,0:T(8,128)(2,1)S(1)}, u32[]{:S(2)}, u32[]{:S(2)}) collective-permute-start(bf16[64,512]{1,0:T(8,128)(2,1)} %weight_hbm.1), channel_id=1, source_target_pairs={{0,264},{1,265},{2,266},{3,267},{4,268},{5,269},{6,270},{7,271},{1... | collective-permute-start | bytes 196616 | tf_op jit(solution)/shard_map/ppermute | solution.py:498
  11.8 2.2 %shard_map.82 = bf16[8,136,128]{2,1,0:T(8,128)(2,1)} custom-call(s32[8,16]{1,0:T(8,128)} %start_hbm.1, s32[8,8]{1,0:T(8,128)} %foot_hbm.1, bf16[2,8,8192]{2,1,0:T(8,128)(2,1)} %pulse_hbm.1, f32[2,64,256]{2,1,0:T(8,128)} %image_hbm.5), custom_call_target="tpu_custom_call" | custom-call | tf_op jit(solution)/shard_map/pallas_call | solution.py:470
  14.0 4.5 %all-to-all-start = ((bf16[8,136,128]{2,1,0:T(8,128)(2,1)}), bf16[8,136,128]{2,1,0:T(8,128)(2,1)S(1)}, u32[]{:S(2)}, u32[]{:S(2)}) async-start(bf16[8,136,128]{2,1,0:T(8,128)(2,1)} %shard_map.82), calls=%async_computation | async-start | bytes 557056 | tf_op jit(solution)/shard_map/all_to_all | solution.py:517
  18.5 0.0 collective-permute-done.other_ref
  18.5 1.1 %shard_map.83 = (f32[8,128]{1,0:T(8,128)S(1)}, bf16[2,64,512]{2,1,0:T(8,128)(2,1)S(1)}) custom-call(f32[2,64,256]{2,1,0:T(8,128)} %image_hbm.5, bf16[64,512]{1,0:T(8,128)(2,1)} %weight_hbm.1, bf16[64,512]{1,0:T(8,128)(2,1)S(1)} %collective-permute-done.other_ref), custom_call_target="tpu_custom_call" | custom-call | flops 17179869184 | bytes 134217728 | tf_op jit(solution)/shard_map/pallas_call | solution.py:470
  19.6 6.6 %all-to-all-done.window_ref = bf16[8,136,128]{2,1,0:T(8,128)(2,1)S(1)} async-done(((bf16[8,136,128]{2,1,0:T(8,128)(2,1)}), bf16[8,136,128]{2,1,0:T(8,128)(2,1)S(1)}, u32[]{:S(2)}, u32[]{:S(2)}) %all-to-all-start) | async-done | bytes 278560 | tf_op jit(solution)/shard_map/all_to_all | solution.py:517
  26.2 1.0 %shard_map.84 = (bf16[16,72,128]{2,1,0:T(8,128)(2,1)}, f32[8,128]{1,0:T(8,128)S(1)}) custom-call(bf16[8,136,128]{2,1,0:T(8,128)(2,1)S(1)} %all-to-all-done.window_ref, bf16[2,64,512]{2,1,0:T(8,128)(2,1)S(1)} %get-tuple-element.16.weight_ref, f32[8,128]{1,0:T(8,128)S(1)} %get-tuple-element.17.column_ref), custom_call_target="tpu_custom_call" | custom-call | tf_op jit(solution)/shard_map/pallas_call | solution.py:470
  27.2 7.2 %all-to-all-start.1 = ((bf16[16,72,128]{2,1,0:T(8,128)(2,1)}), bf16[16,72,128]{2,1,0:T(8,128)(2,1)S(1)}, u32[]{:S(2)}, u32[]{:S(2)}) async-start(bf16[16,72,128]{2,1,0:T(8,128)(2,1)} %get-tuple-element.22), calls=%async_computation.1 | async-start | bytes 589824 | tf_op jit(solution)/shard_map/all_to_all | solution.py:541
  34.5 4.1 %shard_map.85 = (bf16[512,2304]{1,0:T(8,128)(2,1)S(1)}, bf16[512,2304]{1,0:T(8,128)(2,1)}, f32[8,128]{1,0:T(8,128)S(1)}) custom-call(f32[8,128]{1,0:T(8,128)S(1)} %get-tuple-element.18.after_ref.edge_ref, f32[32,128]{1,0:T(8,128)} %bitcast.1, f32[5]{0:T(128)} %taps_hbm.1), custom_call_target="tpu_custom_call" | custom-call | flops 16777216 | bytes 8388608 | tf_op jit(solution)/shard_map/pallas_call | solution.py:470
  38.6 14.4 %all-to-all-done.1.lifted_ref = bf16[16,72,128]{2,1,0:T(8,128)(2,1)S(1)} async-done(((bf16[16,72,128]{2,1,0:T(8,128)(2,1)}), bf16[16,72,128]{2,1,0:T(8,128)(2,1)S(1)}, u32[]{:S(2)}, u32[]{:S(2)}) %all-to-all-start.1) | async-done | bytes 294944 | tf_op jit(solution)/shard_map/all_to_all | solution.py:541
  53.0 0.0 copy-start
  53.0 4.2 %shard_map.86 = (f32[4,264,128]{2,1,0:T(8,128)}, f32[8,128]{1,0:T(8,128)S(1)}) custom-call(f32[8,128]{1,0:T(8,128)S(1)} %get-tuple-element.19.tap_rows_ref, bf16[512,2304]{1,0:T(8,128)(2,1)S(1)} %get-tuple-element.20.near_ref, bf16[512,2304]{1,0:T(8,128)(2,1)} %get-tuple-element.21.far_hbm, bf16[16,72,128]{2,1,0:T(8,128)(2,1)S(1)} %all-to-all-done.1.lifted_ref, ...), custom_call_target="tpu_custom_call" | custom-call | tf_op jit(solution)/shard_map/pallas_call | solution.py:470
  57.2 4.3 %all-to-all-start.2 = ((f32[4,264,128]{2,1,0:T(8,128)}), f32[4,264,128]{2,1,0:T(8,128)S(1)}, u32[]{:S(2)}, u32[]{:S(2)}) async-start(f32[4,264,128]{2,1,0:T(8,128)} %get-tuple-element.23), calls=%async_computation.2 | async-start | bytes 1081344 | tf_op jit(solution)/shard_map/all_to_all | solution.py:577
  61.5 0.0 copy-done
  61.5 1.8 %shard_map.87 = (f32[2,64,256]{2,1,0:T(8,128)S(1)}, f32[8,128]{1,0:T(8,128)S(1)}) custom-call(f32[2]{0:T(128)S(1)} %copy-done, f32[2,64,256]{2,1,0:T(8,128)} %image_hbm.5, f32[8,128]{1,0:T(8,128)S(1)} %get-tuple-element.24.edge_ref), custom_call_target="tpu_custom_call" | custom-call | flops 16777216 | bytes 8388608 | tf_op jit(solution)/shard_map/pallas_call | solution.py:470
  63.3 6.7 %all-to-all-done.2.refs_1_ = f32[4,264,128]{2,1,0:T(8,128)S(1)} async-done(((f32[4,264,128]{2,1,0:T(8,128)}), f32[4,264,128]{2,1,0:T(8,128)S(1)}, u32[]{:S(2)}, u32[]{:S(2)}) %all-to-all-start.2) | async-done | bytes 540704 | tf_op jit(solution)/shard_map/all_to_all | solution.py:577
  70.0 1.6 %shard_map.88 = f32[2,64,256]{2,1,0:T(8,128)} custom-call(f32[2]{0:T(128)S(1)} %copy-done, f32[4,264,128]{2,1,0:T(8,128)S(1)} %all-to-all-done.2.refs_1_, f32[2,64,256]{2,1,0:T(8,128)S(1)} %get-tuple-element.25.refs_2_, f32[8,128]{1,0:T(8,128)S(1)} %get-tuple-element.26.refs_3_), custom_call_target="tpu_custom_call" | custom-call | tf_op jit(solution)/shard_map/pallas_call | solution.py:470
Async XLA Ops:
  0.0 18.5 %collective-permute-start = (bf16[64,512]{1,0:T(8,128)(2,1)}, bf16[64,512]{1,0:T(8,128)(2,1)S(1)}, u32[]{:S(2)}, u32[]{:S(2)}) collective-permute-start(bf16[64,512]{1,0:T(8,128)(2,1)} %weight_hbm.1), channel_id=1, source_target_pairs={{0,264},{1,265},{2,266},{3,267},{4,268},{5,269},{6,270},{7,271},{1... | collective-permute-start | bytes 196616 | tf_op jit(solution)/shard_map/ppermute | solution.py:498
  14.0 12.2 %all-to-all-start = ((bf16[8,136,128]{2,1,0:T(8,128)(2,1)}), bf16[8,136,128]{2,1,0:T(8,128)(2,1)S(1)}, u32[]{:S(2)}, u32[]{:S(2)}) async-start(bf16[8,136,128]{2,1,0:T(8,128)(2,1)} %shard_map.82), calls=%async_computation | async-start | bytes 557056 | tf_op jit(solution)/shard_map/all_to_all | solution.py:517
  27.2 25.8 %all-to-all-start.1 = ((bf16[16,72,128]{2,1,0:T(8,128)(2,1)}), bf16[16,72,128]{2,1,0:T(8,128)(2,1)S(1)}, u32[]{:S(2)}, u32[]{:S(2)}) async-start(bf16[16,72,128]{2,1,0:T(8,128)(2,1)} %get-tuple-element.22), calls=%async_computation.1 | async-start | bytes 589824 | tf_op jit(solution)/shard_map/all_to_all | solution.py:541
  53.0 8.5 %copy-start = (f32[2]{0:T(128)S(1)}, f32[2]{0:T(128)}, u32[]{:S(2)}) copy-start(f32[2]{0:T(128)} %refs_0_.1) | copy-start | bytes 28
  57.2 12.8 %all-to-all-start.2 = ((f32[4,264,128]{2,1,0:T(8,128)}), f32[4,264,128]{2,1,0:T(8,128)S(1)}, u32[]{:S(2)}, u32[]{:S(2)}) async-start(f32[4,264,128]{2,1,0:T(8,128)} %get-tuple-element.23), calls=%async_computation.2 | async-start | bytes 1081344 | tf_op jit(solution)/shard_map/all_to_all | solution.py:577

commit v4 on v3

--- a/solution.py
+++ b/solution.py
@@ -227,13 +227,13 @@
     ramp_hbm,
     taps_hbm,
     near_ref,
-    far_hbm,
+    fine_ref,
+    coarse_ref,
     tap_rows_ref,
     ramp_ref,
     taps_ref,
-    far_ref,
     rate_ref,
-    coarse_ref,
+    spare_ref,
     sem,
 ):
     del after_ref
@@ -245,7 +245,7 @@
         copy.start()
     _, z_lo, x, _ = place_of()
     n_groups = ramp_ref.shape[0]
-    half, depth = near_ref.shape[0], near_ref.shape[1] // 2
+    half = near_ref.shape[0]
     for copy in copies:
         copy.wait()
     for t in range(2 * TAPS_K + 1):
@@ -273,31 +273,40 @@
         first + FINE * lax.broadcasted_iota(jnp.int32, (n_coarse, LANES), 0)
     ).astype(F32)
     for i in range(Z_LO + 1):
+        span = pl.ds(i * LANES, LANES)
         rate = rate_ref[i : i + 1, :]
         fine_sin, fine_cos = sin_cos(rate * fine_step)
         coarse_sin, coarse_cos = sin_cos(rate * coarse_step)
-        coarse_ref[0] = coarse_sin
-        coarse_ref[1] = coarse_cos
-        for a in range(n_coarse):
-            s = coarse_ref[0, a : a + 1, :]
-            c = coarse_ref[1, a : a + 1, :]
-            table_ref = near_ref if a < n_coarse // 2 else far_ref
-            row = a % (n_coarse // 2) * FINE
-            table_ref[row : row + FINE, i * LANES : (i + 1) * LANES] = (
-                c * fine_cos - s * fine_sin
-            ).astype(BF16)
-            table_ref[row : row + FINE, depth + i * LANES : depth + (i + 1) * LANES] = (
-                s * fine_cos + c * fine_sin
-            ).astype(BF16)
-    copy = pltpu.make_async_copy(far_ref, far_hbm, sem.at[2])
-    copy.start()
-    copy.wait()
+        fine_ref[0, :, span], fine_ref[1, :, span] = fine_sin, fine_cos
+        spare_ref[0], spare_ref[1] = coarse_sin, coarse_cos
+        coarse_ref[0, :, span] = coarse_sin[n_coarse // 2 :]
+        coarse_ref[1, :, span] = coarse_cos[n_coarse // 2 :]
+        for a in range(n_coarse // 2):
+            fill(
+                near_ref,
+                a * FINE,
+                i,
+                (spare_ref[0, a : a + 1, :], spare_ref[1, a : a + 1, :]),
+                (fine_sin, fine_cos),
+            )
+
+
+def fill(table_ref, row, i, coarse, fine):
+    depth = table_ref.shape[1] // 2
+    (s, c), (fine_sin, fine_cos) = coarse, fine
+    table_ref[row : row + FINE, i * LANES : (i + 1) * LANES] = (
+        c * fine_cos - s * fine_sin
+    ).astype(BF16)
+    table_ref[row : row + FINE, depth + i * LANES : depth + (i + 1) * LANES] = (
+        s * fine_cos + c * fine_sin
+    ).astype(BF16)
 
 
 def sum_pulses(
     tap_rows_ref,
     near_ref,
-    far_hbm,
+    fine_ref,
+    coarse_ref,
     lifted_ref,
     column_ref,
     edge_ref,
@@ -306,10 +315,7 @@
     pad_ref,
     blend_ref,
     far_ref,
-    sem,
 ):
-    copy = pltpu.make_async_copy(far_hbm, far_ref, sem)
-    copy.start()
     z_hi, z_lo, x, yc = place_of()
     width = lifted_ref.shape[2]
     half_pulses = LANES // Z_HI
@@ -339,9 +345,13 @@
             outside = jnp.concatenate([value[:EDGE], value[EDGE + LANES :]], axis=0)
             blend_ref[pl.ds(k * depth + main + i * 2 * EDGE, 2 * EDGE), :] = outside
 
+    for i in range(Z_LO + 1):
+        span = pl.ds(i * LANES, LANES)
+        fine = fine_ref[0, :, span], fine_ref[1, :, span]
+        for a in range(far_ref.shape[0] // FINE):
+            coarse = coarse_ref[0, a : a + 1, span], coarse_ref[1, a : a + 1, span]
+            fill(far_ref, a * FINE, i, coarse, fine)
     for block in range(blocks):
-        if block == blocks // 2:
-            copy.wait()
         table_ref = near_ref if block < blocks // 2 else far_ref
         row = block % (blocks // 2) * columns
         out_ref[block, :columns, :] = jnp.dot(
@@ -466,7 +476,7 @@
 
 def call(kernel, out_shape, in_specs, args, scratch=(), cost=None, out_specs=None):
     if out_specs is None:
-        out_specs = jax.tree.map(lambda _: VMEM, out_shape)
+        out_specs = [VMEM] * len(out_shape) if isinstance(out_shape, tuple) else VMEM
     return pl.pallas_call(
         kernel,
         out_shape=out_shape,
@@ -499,7 +509,7 @@
     block = window_len // LANES * comps * pulses
     windows = call(
         cut_windows,
-        shape((N_YC, Z_HI * block + EDGE, LANES), BF16),
+        pltpu.VMEM((N_YC, Z_HI * block + EDGE, LANES), BF16),
         [HBM, HBM, HBM, HBM],
         in_hbm(window_start, footprint, pulse_data, image_now),
         [
@@ -531,7 +541,7 @@
     lifted, edges = call(
         lift_windows,
         (
-            shape((N_Z, N_YC * pulses + EDGE, width), BF16),
+            pltpu.VMEM((N_Z, N_YC * pulses + EDGE, width), BF16),
             shape((EDGE, LANES), F32),
         ),
         [VMEM] * 3,
@@ -541,11 +551,12 @@
     lifted = lax.all_to_all(lifted, ("aper", "band"), 0, 0, axis_index_groups=z_rings(), tiled=True)
     depth = (Z_LO + 1) * LANES
     half = N_X * columns // 2
-    near, far, tap_rows = call(
+    near, fine, coarse, tap_rows = call(
         make_table,
         (
             shape((half, 2 * depth), BF16),
-            pltpu.HBM((half, 2 * depth), BF16),
+            shape((2, FINE, depth), F32),
+            shape((2, half // FINE, depth), F32),
             shape((EDGE, LANES), F32),
         ),
         [ANY, HBM, HBM],
@@ -553,24 +564,21 @@
         [
             pltpu.VMEM((groups, LANES), F32),
             pltpu.SMEM(slow_taps.shape, F32),
-            pltpu.VMEM((half, 2 * depth), BF16),
             pltpu.VMEM((2 * EDGE, LANES), F32),
             pltpu.VMEM((2, 2 * half // FINE, LANES), F32),
-            pltpu.SemaphoreType.DMA((3,)),
+            pltpu.SemaphoreType.DMA((2,)),
         ],
         pl.CostEstimate(flops=1 << 24, bytes_accessed=1 << 23, transcendentals=0),
-        [VMEM, HBM, VMEM],
     )
     sums, edges = call(
         sum_pulses,
-        (shape((N_X, columns + EDGE, width), F32), shape((EDGE, LANES), F32)),
-        [VMEM, VMEM, HBM, VMEM, VMEM, VMEM],
-        (tap_rows, near, *in_hbm(far), lifted, side, edges),
+        (pltpu.VMEM((N_X, columns + EDGE, width), F32), shape((EDGE, LANES), F32)),
+        [VMEM] * 7,
+        (tap_rows, near, fine, coarse, lifted, side, edges),
         [
             pltpu.VMEM((LANES + 4 * EDGE, width), F32),
             pltpu.VMEM((2 * depth, width), BF16),
             pltpu.VMEM((half, 2 * depth), BF16),
-            pltpu.SemaphoreType.DMA,
         ],
     )
     along_x = [[z * N_X + x for x in range(N_X)] for z in range(Z_LO)]

time: 72.1 us -> 70.9 us (0.983)
  Pallas kernels: 15.9 us -> 12.5 us
  waiting for transfers between devices: 27.7 us -> 29.8 us
    pallas_call x7, Pallas kernels: 15.9 us -> 12.5 us  [call(): pl.pallas_call(kernel, out_shape=out_shape, in_specs=in_specs, out_specs=...]
    all_to_all x1, waiting for transfers between devices: 14.4 us -> 16.5 us  [local(): lax.all_to_all(lifted, ('aper', 'band'), 0, 0, axis_index_groups=z_rings(...]
  transfers between devices with their start and end apart: 4 -> 4, of which waited for: 3 -> 3; matrix products, arithmetic and copies ran while one was open for 0% -> 0% of each run, Pallas kernels for 13% -> 10%
where the time goes in v4:
time: 70.9 us; the launch traced here: 70.4 us
  waiting for transfers between devices  29.8 us (42%)
  starting transfers between devices  28 us (39%)
  Pallas kernels  12.5 us (18%)
    all_to_all x1, waiting for transfers between devices, local(): lax.all_to_all(lifted, ('aper', 'band'), 0, 0, axis_index_groups=z_rings(...  16.5 us
    pallas_call x7, Pallas kernels, call(): pl.pallas_call(kernel, out_shape=out_shape, in_specs=in_specs, out_specs=...  12.5 us
    ppermute x1, starting transfers between devices, local(): lax.ppermute(range_to_row_weight, ('aper', 'band'), halves_swapped())  11.8 us
    all_to_all x1, starting transfers between devices, local(): lax.all_to_all(lifted, ('aper', 'band'), 0, 0, axis_index_groups=z_rings(...  7.33 us
    all_to_all x1, waiting for transfers between devices, local(): lax.all_to_all(sums, 'aper', 0, 0, axis_index_groups=along_x, tiled=True)  6.68 us
    all_to_all x1, waiting for transfers between devices, local(): lax.all_to_all(windows, 'band', 0, 0, axis_index_groups=in_plane, tiled=T...  6.64 us
    all_to_all x1, starting transfers between devices, local(): lax.all_to_all(windows, 'band', 0, 0, axis_index_groups=in_plane, tiled=T...  4.48 us
    all_to_all x1, starting transfers between devices, local(): lax.all_to_all(sums, 'aper', 0, 0, axis_index_groups=along_x, tiled=True)  4.31 us
  transfers between devices with their start and end apart: 4, of which 3 were waited for; matrix products, arithmetic and copies ran while one was open for 0% of the time, Pallas kernels for 10%

profile of v4, /device:TPU:32, one launch (start us, length us, event | category | flops | bytes accessed | tf_op | source)
XLA Modules:
  0.0 70.4 jit_solution(16984130288622850903)
XLA Ops:
  0.0 11.8 %collective-permute-start = (bf16[64,512]{1,0:T(8,128)(2,1)}, bf16[64,512]{1,0:T(8,128)(2,1)S(1)}, u32[]{:S(2)}, u32[]{:S(2)}) collective-permute-start(bf16[64,512]{1,0:T(8,128)(2,1)} %weight_hbm.1), channel_id=1, source_target_pairs={{0,264},{1,265},{2,266},{3,267},{4,268},{5,269},{6,270},{7,271},{1... | collective-permute-start | bytes 196616 | tf_op jit(solution)/shard_map/ppermute | solution.py:508
  11.8 2.2 %shard_map.82 = bf16[8,136,128]{2,1,0:T(8,128)(2,1)} custom-call(s32[8,16]{1,0:T(8,128)} %start_hbm.1, s32[8,8]{1,0:T(8,128)} %foot_hbm.1, bf16[2,8,8192]{2,1,0:T(8,128)(2,1)} %pulse_hbm.1, f32[2,64,256]{2,1,0:T(8,128)} %image_hbm.5), custom_call_target="tpu_custom_call" | custom-call | tf_op jit(solution)/shard_map/pallas_call | solution.py:480
  14.0 4.5 %all-to-all-start = ((bf16[8,136,128]{2,1,0:T(8,128)(2,1)}), bf16[8,136,128]{2,1,0:T(8,128)(2,1)S(1)}, u32[]{:S(2)}, u32[]{:S(2)}) async-start(bf16[8,136,128]{2,1,0:T(8,128)(2,1)} %shard_map.82), calls=%async_computation | async-start | bytes 557056 | tf_op jit(solution)/shard_map/all_to_all | solution.py:527
  18.5 0.0 collective-permute-done.other_ref
  18.5 1.1 %shard_map.83 = (f32[8,128]{1,0:T(8,128)S(1)}, bf16[2,64,512]{2,1,0:T(8,128)(2,1)S(1)}) custom-call(f32[2,64,256]{2,1,0:T(8,128)} %image_hbm.5, bf16[64,512]{1,0:T(8,128)(2,1)} %weight_hbm.1, bf16[64,512]{1,0:T(8,128)(2,1)S(1)} %collective-permute-done.other_ref), custom_call_target="tpu_custom_call" | custom-call | flops 17179869184 | bytes 134217728 | tf_op jit(solution)/shard_map/pallas_call | solution.py:480
  19.6 6.6 %all-to-all-done.window_ref = bf16[8,136,128]{2,1,0:T(8,128)(2,1)S(1)} async-done(((bf16[8,136,128]{2,1,0:T(8,128)(2,1)}), bf16[8,136,128]{2,1,0:T(8,128)(2,1)S(1)}, u32[]{:S(2)}, u32[]{:S(2)}) %all-to-all-start) | async-done | bytes 278560 | tf_op jit(solution)/shard_map/all_to_all | solution.py:527
  26.2 1.0 %shard_map.84 = (bf16[16,72,128]{2,1,0:T(8,128)(2,1)}, f32[8,128]{1,0:T(8,128)S(1)}) custom-call(bf16[8,136,128]{2,1,0:T(8,128)(2,1)S(1)} %all-to-all-done.window_ref, bf16[2,64,512]{2,1,0:T(8,128)(2,1)S(1)} %get-tuple-element.17.weight_ref, f32[8,128]{1,0:T(8,128)S(1)} %get-tuple-element.18.column_ref), custom_call_target="tpu_custom_call" | custom-call | tf_op jit(solution)/shard_map/pallas_call | solution.py:480
  27.3 0.0 copy-start
  27.3 7.3 %all-to-all-start.1 = ((bf16[16,72,128]{2,1,0:T(8,128)(2,1)}), bf16[16,72,128]{2,1,0:T(8,128)(2,1)S(1)}, u32[]{:S(2)}, u32[]{:S(2)}) async-start(bf16[16,72,128]{2,1,0:T(8,128)(2,1)} %get-tuple-element.24), calls=%async_computation.1 | async-start | bytes 589824 | tf_op jit(solution)/shard_map/all_to_all | solution.py:551
  34.6 2.0 %shard_map.85 = (bf16[512,2304]{1,0:T(8,128)(2,1)S(1)}, f32[2,16,1152]{2,1,0:T(8,128)S(1)}, f32[2,32,1152]{2,1,0:T(8,128)S(1)}, f32[8,128]{1,0:T(8,128)S(1)}) custom-call(f32[8,128]{1,0:T(8,128)S(1)} %get-tuple-element.19.after_ref.edge_ref, f32[32,128]{1,0:T(8,128)} %bitcast.1, f32[5]{0:T(128)} %taps_hbm.1), custom_call_target="tpu_custom_call" | custom-call | flops 16777216 | bytes 8388608 | tf_op jit(solution)/shard_map/pallas_call | solution.py:480
  36.6 16.5 %all-to-all-done.1.lifted_ref = bf16[16,72,128]{2,1,0:T(8,128)(2,1)S(1)} async-done(((bf16[16,72,128]{2,1,0:T(8,128)(2,1)}), bf16[16,72,128]{2,1,0:T(8,128)(2,1)S(1)}, u32[]{:S(2)}, u32[]{:S(2)}) %all-to-all-start.1) | async-done | bytes 294944 | tf_op jit(solution)/shard_map/all_to_all | solution.py:551
  53.1 2.9 %shard_map.86 = (f32[4,264,128]{2,1,0:T(8,128)}, f32[8,128]{1,0:T(8,128)S(1)}) custom-call(f32[8,128]{1,0:T(8,128)S(1)} %get-tuple-element.20.tap_rows_ref, bf16[512,2304]{1,0:T(8,128)(2,1)S(1)} %get-tuple-element.21.near_ref, f32[2,16,1152]{2,1,0:T(8,128)S(1)} %get-tuple-element.22.fine_ref, f32[2,32,1152]{2,1,0:T(8,128)S(1)} %get-tuple-element.23.coarse_ref, ...), custom_call_target="tpu_custom_call" | custom-call | tf_op jit(solution)/shard_map/pallas_call | solution.py:480
  56.0 4.3 %all-to-all-start.2 = ((f32[4,264,128]{2,1,0:T(8,128)}), f32[4,264,128]{2,1,0:T(8,128)S(1)}, u32[]{:S(2)}, u32[]{:S(2)}) async-start(f32[4,264,128]{2,1,0:T(8,128)} %get-tuple-element.25), calls=%async_computation.2 | async-start | bytes 1081344 | tf_op jit(solution)/shard_map/all_to_all | solution.py:585
  60.3 0.0 copy-done
  60.3 1.8 %shard_map.87 = (f32[2,64,256]{2,1,0:T(8,128)S(1)}, f32[8,128]{1,0:T(8,128)S(1)}) custom-call(f32[2]{0:T(128)S(1)} %copy-done, f32[2,64,256]{2,1,0:T(8,128)} %image_hbm.5, f32[8,128]{1,0:T(8,128)S(1)} %get-tuple-element.26.edge_ref), custom_call_target="tpu_custom_call" | custom-call | flops 16777216 | bytes 8388608 | tf_op jit(solution)/shard_map/pallas_call | solution.py:480
  62.1 6.7 %all-to-all-done.2.refs_1_ = f32[4,264,128]{2,1,0:T(8,128)S(1)} async-done(((f32[4,264,128]{2,1,0:T(8,128)}), f32[4,264,128]{2,1,0:T(8,128)S(1)}, u32[]{:S(2)}, u32[]{:S(2)}) %all-to-all-start.2) | async-done | bytes 540704 | tf_op jit(solution)/shard_map/all_to_all | solution.py:585
  68.8 1.6 %shard_map.88 = f32[2,64,256]{2,1,0:T(8,128)} custom-call(f32[2]{0:T(128)S(1)} %copy-done, f32[4,264,128]{2,1,0:T(8,128)S(1)} %all-to-all-done.2.refs_1_, f32[2,64,256]{2,1,0:T(8,128)S(1)} %get-tuple-element.27.refs_2_, f32[8,128]{1,0:T(8,128)S(1)} %get-tuple-element.28.refs_3_), custom_call_target="tpu_custom_call" | custom-call | tf_op jit(solution)/shard_map/pallas_call | solution.py:480
Async XLA Ops:
  0.0 18.5 %collective-permute-start = (bf16[64,512]{1,0:T(8,128)(2,1)}, bf16[64,512]{1,0:T(8,128)(2,1)S(1)}, u32[]{:S(2)}, u32[]{:S(2)}) collective-permute-start(bf16[64,512]{1,0:T(8,128)(2,1)} %weight_hbm.1), channel_id=1, source_target_pairs={{0,264},{1,265},{2,266},{3,267},{4,268},{5,269},{6,270},{7,271},{1... | collective-permute-start | bytes 196616 | tf_op jit(solution)/shard_map/ppermute | solution.py:508
  14.0 12.2 %all-to-all-start = ((bf16[8,136,128]{2,1,0:T(8,128)(2,1)}), bf16[8,136,128]{2,1,0:T(8,128)(2,1)S(1)}, u32[]{:S(2)}, u32[]{:S(2)}) async-start(bf16[8,136,128]{2,1,0:T(8,128)(2,1)} %shard_map.82), calls=%async_computation | async-start | bytes 557056 | tf_op jit(solution)/shard_map/all_to_all | solution.py:527
  27.3 33.1 %copy-start = (f32[2]{0:T(128)S(1)}, f32[2]{0:T(128)}, u32[]{:S(2)}) copy-start(f32[2]{0:T(128)} %refs_0_.1) | copy-start | bytes 28
  27.3 25.9 %all-to-all-start.1 = ((bf16[16,72,128]{2,1,0:T(8,128)(2,1)}), bf16[16,72,128]{2,1,0:T(8,128)(2,1)S(1)}, u32[]{:S(2)}, u32[]{:S(2)}) async-start(bf16[16,72,128]{2,1,0:T(8,128)(2,1)} %get-tuple-element.24), calls=%async_computation.1 | async-start | bytes 589824 | tf_op jit(solution)/shard_map/all_to_all | solution.py:551
  56.0 12.8 %all-to-all-start.2 = ((f32[4,264,128]{2,1,0:T(8,128)}), f32[4,264,128]{2,1,0:T(8,128)S(1)}, u32[]{:S(2)}, u32[]{:S(2)}) async-start(f32[4,264,128]{2,1,0:T(8,128)} %get-tuple-element.25), calls=%async_computation.2 | async-start | bytes 1081344 | tf_op jit(solution)/shard_map/all_to_all | solution.py:585

commit v5 on v4

--- a/solution.py
+++ b/solution.py
@@ -80,7 +80,9 @@
     foot_hbm,
     pulse_hbm,
     image_hbm,
+    weight_hbm,
     out_ref,
+    sent_ref,
     start_ref,
     foot_ref,
     pulse_ref,
@@ -98,6 +100,8 @@
         pltpu.make_async_copy(image_hbm.at[:, pl.ds(0, EDGE), :], edge_ref.at[0], sem.at[3]),
         pltpu.make_async_copy(image_hbm.at[:, pl.ds(rows - EDGE, EDGE), :], edge_ref.at[1], sem.at[4]),
     ]
+    handed = pltpu.make_async_copy(weight_hbm, sent_ref, sem.at[5])
+    handed.start()
     for copy in copies:
         copy.start()
     window_ref[...] = jnp.zeros_like(window_ref)
@@ -133,6 +137,7 @@
         edge = [edge_ref[side, comp, line : line + 1, :] for comp in range(comps)]
         edge = [e[:, i * LANES : (i + 1) * LANES] for e in edge for i in range(2)]
         out_ref[to % N_YC, tall:, :] = two_parts(jnp.concatenate(edge, axis=0), spare_ref)
+    handed.wait()
 
 
 def side_columns(image_hbm, weight_hbm, other_ref, out_ref, weight_ref, pad_ref, block_ref, sem):
@@ -220,18 +225,21 @@
 
 
 FINE = 16
+STEP = 2 * TAPS_K + 1
 
 
 def make_table(
     after_ref,
     ramp_hbm,
     taps_hbm,
+    step_hbm,
     near_ref,
     fine_ref,
     coarse_ref,
     tap_rows_ref,
     ramp_ref,
     taps_ref,
+    step_ref,
     rate_ref,
     spare_ref,
     sem,
@@ -240,6 +248,7 @@
     copies = [
         pltpu.make_async_copy(ramp_hbm, ramp_ref, sem.at[0]),
         pltpu.make_async_copy(taps_hbm, taps_ref, sem.at[1]),
+        pltpu.make_async_copy(step_hbm, step_ref, sem.at[2]),
     ]
     for copy in copies:
         copy.start()
@@ -250,6 +259,9 @@
         copy.wait()
     for t in range(2 * TAPS_K + 1):
         tap_rows_ref[t : t + 1, :] = jnp.full((1, LANES), taps_ref[t], F32)
+    scale = 1.0 / math.sqrt(n_groups * LANES)
+    tap_rows_ref[STEP : STEP + 1, :] = jnp.full((1, LANES), step_ref[0] * scale, F32)
+    tap_rows_ref[STEP + 1 : STEP + 2, :] = jnp.full((1, LANES), step_ref[0] * step_ref[1], F32)
 
     lane = lax.broadcasted_iota(jnp.int32, (1, LANES), 1)
     ends = jnp.zeros((1, LANES), F32)
@@ -311,10 +323,13 @@
     column_ref,
     edge_ref,
     out_ref,
+    mine_ref,
     edge_out_ref,
     pad_ref,
     blend_ref,
     far_ref,
+    total_ref,
+    spare_ref,
 ):
     z_hi, z_lo, x, yc = place_of()
     width = lifted_ref.shape[2]
@@ -354,11 +369,14 @@
     for block in range(blocks):
         table_ref = near_ref if block < blocks // 2 else far_ref
         row = block % (blocks // 2) * columns
-        out_ref[block, :columns, :] = jnp.dot(
+        total = jnp.dot(
             table_ref[row : row + columns, :],
             blend_ref[...],
             preferred_element_type=F32,
         )
+        total_ref[block] = total
+        out_ref[block, :columns, :] = total.astype(BF16)
+    mine_ref[...] = total_ref[x]
 
     def came(half, z):
         return joined(lifted_ref[half * Z_LO + z % Z_LO, half_pulses:, :])
@@ -377,52 +395,58 @@
     right = came(z_hi, z_lo + 1)
     right_fixed = with_corners(right, came(1 - z_hi, z_lo + 1), below)
     right = jnp.where(first_band, right_fixed, right)
-    out_ref[:, columns:, :] = jnp.zeros((blocks, EDGE, LANES), F32)
-    out_ref[(x + 1) % N_X, columns : columns + 2, :] = jnp.where(x < N_X - 1, own, left)[2:4]
-    out_ref[(x + N_X - 1) % N_X, columns : columns + 2, :] = jnp.where(x > 0, own, right)[0:2]
-
-
-def variation_inside(step_ref, image_hbm, edge_ref, out_ref, line_ref, pad_ref, flow_ref, sem):
-    comps, rows, columns = image_hbm.shape
-    copies = [
-        pltpu.make_async_copy(
-            image_hbm.at[comp],
-            pad_ref.at[comp, pl.ds(EDGE, rows), pl.ds(LANES, columns)],
-            sem.at[comp],
-        )
-        for comp in range(comps)
-    ]
-    for copy in copies:
-        copy.start()
+    out_ref[:, columns:, :] = jnp.zeros((blocks, EDGE, LANES), BF16)
+    after = two_parts(jnp.where(x < N_X - 1, own, left), spare_ref)
+    before = two_parts(jnp.where(x > 0, own, right), spare_ref)
+    out_ref[(x + 1) % N_X, columns:, :] = after
+    out_ref[(x + N_X - 1) % N_X, columns:, :] = before
+
+
+def finish(
+    rows_ref, sums_ref, mine_ref, edge_ref, image_ref, out_ref, pad_ref, side_ref, flow_ref
+):
+    _, z_lo, x, _ = place_of()
+    group = z_lo * N_X + x
+    comps, rows, columns = image_ref.shape
+    tall = pad_ref.shape[1]
+    total = mine_ref[...]
+    for k in range(1, N_X):
+        total = total + sums_ref[(x + k) % N_X, :columns, :].astype(F32)
+    step, weight = rows_ref[STEP : STEP + 1, :1], rows_ref[STEP + 1 : STEP + 2, :1]
+    total = (total * step).T.reshape(image_ref.shape)
+
+    zero = jnp.zeros((2, LANES), F32)
+    left = joined(sums_ref[(x + N_X - 1) % N_X, columns:, :])[2:4]
+    right = joined(sums_ref[(x + 1) % N_X, columns:, :])[0:2]
+    side_ref[...] = jnp.zeros_like(side_ref)
+    side_ref[0:2, :] = jnp.where(group > 0, left, zero)
+    side_ref[2:4, :] = jnp.where(group < Z_LO * N_X - 1, right, zero)
+    sides = side_ref[...].T[:tall]
+    lane = lax.broadcasted_iota(jnp.int32, (tall, LANES), 1)
+    blank = jnp.zeros((tall, LANES), F32)
+    pad_ref[...] = jnp.zeros_like(pad_ref)
     for comp in range(comps):
-        pad_ref[comp, :, :LANES] = jnp.zeros((LANES, LANES), F32)
-        pad_ref[comp, :EDGE, LANES:] = jnp.zeros((EDGE, columns), F32)
-        pad_ref[comp, LOW:, LANES:] = jnp.zeros((LANES - LOW, columns), F32)
+        pad_ref[comp, EDGE : EDGE + rows, LANES : LANES + columns] = image_ref[comp]
         for half in range(2):
             span = pl.ds((1 + half) * LANES, LANES)
             pad_ref[comp, TOP : TOP + 1, span] = edge_ref[2 * comp + half : 2 * comp + half + 1, :]
             pad_ref[comp, LOW : LOW + 1, span] = edge_ref[4 + 2 * comp + half : 5 + 2 * comp + half, :]
-    for copy in copies:
-        copy.wait()
-    line_ref[...] = jnp.zeros_like(line_ref)
-    for comp in range(comps):
-        first = pad_ref[comp, :, LANES : 2 * LANES].T
-        last = pad_ref[comp, :, columns : columns + LANES].T
-        line_ref[comp : comp + 1, :] = first[0:1]
-        line_ref[2 + comp : 3 + comp, :] = last[LANES - 1 : LANES]
+        pad_ref[comp, :, :LANES] = jnp.where(lane == LANES - 1, sides[:, comp : comp + 1], blank)
+        pad_ref[comp, :, LANES + columns :] = jnp.where(
+            lane == 0, sides[:, 2 + comp : 3 + comp], blank
+        )
 
     high, wide = rows + EDGE, columns + LANES
-    lane = lax.broadcasted_iota(jnp.int32, (high, wide), 1)
-    whole = (lane >= LANES) & (lane < wide - 1)
     row_step, col_step = [], []
     square = jnp.zeros((high, wide), F32) + smooth_eps
     for comp in range(comps):
         here = pad_ref[comp, :high, :]
-        row_step.append(pad_ref[comp, 1 : high + 1, :] - here)
-        col_step.append(pltpu.roll(here, wide - 1, 1) - here)
+        following = pltpu.roll(here, here.shape[1] - 1, 1)[:, :wide]
+        here = here[:, :wide]
+        row_step.append(pad_ref[comp, 1 : high + 1, :wide] - here)
+        col_step.append(following - here)
         square = square + row_step[-1] * row_step[-1] + col_step[-1] * col_step[-1]
-    inverse = jnp.where(whole, lax.rsqrt(square), jnp.zeros_like(square))
-    weight = step_ref[0] * step_ref[1]
+    inverse = lax.rsqrt(square)
     for comp in range(comps):
         row_flow = row_step[comp] * inverse
         col_flow = col_step[comp] * inverse
@@ -430,44 +454,7 @@
         across = col_flow - pltpu.roll(col_flow, 1, 1)
         down = row_flow[EDGE:, LANES:] - flow_ref[EDGE - 1 : high - 1, LANES:]
         variation = -(down + across[EDGE:, LANES:])
-        out_ref[comp] = pad_ref[comp, EDGE:high, LANES:] - weight * variation
-
-
-def finish(scale, step_ref, sums_ref, base_ref, line_ref, out_ref, side_ref):
-    _, z_lo, x, _ = place_of()
-    group = z_lo * N_X + x
-    comps, rows, columns = base_ref.shape
-    total = sums_ref[0, :columns, :]
-    for k in range(1, N_X):
-        total = total + sums_ref[k, :columns, :]
-    total = total.T.reshape(base_ref.shape) * (scale * step_ref[0])
-
-    zero = jnp.zeros((comps, LANES), F32)
-    left = jnp.where(group > 0, sums_ref[(x + N_X - 1) % N_X, columns : columns + comps, :], zero)
-    right = jnp.where(
-        group < Z_LO * N_X - 1, sums_ref[(x + 1) % N_X, columns : columns + comps, :], zero
-    )
-    first, last = line_ref[0:comps, :], line_ref[comps : 2 * comps, :]
-
-    def flows(here, beside):
-        down = pltpu.roll(here, LANES - 1, 1) - here
-        across = beside - here
-        inverse = lax.rsqrt(jnp.sum(down * down + across * across, axis=0, keepdims=True) + smooth_eps)
-        return down * inverse, across * inverse
-
-    side_ref[...] = jnp.zeros_like(side_ref)
-    side_ref[0:comps, :] = flows(left, first)[1]
-    down, across = flows(last, right)
-    side_ref[comps : 2 * comps, :] = pltpu.roll(down, 1, 1) - down - across
-    sides = side_ref[...].T[EDGE : EDGE + rows] * (step_ref[0] * step_ref[1])
-    lane = lax.broadcasted_iota(jnp.int32, (rows, LANES), 1)
-    blank = jnp.zeros((rows, LANES), F32)
-    for comp in range(comps):
-        added = jnp.where(lane == 0, sides[:, comp : comp + 1], blank)
-        out_ref[comp, :, :LANES] = base_ref[comp, :, :LANES] - total[comp, :, :LANES] - added
-        added = jnp.where(lane == LANES - 1, sides[:, comps + comp : comps + comp + 1], blank)
-        tail = columns - LANES
-        out_ref[comp, :, tail:] = base_ref[comp, :, tail:] - total[comp, :, tail:] - added
+        out_ref[comp] = image_ref[comp] - (total[comp] + weight * variation)
 
 
 def in_hbm(*values):
@@ -505,13 +492,15 @@
     columns = image_now.shape[2]
     shape = jax.ShapeDtypeStruct
 
-    other_weight = lax.ppermute(range_to_row_weight, ("aper", "band"), halves_swapped())
     block = window_len // LANES * comps * pulses
-    windows = call(
+    windows, sent_weight = call(
         cut_windows,
-        pltpu.VMEM((N_YC, Z_HI * block + EDGE, LANES), BF16),
-        [HBM, HBM, HBM, HBM],
-        in_hbm(window_start, footprint, pulse_data, image_now),
+        (
+            shape((N_YC, Z_HI * block + EDGE, LANES), BF16),
+            shape(range_to_row_weight.shape, BF16),
+        ),
+        [HBM] * 5,
+        in_hbm(window_start, footprint, pulse_data, image_now, range_to_row_weight),
         [
             pltpu.SMEM(window_start.shape, jnp.int32),
             pltpu.SMEM(footprint.shape, jnp.int32),
@@ -520,9 +509,10 @@
             pltpu.VMEM((pulses * comps * (bins // LANES + 1), LANES), F32),
             pltpu.VMEM((band_count * block, LANES), F32),
             pltpu.VMEM((EDGE, LANES), F32),
-            pltpu.SemaphoreType.DMA((5,)),
+            pltpu.SemaphoreType.DMA((6,)),
         ],
     )
+    other_weight = lax.ppermute(sent_weight, ("aper", "band"), halves_swapped())
     in_plane = [[h * N_YC + i for i in range(N_YC)] for h in range(Z_HI)]
     windows = lax.all_to_all(windows, "band", 0, 0, axis_index_groups=in_plane, tiled=True)
     side, weights = call(
@@ -541,7 +531,7 @@
     lifted, edges = call(
         lift_windows,
         (
-            pltpu.VMEM((N_Z, N_YC * pulses + EDGE, width), BF16),
+            shape((N_Z, N_YC * pulses + EDGE, width), BF16),
             shape((EDGE, LANES), F32),
         ),
         [VMEM] * 3,
@@ -559,49 +549,50 @@
             shape((2, half // FINE, depth), F32),
             shape((EDGE, LANES), F32),
         ),
-        [ANY, HBM, HBM],
-        (edges, *in_hbm(ramp_rate.reshape(groups, LANES), slow_taps)),
+        [ANY, HBM, HBM, HBM],
+        (
+            edges,
+            *in_hbm(ramp_rate.reshape(groups, LANES), slow_taps, step_and_variation_weight),
+        ),
         [
             pltpu.VMEM((groups, LANES), F32),
             pltpu.SMEM(slow_taps.shape, F32),
+            pltpu.SMEM(step_and_variation_weight.shape, F32),
             pltpu.VMEM((2 * EDGE, LANES), F32),
             pltpu.VMEM((2, 2 * half // FINE, LANES), F32),
-            pltpu.SemaphoreType.DMA((2,)),
+            pltpu.SemaphoreType.DMA((3,)),
         ],
         pl.CostEstimate(flops=1 << 24, bytes_accessed=1 << 23, transcendentals=0),
     )
-    sums, edges = call(
+    sums, mine, edges = call(
         sum_pulses,
-        (pltpu.VMEM((N_X, columns + EDGE, width), F32), shape((EDGE, LANES), F32)),
+        (
+            shape((N_X, columns + EDGE, width), BF16),
+            shape((columns, width), F32),
+            shape((EDGE, LANES), F32),
+        ),
         [VMEM] * 7,
         (tap_rows, near, fine, coarse, lifted, side, edges),
         [
             pltpu.VMEM((LANES + 4 * EDGE, width), F32),
             pltpu.VMEM((2 * depth, width), BF16),
             pltpu.VMEM((half, 2 * depth), BF16),
+            pltpu.VMEM((N_X, columns, width), F32),
+            pltpu.VMEM((EDGE, LANES), F32),
         ],
     )
     along_x = [[z * N_X + x for x in range(N_X)] for z in range(Z_LO)]
     sums = lax.all_to_all(sums, "aper", 0, 0, axis_index_groups=along_x, tiled=True)
-    base, lines = call(
-        variation_inside,
-        (shape(image_now.shape, F32), shape((EDGE, LANES), F32)),
-        [SMEM, HBM, VMEM],
-        (step_and_variation_weight, *in_hbm(image_now), edges),
+    return call(
+        finish,
+        shape(image_now.shape, F32),
+        [VMEM] * 5,
+        (tap_rows, sums, mine, edges, image_now),
         [
-            pltpu.VMEM((comps, LANES, columns + LANES), F32),
+            pltpu.VMEM((comps, band_rows + 2 * EDGE, columns + 2 * LANES), F32),
+            pltpu.VMEM((LANES, LANES), F32),
             pltpu.VMEM((band_rows + EDGE, columns + LANES), F32),
-            pltpu.SemaphoreType.DMA((comps,)),
         ],
-        pl.CostEstimate(flops=1 << 24, bytes_accessed=1 << 23, transcendentals=0),
-    )
-    scale = 1.0 / math.sqrt(groups * LANES)
-    return call(
-        lambda *refs: finish(scale, *refs),
-        shape(image_now.shape, F32),
-        [SMEM, VMEM, VMEM, VMEM],
-        (step_and_variation_weight, sums, base, lines),
-        [pltpu.VMEM((LANES, LANES), F32)],
     )
 
 

time: 70.9 us -> 67.8 us (0.956)
  blocking collectives: 0 us -> 10.8 us
  waiting for transfers between devices: 29.8 us -> 23.1 us
  starting transfers between devices: 28 us -> 23.5 us
  Pallas kernels: 12.5 us -> 9.65 us
    all_to_all x0 -> x1, blocking collectives: none -> 10.8 us  [local(): lax.all_to_all(sums, 'aper', 0, 0, axis_index_groups=along_x, tiled=True)]
    all_to_all x1 -> x0, waiting for transfers between devices: 6.68 us -> none  [local(): lax.all_to_all(sums, 'aper', 0, 0, axis_index_groups=along_x, tiled=True)]
    all_to_all x1 -> x0, starting transfers between devices: 4.31 us -> none  [local(): lax.all_to_all(sums, 'aper', 0, 0, axis_index_groups=along_x, tiled=True)]
    pallas_call x7 -> x6, Pallas kernels: 12.5 us -> 9.65 us  [call(): pl.pallas_call(kernel, out_shape=out_shape, in_specs=in_specs, out_specs=...]
  transfers between devices with their start and end apart: 4 -> 3, of which waited for: 3 -> 2; matrix products, arithmetic and copies ran while one was open for 0% -> 0% of each run, Pallas kernels for 10% -> 5%
where the time goes in v5:
time: 67.8 us; the launch traced here: 67.2 us
  starting transfers between devices  23.5 us (35%)
  waiting for transfers between devices  23.1 us (34%)
  blocking collectives  10.8 us (16%)
  Pallas kernels  9.65 us (14%)
    all_to_all x1, waiting for transfers between devices, local(): lax.all_to_all(lifted, ('aper', 'band'), 0, 0, axis_index_groups=z_rings(...  16.5 us
    ppermute x1, starting transfers between devices, local(): other_weight = lax.ppermute(sent_weight, ('aper', 'band'), halves_swapped())  11.8 us
    all_to_all x1, blocking collectives, local(): lax.all_to_all(sums, 'aper', 0, 0, axis_index_groups=along_x, tiled=True)  10.8 us
    pallas_call x6, Pallas kernels, call(): pl.pallas_call(kernel, out_shape=out_shape, in_specs=in_specs, out_specs=...  9.65 us
    all_to_all x1, starting transfers between devices, local(): lax.all_to_all(lifted, ('aper', 'band'), 0, 0, axis_index_groups=z_rings(...  7.21 us
    all_to_all x1, waiting for transfers between devices, local(): lax.all_to_all(windows, 'band', 0, 0, axis_index_groups=in_plane, tiled=T...  6.64 us
    all_to_all x1, starting transfers between devices, local(): lax.all_to_all(windows, 'band', 0, 0, axis_index_groups=in_plane, tiled=T...  4.48 us
  transfers between devices with their start and end apart: 3, of which 2 were waited for; matrix products, arithmetic and copies ran while one was open for 0% of the time, Pallas kernels for 5%

profile of v5, /device:TPU:32, one launch (start us, length us, event | category | flops | bytes accessed | tf_op | source)
XLA Modules:
  0.0 67.2 jit_solution(5041394589111037798)
XLA Ops:
  0.0 2.2 %shard_map.82 = (bf16[8,136,128]{2,1,0:T(8,128)(2,1)}, bf16[64,512]{1,0:T(8,128)(2,1)S(1)}) custom-call(s32[8,16]{1,0:T(8,128)} %start_hbm.1, s32[8,8]{1,0:T(8,128)} %foot_hbm.1, bf16[2,8,8192]{2,1,0:T(8,128)(2,1)} %pulse_hbm.1, f32[2,64,256]{2,1,0:T(8,128)} %image_ref.1, bf16[64,512]{1,0:T(8,128)(2,1)} %weight_hbm.3), custom_call_target="tpu_custom_call" | custom-call | tf_op jit(solution)/shard_map/pallas_call | solution.py:467
  2.2 11.8 %collective-permute-start = (bf16[64,512]{1,0:T(8,128)(2,1)S(1)}, bf16[64,512]{1,0:T(8,128)(2,1)S(1)}, u32[]{:S(2)}, u32[]{:S(2)}) collective-permute-start(bf16[64,512]{1,0:T(8,128)(2,1)S(1)} %get-tuple-element.19), channel_id=1, source_target_pairs={{0,264},{1,265},{2,266},{3,267},{4,268},{5,269},{6,270},{7,271},{1... | collective-permute-start | bytes 196616 | tf_op jit(solution)/shard_map/ppermute | solution.py:515
  14.1 4.5 %all-to-all-start = ((bf16[8,136,128]{2,1,0:T(8,128)(2,1)}), bf16[8,136,128]{2,1,0:T(8,128)(2,1)S(1)}, u32[]{:S(2)}, u32[]{:S(2)}) async-start(bf16[8,136,128]{2,1,0:T(8,128)(2,1)} %get-tuple-element.18), calls=%async_computation | async-start | bytes 557056 | tf_op jit(solution)/shard_map/all_to_all | solution.py:517
  18.6 0.0 collective-permute-done.other_ref
  18.6 1.1 %shard_map.83 = (f32[8,128]{1,0:T(8,128)S(1)}, bf16[2,64,512]{2,1,0:T(8,128)(2,1)S(1)}) custom-call(f32[2,64,256]{2,1,0:T(8,128)} %image_ref.1, bf16[64,512]{1,0:T(8,128)(2,1)} %weight_hbm.3, bf16[64,512]{1,0:T(8,128)(2,1)S(1)} %collective-permute-done.other_ref), custom_call_target="tpu_custom_call" | custom-call | flops 17179869184 | bytes 134217728 | tf_op jit(solution)/shard_map/pallas_call | solution.py:467
  19.6 6.6 %all-to-all-done.window_ref = bf16[8,136,128]{2,1,0:T(8,128)(2,1)S(1)} async-done(((bf16[8,136,128]{2,1,0:T(8,128)(2,1)}), bf16[8,136,128]{2,1,0:T(8,128)(2,1)S(1)}, u32[]{:S(2)}, u32[]{:S(2)}) %all-to-all-start) | async-done | bytes 278560 | tf_op jit(solution)/shard_map/all_to_all | solution.py:517
  26.3 0.0 copy-start
  26.3 1.0 %shard_map.84 = (bf16[16,72,128]{2,1,0:T(8,128)(2,1)}, f32[8,128]{1,0:T(8,128)S(1)}) custom-call(bf16[8,136,128]{2,1,0:T(8,128)(2,1)S(1)} %all-to-all-done.window_ref, bf16[2,64,512]{2,1,0:T(8,128)(2,1)S(1)} %get-tuple-element.20.weight_ref, f32[8,128]{1,0:T(8,128)S(1)} %get-tuple-element.21.column_ref), custom_call_target="tpu_custom_call" | custom-call | tf_op jit(solution)/shard_map/pallas_call | solution.py:467
  27.3 7.2 %all-to-all-start.1 = ((bf16[16,72,128]{2,1,0:T(8,128)(2,1)}), bf16[16,72,128]{2,1,0:T(8,128)(2,1)S(1)}, u32[]{:S(2)}, u32[]{:S(2)}) async-start(bf16[16,72,128]{2,1,0:T(8,128)(2,1)} %get-tuple-element.27), calls=%async_computation.1 | async-start | bytes 589824 | tf_op jit(solution)/shard_map/all_to_all | solution.py:541
  34.5 2.0 %shard_map.85 = (bf16[512,2304]{1,0:T(8,128)(2,1)S(1)}, f32[2,16,1152]{2,1,0:T(8,128)S(1)}, f32[2,32,1152]{2,1,0:T(8,128)S(1)}, f32[8,128]{1,0:T(8,128)S(1)}) custom-call(f32[8,128]{1,0:T(8,128)S(1)} %get-tuple-element.22.after_ref.edge_ref, f32[32,128]{1,0:T(8,128)} %bitcast.1, f32[5]{0:T(128)} %taps_hbm.1, f32[2]{0:T(128)} %step_hbm.1), custom_call_target="tpu_custom_call" | custom-call | flops 16777216 | bytes 8388608 | tf_op jit(solution)/shard_map/pallas_call | solution.py:467
  36.5 16.5 %all-to-all-done.1.lifted_ref = bf16[16,72,128]{2,1,0:T(8,128)(2,1)S(1)} async-done(((bf16[16,72,128]{2,1,0:T(8,128)(2,1)}), bf16[16,72,128]{2,1,0:T(8,128)(2,1)S(1)}, u32[]{:S(2)}, u32[]{:S(2)}) %all-to-all-start.1) | async-done | bytes 294944 | tf_op jit(solution)/shard_map/all_to_all | solution.py:541
  53.0 2.1 %shard_map.86 = (bf16[4,264,128]{2,1,0:T(8,128)(2,1)S(1)}, f32[256,128]{1,0:T(8,128)S(1)}, f32[8,128]{1,0:T(8,128)S(1)}) custom-call(f32[8,128]{1,0:T(8,128)S(1)} %get-tuple-element.23.tap_rows_ref.rows_ref, bf16[512,2304]{1,0:T(8,128)(2,1)S(1)} %get-tuple-element.24.near_ref, f32[2,16,1152]{2,1,0:T(8,128)S(1)} %get-tuple-element.25.fine_ref, ...), custom_call_target="tpu_custom_call" | custom-call | tf_op jit(solution)/shard_map/pallas_call | solution.py:467
  55.1 10.8 %all_to_all.15.sums_ref = bf16[4,264,128]{2,1,0:T(8,128)(2,1)S(1)} all-to-all(bf16[4,264,128]{2,1,0:T(8,128)(2,1)S(1)} %get-tuple-element.28), channel_id=1, replica_groups={{0,16,32,48},{64,80,96,112},{128,144,160,176},{192,208,224,240},{256,27..., dimensions={0} | all-to-all | bytes 540672 | tf_op jit(solution)/shard_map/all_to_all | solution.py:585
  65.9 0.0 copy-done
  65.9 1.2 %shard_map.87 = f32[2,64,256]{2,1,0:T(8,128)} custom-call(f32[8,128]{1,0:T(8,128)S(1)} %get-tuple-element.23.tap_rows_ref.rows_ref, bf16[4,264,128]{2,1,0:T(8,128)(2,1)S(1)} %all_to_all.15.sums_ref, f32[256,128]{1,0:T(8,128)S(1)} %get-tuple-element.29.mine_ref, f32[8,128]{1,0:T(8,128)S(1)} %get-tuple-element.30.edge_ref, f32[2,64,256]{2,1,0:T(8,128)S(1)} %copy-done), custom_call_target="tpu_custom_call" | custom-call | tf_op jit(solution)/shard_map/pallas_call | solution.py:467
Async XLA Ops:
  2.2 16.3 %collective-permute-start = (bf16[64,512]{1,0:T(8,128)(2,1)S(1)}, bf16[64,512]{1,0:T(8,128)(2,1)S(1)}, u32[]{:S(2)}, u32[]{:S(2)}) collective-permute-start(bf16[64,512]{1,0:T(8,128)(2,1)S(1)} %get-tuple-element.19), channel_id=1, source_target_pairs={{0,264},{1,265},{2,266},{3,267},{4,268},{5,269},{6,270},{7,271},{1... | collective-permute-start | bytes 196616 | tf_op jit(solution)/shard_map/ppermute | solution.py:515
  14.1 12.2 %all-to-all-start = ((bf16[8,136,128]{2,1,0:T(8,128)(2,1)}), bf16[8,136,128]{2,1,0:T(8,128)(2,1)S(1)}, u32[]{:S(2)}, u32[]{:S(2)}) async-start(bf16[8,136,128]{2,1,0:T(8,128)(2,1)} %get-tuple-element.18), calls=%async_computation | async-start | bytes 557056 | tf_op jit(solution)/shard_map/all_to_all | solution.py:517
  26.3 39.7 %copy-start = (f32[2,64,256]{2,1,0:T(8,128)S(1)}, f32[2,64,256]{2,1,0:T(8,128)}, u32[]{:S(2)}) copy-start(f32[2,64,256]{2,1,0:T(8,128)} %image_ref.1) | copy-start | bytes 393220
  27.3 25.7 %all-to-all-start.1 = ((bf16[16,72,128]{2,1,0:T(8,128)(2,1)}), bf16[16,72,128]{2,1,0:T(8,128)(2,1)S(1)}, u32[]{:S(2)}, u32[]{:S(2)}) async-start(bf16[16,72,128]{2,1,0:T(8,128)(2,1)} %get-tuple-element.27), calls=%async_computation.1 | async-start | bytes 589824 | tf_op jit(solution)/shard_map/all_to_all | solution.py:541

commit v6 on v5

--- a/solution.py
+++ b/solution.py
@@ -1,3 +1,4 @@
+import functools
 import math
 
 import jax
@@ -12,6 +13,7 @@
 EDGE = 8
 Z_HI, Z_LO, N_X, N_YC = 2, 8, 4, 8
 N_Z = Z_HI * Z_LO
+FIRST_Z = 8
 smooth_eps = 0.05
 BF16, F32 = jnp.bfloat16, jnp.float32
 VMEM = pl.BlockSpec(memory_space=pltpu.VMEM)
@@ -25,11 +27,16 @@
 
 
 def z_rings():
+    order = [(FIRST_Z + k) % N_Z for k in range(N_Z)]
     return [
-        [device_index(z // Z_LO, z % Z_LO, x, yc) for z in range(N_Z)]
+        [device_index(z // Z_LO, z % Z_LO, x, yc) for z in order]
         for x in range(N_X)
         for yc in range(N_YC)
     ]
+
+
+def in_ring(z):
+    return (z + N_Z - FIRST_Z) % N_Z
 
 
 def halves_swapped():
@@ -75,69 +82,72 @@
     return columns
 
 
-def cut_windows(
-    start_hbm,
-    foot_hbm,
-    pulse_hbm,
-    image_hbm,
-    weight_hbm,
-    out_ref,
-    sent_ref,
-    start_ref,
-    foot_ref,
-    pulse_ref,
-    edge_ref,
-    flat_ref,
-    window_ref,
-    spare_ref,
-    sem,
-):
-    rows = image_hbm.shape[1]
-    copies = [
-        pltpu.make_async_copy(pulse_hbm, pulse_ref, sem.at[0]),
-        pltpu.make_async_copy(start_hbm, start_ref, sem.at[1]),
-        pltpu.make_async_copy(foot_hbm, foot_ref, sem.at[2]),
-        pltpu.make_async_copy(image_hbm.at[:, pl.ds(0, EDGE), :], edge_ref.at[0], sem.at[3]),
-        pltpu.make_async_copy(image_hbm.at[:, pl.ds(rows - EDGE, EDGE), :], edge_ref.at[1], sem.at[4]),
-    ]
-    handed = pltpu.make_async_copy(weight_hbm, sent_ref, sem.at[5])
-    handed.start()
-    for copy in copies:
-        copy.start()
-    window_ref[...] = jnp.zeros_like(window_ref)
-    comps, pulses, bins = pulse_ref.shape
-    parts = bins // LANES
-    pitch = comps * (parts + 1)
-    block = window_ref.shape[0] // (Z_HI * N_YC)
-    for copy in copies:
-        copy.wait()
-    for part in range(parts):
-        for comp in range(comps):
-            flat_ref[pl.ds(part * comps + comp, pulses, stride=pitch), :] = pulse_ref[
-                comp, :, part * LANES : (part + 1) * LANES
-            ].astype(F32)
-    lane = lax.broadcasted_iota(jnp.int32, (block // pulses, LANES), 1)
-    for pulse in range(pulses):
-        for k in range(foot_ref.shape[1]):
-            band = foot_ref[pulse, k]
-            start = start_ref[pulse, band]
-            row = pulse * pitch + comps * (start >> 7)
-            shift = start & (LANES - 1)
-            here = flat_ref[pl.ds(row, block // pulses), :]
-            following = flat_ref[pl.ds(row + comps, block // pulses), :]
-            both = jnp.where(lane >= shift, here, following)
-            both = pltpu.roll(both, (LANES - shift) & (LANES - 1), 1)
-            place = ((band & (N_YC - 1)) * Z_HI + (band >> 3)) * block + pulse
-            window_ref[pl.ds(place, block // pulses, stride=pulses), :] = both
-    tall = Z_HI * block
-    out_ref[:, :tall, :] = window_ref[...].astype(BF16).reshape(N_YC, tall, LANES)
-    out_ref[:, tall:, :] = jnp.zeros((N_YC, EDGE, LANES), BF16)
-    yc = place_of()[3]
-    for side, line, to in ((0, 0, yc + N_YC - 1), (1, EDGE - 1, yc + 1)):
-        edge = [edge_ref[side, comp, line : line + 1, :] for comp in range(comps)]
-        edge = [e[:, i * LANES : (i + 1) * LANES] for e in edge for i in range(2)]
-        out_ref[to % N_YC, tall:, :] = two_parts(jnp.concatenate(edge, axis=0), spare_ref)
-    handed.wait()
+def cut_windows(wanted, start_hbm, foot_hbm, pulse_hbm, image_hbm, *refs):
+    (
+        out_hbm,
+        start_ref,
+        foot_ref,
+        pulse_ref,
+        edge_ref,
+        flat_ref,
+        window_ref,
+        packed_ref,
+        spare_ref,
+        sem,
+        out_sem,
+    ) = refs[-11:]
+
+    @pl.when(place_of()[0] == wanted)
+    def _():
+        rows = image_hbm.shape[1]
+        copies = [
+            pltpu.make_async_copy(pulse_hbm, pulse_ref, sem.at[0]),
+            pltpu.make_async_copy(start_hbm, start_ref, sem.at[1]),
+            pltpu.make_async_copy(foot_hbm, foot_ref, sem.at[2]),
+            pltpu.make_async_copy(image_hbm.at[:, pl.ds(0, EDGE), :], edge_ref.at[0], sem.at[3]),
+            pltpu.make_async_copy(image_hbm.at[:, pl.ds(rows - EDGE, EDGE), :], edge_ref.at[1], sem.at[4]),
+        ]
+        for copy in copies:
+            copy.start()
+        window_ref[...] = jnp.zeros_like(window_ref)
+        comps, pulses, bins = pulse_ref.shape
+        parts = bins // LANES
+        pitch = comps * (parts + 1)
+        block = window_ref.shape[0] // (Z_HI * N_YC)
+        for copy in copies:
+            copy.wait()
+        for part in range(parts):
+            for comp in range(comps):
+                flat_ref[pl.ds(part * comps + comp, pulses, stride=pitch), :] = pulse_ref[
+                    comp, :, part * LANES : (part + 1) * LANES
+                ].astype(F32)
+        lane = lax.broadcasted_iota(jnp.int32, (block // pulses, LANES), 1)
+        for pulse in range(pulses):
+            for k in range(foot_ref.shape[1]):
+                band = foot_ref[pulse, k]
+                start = start_ref[pulse, band]
+                row = pulse * pitch + comps * (start >> 7)
+                shift = start & (LANES - 1)
+                here = flat_ref[pl.ds(row, block // pulses), :]
+                following = flat_ref[pl.ds(row + comps, block // pulses), :]
+                both = jnp.where(lane >= shift, here, following)
+                both = pltpu.roll(both, (LANES - shift) & (LANES - 1), 1)
+                place = ((band & (N_YC - 1)) * Z_HI + (band >> 3)) * block + pulse
+                window_ref[pl.ds(place, block // pulses, stride=pulses), :] = both
+        tall = Z_HI * block
+        packed_ref[:, tall:, :] = jnp.zeros((N_YC, EDGE, LANES), BF16)
+        yc = place_of()[3]
+        for side, line, to in ((0, 0, yc + N_YC - 1), (1, EDGE - 1, yc + 1)):
+            edge = [edge_ref[side, comp, line : line + 1, :] for comp in range(comps)]
+            edge = [e[:, i * LANES : (i + 1) * LANES] for e in edge for i in range(2)]
+            packed_ref[to % N_YC, tall:, :] = two_parts(jnp.concatenate(edge, axis=0), spare_ref)
+        leaving = []
+        for to in range(N_YC):
+            packed_ref[to, :tall, :] = window_ref[to * tall : (to + 1) * tall, :].astype(BF16)
+            leaving.append(pltpu.make_async_copy(packed_ref.at[to], out_hbm.at[to], out_sem.at[to]))
+            leaving[-1].start()
+        for copy in leaving:
+            copy.wait()
 
 
 def side_columns(image_hbm, weight_hbm, other_ref, out_ref, weight_ref, pad_ref, block_ref, sem):
@@ -201,8 +211,8 @@
         both = both.reshape(tall, 2 * band_rows).astype(BF16)
         extra = two_parts(extra, spare_ref)
         for z in range(Z_LO):
-            out_ref[z_half * Z_LO + z, :tall, :] = both
-            out_ref[z_half * Z_LO + z, tall:, :] = extra
+            out_ref[in_ring(z_half * Z_LO + z), :tall, :] = both
+            out_ref[in_ring(z_half * Z_LO + z), tall:, :] = extra
 
 
 def sin_cos(angle):
@@ -344,7 +354,7 @@
     for i in range(Z_LO):
         for h in range(Z_HI):
             pad_ref[pl.ds(2 * EDGE + h * half_pulses, half_pulses), :] = lifted_ref[
-                h * Z_LO + i, :half_pulses, :
+                in_ring(h * Z_LO + i), :half_pulses, :
             ].astype(F32)
         blended = jnp.zeros((LANES + 2 * EDGE, width), F32)
         for t in range(2 * TAPS_K + 1):
@@ -379,7 +389,7 @@
     mine_ref[...] = total_ref[x]
 
     def came(half, z):
-        return joined(lifted_ref[half * Z_LO + z % Z_LO, half_pulses:, :])
+        return joined(lifted_ref[in_ring(half * Z_LO + z % Z_LO), half_pulses:, :])
 
     first_band = (z_hi == 1) & (yc == 0)
     last_band = (z_hi == 0) & (yc == N_YC - 1)
@@ -493,26 +503,34 @@
     shape = jax.ShapeDtypeStruct
 
     block = window_len // LANES * comps * pulses
-    windows, sent_weight = call(
-        cut_windows,
-        (
-            shape((N_YC, Z_HI * block + EDGE, LANES), BF16),
-            shape(range_to_row_weight.shape, BF16),
-        ),
-        [HBM] * 5,
-        in_hbm(window_start, footprint, pulse_data, image_now, range_to_row_weight),
-        [
-            pltpu.SMEM(window_start.shape, jnp.int32),
-            pltpu.SMEM(footprint.shape, jnp.int32),
-            pltpu.VMEM(pulse_data.shape, BF16),
-            pltpu.VMEM((2, comps, EDGE, columns), F32),
-            pltpu.VMEM((pulses * comps * (bins // LANES + 1), LANES), F32),
-            pltpu.VMEM((band_count * block, LANES), F32),
-            pltpu.VMEM((EDGE, LANES), F32),
-            pltpu.SemaphoreType.DMA((6,)),
-        ],
-    )
-    other_weight = lax.ppermute(sent_weight, ("aper", "band"), halves_swapped())
+    given = in_hbm(window_start, footprint, pulse_data, image_now)
+    windows = ()
+    weight = range_to_row_weight
+    for wanted in range(Z_HI):
+        windows = pl.pallas_call(
+            functools.partial(cut_windows, wanted),
+            out_shape=pltpu.HBM((N_YC, Z_HI * block + EDGE, LANES), BF16),
+            in_specs=[HBM] * (len(given) + len(windows)),
+            out_specs=HBM,
+            scratch_shapes=[
+                pltpu.SMEM(window_start.shape, jnp.int32),
+                pltpu.SMEM(footprint.shape, jnp.int32),
+                pltpu.VMEM(pulse_data.shape, BF16),
+                pltpu.VMEM((2, comps, EDGE, columns), F32),
+                pltpu.VMEM((pulses * comps * (bins // LANES + 1), LANES), F32),
+                pltpu.VMEM((band_count * block, LANES), F32),
+                pltpu.VMEM((N_YC, Z_HI * block + EDGE, LANES), BF16),
+                pltpu.VMEM((EDGE, LANES), F32),
+                pltpu.SemaphoreType.DMA((5,)),
+                pltpu.SemaphoreType.DMA((N_YC,)),
+            ],
+            input_output_aliases={len(given): 0} if windows else {},
+            compiler_params=pltpu.CompilerParams(vmem_limit_bytes=16 * 1024 * 1024),
+        )(*given, *windows)
+        if wanted == 0:
+            weight, windows = lax.optimization_barrier((weight, windows))
+            other_weight = lax.ppermute(weight, ("aper", "band"), halves_swapped())
+            windows = (windows,)
     in_plane = [[h * N_YC + i for i in range(N_YC)] for h in range(Z_HI)]
     windows = lax.all_to_all(windows, "band", 0, 0, axis_index_groups=in_plane, tiled=True)
     side, weights = call(

time: 67.8 us -> 65.6 us (0.968)
  waiting for transfers between devices: 23.1 us -> 18.5 us
  starting transfers between devices: 23.5 us -> 25.8 us
    all_to_all x1, waiting for transfers between devices: 16.5 us -> 11.9 us  [local(): lax.all_to_all(lifted, ('aper', 'band'), 0, 0, axis_index_groups=z_rings(...]
    all_to_all x1, starting transfers between devices: 7.21 us -> 11.6 us  [local(): lax.all_to_all(lifted, ('aper', 'band'), 0, 0, axis_index_groups=z_rings(...]
    pallas_call x0 -> x2, Pallas kernels: none -> 2.39 us  [local(): pl.pallas_call(functools.partial(cut_windows, wanted), out_shape=pltpu.HB...]
    ppermute x1, starting transfers between devices: 11.8 us -> 9.7 us  [local(): other_weight = lax.ppermute(weight, ('aper', 'band'), halves_swapped())]
    pallas_call x6 -> x5, Pallas kernels: 9.65 us -> 7.51 us  [call(): pl.pallas_call(kernel, out_shape=out_shape, in_specs=in_specs, out_specs=...]
where the time goes in v6:
time: 65.6 us; the launch traced here: 65.1 us
  starting transfers between devices  25.8 us (39%)
  waiting for transfers between devices  18.5 us (28%)
  blocking collectives  10.8 us (16%)
  Pallas kernels  9.91 us (15%)
    all_to_all x1, waiting for transfers between devices, local(): lax.all_to_all(lifted, ('aper', 'band'), 0, 0, axis_index_groups=z_rings(...  11.9 us
    all_to_all x1, starting transfers between devices, local(): lax.all_to_all(lifted, ('aper', 'band'), 0, 0, axis_index_groups=z_rings(...  11.6 us
    all_to_all x1, blocking collectives, local(): lax.all_to_all(sums, 'aper', 0, 0, axis_index_groups=along_x, tiled=True)  10.8 us
    ppermute x1, starting transfers between devices, local(): other_weight = lax.ppermute(weight, ('aper', 'band'), halves_swapped())  9.7 us
    pallas_call x5, Pallas kernels, call(): pl.pallas_call(kernel, out_shape=out_shape, in_specs=in_specs, out_specs=...  7.51 us
    all_to_all x1, waiting for transfers between devices, local(): lax.all_to_all(windows, 'band', 0, 0, axis_index_groups=in_plane, tiled=T...  6.64 us
    all_to_all x1, starting transfers between devices, local(): lax.all_to_all(windows, 'band', 0, 0, axis_index_groups=in_plane, tiled=T...  4.48 us
    pallas_call x2, Pallas kernels, local(): pl.pallas_call(functools.partial(cut_windows, wanted), out_shape=pltpu.HB...  2.39 us
  transfers between devices with their start and end apart: 3, of which 2 were waited for; matrix products, arithmetic and copies ran while one was open for 0% of the time, Pallas kernels for 5%

profile of v6, /device:TPU:32, one launch (start us, length us, event | category | flops | bytes accessed | tf_op | source)
XLA Modules:
  0.0 65.1 jit_solution(3135665249563398338)
XLA Ops:
  0.0 2.3 %shard_map.82.refs_0_ = bf16[8,136,128]{2,1,0:T(8,128)(2,1)} custom-call(s32[8,16]{1,0:T(8,128)} %start_hbm.3, s32[8,8]{1,0:T(8,128)} %foot_hbm.3, bf16[2,8,8192]{2,1,0:T(8,128)(2,1)} %pulse_hbm.3, f32[2,64,256]{2,1,0:T(8,128)} %image_ref.1), custom_call_target="tpu_custom_call" | custom-call | tf_op jit(solution)/shard_map/pallas_call | solution.py:510
  2.3 9.7 %collective-permute-start = (bf16[64,512]{1,0:T(8,128)(2,1)}, bf16[64,512]{1,0:T(8,128)(2,1)S(1)}, u32[]{:S(2)}, u32[]{:S(2)}) collective-permute-start(bf16[64,512]{1,0:T(8,128)(2,1)} %weight_hbm.1), channel_id=1, source_target_pairs={{0,264},{1,265},{2,266},{3,267},{4,268},{5,269},{6,270},{7,271},{1... | collective-permute-start | bytes 196616 | tf_op jit(solution)/shard_map/ppermute | solution.py:532
  12.0 0.1 shard_map.83
  12.1 4.5 %all-to-all-start = ((bf16[8,136,128]{2,1,0:T(8,128)(2,1)}), bf16[8,136,128]{2,1,0:T(8,128)(2,1)S(1)}, u32[]{:S(2)}, u32[]{:S(2)}) async-start(bf16[8,136,128]{2,1,0:T(8,128)(2,1)} %shard_map.83), calls=%async_computation | async-start | bytes 557056 | tf_op jit(solution)/shard_map/all_to_all | solution.py:535
  16.6 0.0 collective-permute-done.other_ref
  16.6 1.1 %shard_map.84 = (f32[8,128]{1,0:T(8,128)S(1)}, bf16[2,64,512]{2,1,0:T(8,128)(2,1)S(1)}) custom-call(f32[2,64,256]{2,1,0:T(8,128)} %image_ref.1, bf16[64,512]{1,0:T(8,128)(2,1)} %weight_hbm.1, bf16[64,512]{1,0:T(8,128)(2,1)S(1)} %collective-permute-done.other_ref), custom_call_target="tpu_custom_call" | custom-call | flops 17179869184 | bytes 134217728 | tf_op jit(solution)/shard_map/pallas_call | solution.py:477
  17.7 6.6 %all-to-all-done.window_ref = bf16[8,136,128]{2,1,0:T(8,128)(2,1)S(1)} async-done(((bf16[8,136,128]{2,1,0:T(8,128)(2,1)}), bf16[8,136,128]{2,1,0:T(8,128)(2,1)S(1)}, u32[]{:S(2)}, u32[]{:S(2)}) %all-to-all-start) | async-done | bytes 278560 | tf_op jit(solution)/shard_map/all_to_all | solution.py:535
  24.3 0.0 copy-start
  24.3 1.0 %shard_map.85 = (bf16[16,72,128]{2,1,0:T(8,128)(2,1)}, f32[8,128]{1,0:T(8,128)S(1)}) custom-call(bf16[8,136,128]{2,1,0:T(8,128)(2,1)S(1)} %all-to-all-done.window_ref, bf16[2,64,512]{2,1,0:T(8,128)(2,1)S(1)} %get-tuple-element.20.weight_ref, f32[8,128]{1,0:T(8,128)S(1)} %get-tuple-element.21.column_ref), custom_call_target="tpu_custom_call" | custom-call | tf_op jit(solution)/shard_map/pallas_call | solution.py:477
  25.3 11.6 %all-to-all-start.1 = ((bf16[16,72,128]{2,1,0:T(8,128)(2,1)}), bf16[16,72,128]{2,1,0:T(8,128)(2,1)S(1)}, u32[]{:S(2)}, u32[]{:S(2)}) async-start(bf16[16,72,128]{2,1,0:T(8,128)(2,1)} %get-tuple-element.27), calls=%async_computation.1 | async-start | bytes 589824 | tf_op jit(solution)/shard_map/all_to_all | solution.py:559
  36.9 2.0 %shard_map.86 = (bf16[512,2304]{1,0:T(8,128)(2,1)S(1)}, f32[2,16,1152]{2,1,0:T(8,128)S(1)}, f32[2,32,1152]{2,1,0:T(8,128)S(1)}, f32[8,128]{1,0:T(8,128)S(1)}) custom-call(f32[8,128]{1,0:T(8,128)S(1)} %get-tuple-element.22.after_ref.edge_ref, f32[32,128]{1,0:T(8,128)} %bitcast.1, f32[5]{0:T(128)} %taps_hbm.1, f32[2]{0:T(128)} %step_hbm.1), custom_call_target="tpu_custom_call" | custom-call | flops 16777216 | bytes 8388608 | tf_op jit(solution)/shard_map/pallas_call | solution.py:477
  39.0 11.9 %all-to-all-done.1.lifted_ref = bf16[16,72,128]{2,1,0:T(8,128)(2,1)S(1)} async-done(((bf16[16,72,128]{2,1,0:T(8,128)(2,1)}), bf16[16,72,128]{2,1,0:T(8,128)(2,1)S(1)}, u32[]{:S(2)}, u32[]{:S(2)}) %all-to-all-start.1) | async-done | bytes 294944 | tf_op jit(solution)/shard_map/all_to_all | solution.py:559
  50.9 2.2 %shard_map.87 = (bf16[4,264,128]{2,1,0:T(8,128)(2,1)S(1)}, f32[256,128]{1,0:T(8,128)S(1)}, f32[8,128]{1,0:T(8,128)S(1)}) custom-call(f32[8,128]{1,0:T(8,128)S(1)} %get-tuple-element.23.tap_rows_ref.rows_ref, bf16[512,2304]{1,0:T(8,128)(2,1)S(1)} %get-tuple-element.24.near_ref, f32[2,16,1152]{2,1,0:T(8,128)S(1)} %get-tuple-element.25.fine_ref, ...), custom_call_target="tpu_custom_call" | custom-call | tf_op jit(solution)/shard_map/pallas_call | solution.py:477
  53.0 10.8 %all_to_all.15.sums_ref = bf16[4,264,128]{2,1,0:T(8,128)(2,1)S(1)} all-to-all(bf16[4,264,128]{2,1,0:T(8,128)(2,1)S(1)} %get-tuple-element.28), channel_id=1, replica_groups={{0,16,32,48},{64,80,96,112},{128,144,160,176},{192,208,224,240},{256,27..., dimensions={0} | all-to-all | bytes 540672 | tf_op jit(solution)/shard_map/all_to_all | solution.py:603
  63.9 0.0 copy-done
  63.9 1.2 %shard_map.88 = f32[2,64,256]{2,1,0:T(8,128)} custom-call(f32[8,128]{1,0:T(8,128)S(1)} %get-tuple-element.23.tap_rows_ref.rows_ref, bf16[4,264,128]{2,1,0:T(8,128)(2,1)S(1)} %all_to_all.15.sums_ref, f32[256,128]{1,0:T(8,128)S(1)} %get-tuple-element.29.mine_ref, f32[8,128]{1,0:T(8,128)S(1)} %get-tuple-element.30.edge_ref, f32[2,64,256]{2,1,0:T(8,128)S(1)} %copy-done), custom_call_target="tpu_custom_call" | custom-call | tf_op jit(solution)/shard_map/pallas_call | solution.py:477
Async XLA Ops:
  2.3 14.3 %collective-permute-start = (bf16[64,512]{1,0:T(8,128)(2,1)}, bf16[64,512]{1,0:T(8,128)(2,1)S(1)}, u32[]{:S(2)}, u32[]{:S(2)}) collective-permute-start(bf16[64,512]{1,0:T(8,128)(2,1)} %weight_hbm.1), channel_id=1, source_target_pairs={{0,264},{1,265},{2,266},{3,267},{4,268},{5,269},{6,270},{7,271},{1... | collective-permute-start | bytes 196616 | tf_op jit(solution)/shard_map/ppermute | solution.py:532
  12.1 12.2 %all-to-all-start = ((bf16[8,136,128]{2,1,0:T(8,128)(2,1)}), bf16[8,136,128]{2,1,0:T(8,128)(2,1)S(1)}, u32[]{:S(2)}, u32[]{:S(2)}) async-start(bf16[8,136,128]{2,1,0:T(8,128)(2,1)} %shard_map.83), calls=%async_computation | async-start | bytes 557056 | tf_op jit(solution)/shard_map/all_to_all | solution.py:535
  24.3 39.5 %copy-start = (f32[2,64,256]{2,1,0:T(8,128)S(1)}, f32[2,64,256]{2,1,0:T(8,128)}, u32[]{:S(2)}) copy-start(f32[2,64,256]{2,1,0:T(8,128)} %image_ref.1) | copy-start | bytes 393220
  25.3 25.5 %all-to-all-start.1 = ((bf16[16,72,128]{2,1,0:T(8,128)(2,1)}), bf16[16,72,128]{2,1,0:T(8,128)(2,1)S(1)}, u32[]{:S(2)}, u32[]{:S(2)}) async-start(bf16[16,72,128]{2,1,0:T(8,128)(2,1)} %get-tuple-element.27), calls=%async_computation.1 | async-start | bytes 589824 | tf_op jit(solution)/shard_map/all_to_all | solution.py:559

commit v7 on v6

--- a/solution.py
+++ b/solution.py
@@ -174,8 +174,9 @@
 
 
 def lift_windows(
-    window_ref, weight_ref, column_ref, out_ref, edge_ref, spare_ref
+    window_ref, weight_ref, column_ref, after_ref, out_ref, edge_ref, spare_ref
 ):
+    del after_ref
     z_hi, _, _, yc = place_of()
     sources, height = window_ref.shape[0], window_ref.shape[1] - EDGE
     half = height // Z_HI
@@ -376,16 +377,12 @@
         for a in range(far_ref.shape[0] // FINE):
             coarse = coarse_ref[0, a : a + 1, span], coarse_ref[1, a : a + 1, span]
             fill(far_ref, a * FINE, i, coarse, fine)
-    for block in range(blocks):
-        table_ref = near_ref if block < blocks // 2 else far_ref
-        row = block % (blocks // 2) * columns
-        total = jnp.dot(
-            table_ref[row : row + columns, :],
-            blend_ref[...],
-            preferred_element_type=F32,
-        )
-        total_ref[block] = total
-        out_ref[block, :columns, :] = total.astype(BF16)
+    for side, table_ref in enumerate((near_ref, far_ref)):
+        total = jnp.dot(table_ref[...], blend_ref[...], preferred_element_type=F32)
+        for block in range(blocks // 2):
+            part = total[block * columns : (block + 1) * columns]
+            total_ref[side * (blocks // 2) + block] = part
+            out_ref[side * (blocks // 2) + block, :columns, :] = part.astype(BF16)
     mine_ref[...] = total_ref[x]
 
     def came(half, z):
@@ -531,6 +528,35 @@
             weight, windows = lax.optimization_barrier((weight, windows))
             other_weight = lax.ppermute(weight, ("aper", "band"), halves_swapped())
             windows = (windows,)
+    half = N_X * columns // 2
+    depth = (Z_LO + 1) * LANES
+    near, fine, coarse, tap_rows = call(
+        make_table,
+        (
+            shape((half, 2 * depth), BF16),
+            shape((2, FINE, depth), F32),
+            shape((2, half // FINE, depth), F32),
+            shape((EDGE, LANES), F32),
+        ),
+        [HBM] * 4,
+        (
+            *in_hbm(
+                windows,
+                ramp_rate.reshape(groups, LANES),
+                slow_taps,
+                step_and_variation_weight,
+            ),
+        ),
+        [
+            pltpu.VMEM((groups, LANES), F32),
+            pltpu.SMEM(slow_taps.shape, F32),
+            pltpu.SMEM(step_and_variation_weight.shape, F32),
+            pltpu.VMEM((2 * EDGE, LANES), F32),
+            pltpu.VMEM((2, 2 * half // FINE, LANES), F32),
+            pltpu.SemaphoreType.DMA((3,)),
+        ],
+        pl.CostEstimate(flops=1 << 24, bytes_accessed=1 << 23, transcendentals=0),
+    )
     in_plane = [[h * N_YC + i for i in range(N_YC)] for h in range(Z_HI)]
     windows = lax.all_to_all(windows, "band", 0, 0, axis_index_groups=in_plane, tiled=True)
     side, weights = call(
@@ -552,36 +578,11 @@
             shape((N_Z, N_YC * pulses + EDGE, width), BF16),
             shape((EDGE, LANES), F32),
         ),
-        [VMEM] * 3,
-        (windows, weights, side),
+        [VMEM] * 3 + [ANY],
+        (windows, weights, side, tap_rows),
         [pltpu.VMEM((EDGE, LANES), F32)],
     )
     lifted = lax.all_to_all(lifted, ("aper", "band"), 0, 0, axis_index_groups=z_rings(), tiled=True)
-    depth = (Z_LO + 1) * LANES
-    half = N_X * columns // 2
-    near, fine, coarse, tap_rows = call(
-        make_table,
-        (
-            shape((half, 2 * depth), BF16),
-            shape((2, FINE, depth), F32),
-            shape((2, half // FINE, depth), F32),
-            shape((EDGE, LANES), F32),
-        ),
-        [ANY, HBM, HBM, HBM],
-        (
-            edges,
-            *in_hbm(ramp_rate.reshape(groups, LANES), slow_taps, step_and_variation_weight),
-        ),
-        [
-            pltpu.VMEM((groups, LANES), F32),
-            pltpu.SMEM(slow_taps.shape, F32),
-            pltpu.SMEM(step_and_variation_weight.shape, F32),
-            pltpu.VMEM((2 * EDGE, LANES), F32),
-            pltpu.VMEM((2, 2 * half // FINE, LANES), F32),
-            pltpu.SemaphoreType.DMA((3,)),
-        ],
-        pl.CostEstimate(flops=1 << 24, bytes_accessed=1 << 23, transcendentals=0),
-    )
     sums, mine, edges = call(
         sum_pulses,
         (

time: 65.6 us -> 64.1 us (0.977)
  blocking collectives: 10.8 us -> 36.2 us
  waiting for transfers between devices: 18.5 us -> 4.57 us
  starting transfers between devices: 25.8 us -> 14.2 us
  Pallas kernels: 9.91 us -> 8.64 us
    all_to_all x0 -> x1, blocking collectives: none -> 25.3 us  [local(): lax.all_to_all(lifted, ('aper', 'band'), 0, 0, axis_index_groups=z_rings(...]
    all_to_all x1 -> x0, waiting for transfers between devices: 11.9 us -> none  [local(): lax.all_to_all(lifted, ('aper', 'band'), 0, 0, axis_index_groups=z_rings(...]
    all_to_all x1 -> x0, starting transfers between devices: 11.6 us -> none  [local(): lax.all_to_all(lifted, ('aper', 'band'), 0, 0, axis_index_groups=z_rings(...]
    all_to_all x1, waiting for transfers between devices: 6.64 us -> 4.57 us  [local(): lax.all_to_all(windows, 'band', 0, 0, axis_index_groups=in_plane, tiled=T...]
    pallas_call x5, Pallas kernels: 7.51 us -> 6.27 us  [call(): pl.pallas_call(kernel, out_shape=out_shape, in_specs=in_specs, out_specs=...]
  transfers between devices with their start and end apart: 3 -> 2, of which waited for: 2 -> 1; matrix products, arithmetic and copies ran while one was open for 0% -> 0% of each run, Pallas kernels for 5% -> 5%
where the time goes in v7:
time: 64.1 us; the launch traced here: 63.6 us
  blocking collectives  36.2 us (56%)
  starting transfers between devices  14.2 us (22%)
  Pallas kernels  8.64 us (13%)
  waiting for transfers between devices  4.57 us (7%)
    all_to_all x1, blocking collectives, local(): lax.all_to_all(lifted, ('aper', 'band'), 0, 0, axis_index_groups=z_rings(...  25.3 us
    all_to_all x1, blocking collectives, local(): lax.all_to_all(sums, 'aper', 0, 0, axis_index_groups=along_x, tiled=True)  10.8 us
    ppermute x1, starting transfers between devices, local(): other_weight = lax.ppermute(weight, ('aper', 'band'), halves_swapped())  9.72 us
    pallas_call x5, Pallas kernels, call(): pl.pallas_call(kernel, out_shape=out_shape, in_specs=in_specs, out_specs=...  6.27 us
    all_to_all x1, waiting for transfers between devices, local(): lax.all_to_all(windows, 'band', 0, 0, axis_index_groups=in_plane, tiled=T...  4.57 us
    all_to_all x1, starting transfers between devices, local(): lax.all_to_all(windows, 'band', 0, 0, axis_index_groups=in_plane, tiled=T...  4.48 us
    pallas_call x2, Pallas kernels, local(): pl.pallas_call(functools.partial(cut_windows, wanted), out_shape=pltpu.HB...  2.37 us
  transfers between devices with their start and end apart: 2, of which 1 were waited for; matrix products, arithmetic and copies ran while one was open for 0% of the time, Pallas kernels for 5%

profile of v7, /device:TPU:32, one launch (start us, length us, event | category | flops | bytes accessed | tf_op | source)
XLA Modules:
  0.0 63.6 jit_solution(7299974854518606123)
XLA Ops:
  0.0 2.2 %shard_map.82.refs_0_ = bf16[8,136,128]{2,1,0:T(8,128)(2,1)} custom-call(s32[8,16]{1,0:T(8,128)} %start_hbm.3, s32[8,8]{1,0:T(8,128)} %foot_hbm.3, bf16[2,8,8192]{2,1,0:T(8,128)(2,1)} %pulse_hbm.3, f32[2,64,256]{2,1,0:T(8,128)} %image_ref.1), custom_call_target="tpu_custom_call" | custom-call | tf_op jit(solution)/shard_map/pallas_call | solution.py:507
  2.2 9.7 %collective-permute-start = (bf16[64,512]{1,0:T(8,128)(2,1)}, bf16[64,512]{1,0:T(8,128)(2,1)S(1)}, u32[]{:S(2)}, u32[]{:S(2)}) collective-permute-start(bf16[64,512]{1,0:T(8,128)(2,1)} %weight_hbm.1), channel_id=1, source_target_pairs={{0,264},{1,265},{2,266},{3,267},{4,268},{5,269},{6,270},{7,271},{1... | collective-permute-start | bytes 196616 | tf_op jit(solution)/shard_map/ppermute | solution.py:529
  12.0 0.1 shard_map.83.after_ref
  12.1 4.5 %all-to-all-start = ((bf16[8,136,128]{2,1,0:T(8,128)(2,1)}), bf16[8,136,128]{2,1,0:T(8,128)(2,1)S(1)}, u32[]{:S(2)}, u32[]{:S(2)}) async-start(bf16[8,136,128]{2,1,0:T(8,128)(2,1)} %shard_map.83.after_ref), calls=%async_computation | async-start | bytes 557056 | tf_op jit(solution)/shard_map/all_to_all | solution.py:561
  16.6 2.0 %shard_map.84 = (bf16[512,2304]{1,0:T(8,128)(2,1)S(1)}, f32[2,16,1152]{2,1,0:T(8,128)S(1)}, f32[2,32,1152]{2,1,0:T(8,128)S(1)}, f32[8,128]{1,0:T(8,128)S(1)}) custom-call(bf16[8,136,128]{2,1,0:T(8,128)(2,1)} %shard_map.83.after_ref, f32[32,128]{1,0:T(8,128)} %bitcast.1, f32[5]{0:T(128)} %taps_hbm.1, f32[2]{0:T(128)} %step_hbm.1), custom_call_target="tpu_custom_call" | custom-call | flops 16777216 | bytes 8388608 | tf_op jit(solution)/shard_map/pallas_call | solution.py:474
  18.7 0.0 collective-permute-done.other_ref
  18.7 1.1 %shard_map.85 = (f32[8,128]{1,0:T(8,128)S(1)}, bf16[2,64,512]{2,1,0:T(8,128)(2,1)S(1)}) custom-call(f32[2,64,256]{2,1,0:T(8,128)} %image_ref.1, bf16[64,512]{1,0:T(8,128)(2,1)} %weight_hbm.1, bf16[64,512]{1,0:T(8,128)(2,1)S(1)} %collective-permute-done.other_ref), custom_call_target="tpu_custom_call" | custom-call | flops 17179869184 | bytes 134217728 | tf_op jit(solution)/shard_map/pallas_call | solution.py:474
  19.7 0.0 copy-start
  19.7 4.6 %all-to-all-done.window_ref = bf16[8,136,128]{2,1,0:T(8,128)(2,1)S(1)} async-done(((bf16[8,136,128]{2,1,0:T(8,128)(2,1)}), bf16[8,136,128]{2,1,0:T(8,128)(2,1)S(1)}, u32[]{:S(2)}, u32[]{:S(2)}) %all-to-all-start) | async-done | bytes 278560 | tf_op jit(solution)/shard_map/all_to_all | solution.py:561
  24.3 0.3 shard_map.86
  24.6 25.3 %all_to_all.15.lifted_ref = bf16[16,72,128]{2,1,0:T(8,128)(2,1)S(1)} all-to-all(bf16[16,72,128]{2,1,0:T(8,128)(2,1)S(1)} %get-tuple-element.26), channel_id=1, replica_groups={{8,72,136,200,264,328,392,456,0,64,128,192,256,320,384,448},{9,73,137,2..., dimensions={0} | all-to-all | bytes 589824 | tf_op jit(solution)/shard_map/all_to_all | solution.py:585
  49.9 1.6 %shard_map.87 = (bf16[4,264,128]{2,1,0:T(8,128)(2,1)S(1)}, f32[256,128]{1,0:T(8,128)S(1)}, f32[8,128]{1,0:T(8,128)S(1)}) custom-call(f32[8,128]{1,0:T(8,128)S(1)} %get-tuple-element.19.after_ref.tap_rows_ref.rows_ref, bf16[512,2304]{1,0:T(8,128)(2,1)S(1)} %get-tuple-element.20.near_ref, f32[2,16,1152]{2,1,0:T(8,128)S(1)} %get-tuple-element.21.fine_ref, ...), custom_call_target="tpu_custom_call" | custom-call | tf_op jit(solution)/shard_map/pallas_call | solution.py:474
  51.6 10.8 %all_to_all.16.sums_ref = bf16[4,264,128]{2,1,0:T(8,128)(2,1)S(1)} all-to-all(bf16[4,264,128]{2,1,0:T(8,128)(2,1)S(1)} %get-tuple-element.28), channel_id=1, replica_groups={{0,16,32,48},{64,80,96,112},{128,144,160,176},{192,208,224,240},{256,27..., dimensions={0} | all-to-all | bytes 540672 | tf_op jit(solution)/shard_map/all_to_all | solution.py:604
  62.4 0.0 copy-done
  62.4 1.2 %shard_map.88 = f32[2,64,256]{2,1,0:T(8,128)} custom-call(f32[8,128]{1,0:T(8,128)S(1)} %get-tuple-element.19.after_ref.tap_rows_ref.rows_ref, bf16[4,264,128]{2,1,0:T(8,128)(2,1)S(1)} %all_to_all.16.sums_ref, f32[256,128]{1,0:T(8,128)S(1)} %get-tuple-element.29.mine_ref, f32[8,128]{1,0:T(8,128)S(1)} %get-tuple-element.30.edge_ref, f32[2,64,256]{2,1,0:T(8,128)S(1)} %copy-done), custom_call_target="tpu_custom_call" | custom-call | tf_op jit(solution)/shard_map/pallas_call | solution.py:474
Async XLA Ops:
  2.2 16.4 %collective-permute-start = (bf16[64,512]{1,0:T(8,128)(2,1)}, bf16[64,512]{1,0:T(8,128)(2,1)S(1)}, u32[]{:S(2)}, u32[]{:S(2)}) collective-permute-start(bf16[64,512]{1,0:T(8,128)(2,1)} %weight_hbm.1), channel_id=1, source_target_pairs={{0,264},{1,265},{2,266},{3,267},{4,268},{5,269},{6,270},{7,271},{1... | collective-permute-start | bytes 196616 | tf_op jit(solution)/shard_map/ppermute | solution.py:529
  12.1 12.2 %all-to-all-start = ((bf16[8,136,128]{2,1,0:T(8,128)(2,1)}), bf16[8,136,128]{2,1,0:T(8,128)(2,1)S(1)}, u32[]{:S(2)}, u32[]{:S(2)}) async-start(bf16[8,136,128]{2,1,0:T(8,128)(2,1)} %shard_map.83.after_ref), calls=%async_computation | async-start | bytes 557056 | tf_op jit(solution)/shard_map/all_to_all | solution.py:561
  19.7 42.7 %copy-start = (f32[2,64,256]{2,1,0:T(8,128)S(1)}, f32[2,64,256]{2,1,0:T(8,128)}, u32[]{:S(2)}) copy-start(f32[2,64,256]{2,1,0:T(8,128)} %image_ref.1) | copy-start | bytes 393220

commit v8 on v7

--- a/solution.py
+++ b/solution.py
@@ -113,7 +113,7 @@
         comps, pulses, bins = pulse_ref.shape
         parts = bins // LANES
         pitch = comps * (parts + 1)
-        block = window_ref.shape[0] // (Z_HI * N_YC)
+        block = (window_ref.shape[0] - EDGE) // (Z_HI * N_YC)
         for copy in copies:
             copy.wait()
         for part in range(parts):
@@ -135,15 +135,16 @@
                 place = ((band & (N_YC - 1)) * Z_HI + (band >> 3)) * block + pulse
                 window_ref[pl.ds(place, block // pulses, stride=pulses), :] = both
         tall = Z_HI * block
-        packed_ref[:, tall:, :] = jnp.zeros((N_YC, EDGE, LANES), BF16)
+        packed_ref[:, tall // EDGE] = jnp.zeros((N_YC, EDGE, LANES), BF16)
         yc = place_of()[3]
         for side, line, to in ((0, 0, yc + N_YC - 1), (1, EDGE - 1, yc + 1)):
             edge = [edge_ref[side, comp, line : line + 1, :] for comp in range(comps)]
             edge = [e[:, i * LANES : (i + 1) * LANES] for e in edge for i in range(2)]
-            packed_ref[to % N_YC, tall:, :] = two_parts(jnp.concatenate(edge, axis=0), spare_ref)
+            packed_ref[to % N_YC, tall // EDGE] = two_parts(jnp.concatenate(edge, axis=0), spare_ref)
         leaving = []
         for to in range(N_YC):
-            packed_ref[to, :tall, :] = window_ref[to * tall : (to + 1) * tall, :].astype(BF16)
+            part = window_ref[to * tall : (to + 1) * tall, :].reshape(tall // EDGE, EDGE, LANES)
+            packed_ref[to, : tall // EDGE] = part.astype(BF16)
             leaving.append(pltpu.make_async_copy(packed_ref.at[to], out_hbm.at[to], out_sem.at[to]))
             leaving[-1].start()
         for copy in leaving:
@@ -178,15 +179,16 @@
 ):
     del after_ref
     z_hi, _, _, yc = place_of()
-    sources, height = window_ref.shape[0], window_ref.shape[1] - EDGE
+    sources, height = window_ref.shape[0], window_ref.shape[1] - 1
     half = height // Z_HI
     band_rows, window_len = weight_ref.shape[1:]
     parts = window_len // LANES
-    rows = half // parts
+    tiles = half // parts
+    rows = tiles * EDGE
     tall = sources * rows // 2
 
-    above = joined(window_ref[(yc + N_YC - 1) % N_YC, height:, :])
-    below = joined(window_ref[(yc + 1) % N_YC, height:, :])
+    above = joined(window_ref[(yc + N_YC - 1) % N_YC, height])
+    below = joined(window_ref[(yc + 1) % N_YC, height])
     foreign = jnp.where(yc == 0, above, below)
     above = jnp.where(yc > 0, above, jnp.zeros_like(above))
     below = jnp.where(yc < N_YC - 1, below, jnp.zeros_like(below))
@@ -199,8 +201,9 @@
         extra = jnp.where(z_half == z_hi, columns, foreign)
         lifted = jnp.zeros((sources * rows, band_rows), F32)
         for part in range(parts):
-            first = z_half * half + part * rows
-            piece = window_ref[:, pl.ds(first, rows), :].reshape(sources * rows, LANES)
+            first = z_half * half + part * tiles
+            piece = window_ref[:, pl.ds(first, tiles)].astype(F32)
+            piece = piece.reshape(sources * rows, LANES).astype(BF16)
             lifted = lifted + lax.dot_general(
                 piece,
                 weight_ref[z_half, :, part * LANES : (part + 1) * LANES],
@@ -209,11 +212,11 @@
             )
         lifted = lifted.reshape(sources, 2, rows // 2, band_rows)
         both = jnp.concatenate([lifted[:, 0], lifted[:, 1]], axis=-1)
-        both = both.reshape(tall, 2 * band_rows).astype(BF16)
+        both = both.reshape(tall // EDGE, EDGE, 2 * band_rows).astype(BF16)
         extra = two_parts(extra, spare_ref)
         for z in range(Z_LO):
-            out_ref[in_ring(z_half * Z_LO + z), :tall, :] = both
-            out_ref[in_ring(z_half * Z_LO + z), tall:, :] = extra
+            out_ref[in_ring(z_half * Z_LO + z), : tall // EDGE] = both
+            out_ref[in_ring(z_half * Z_LO + z), tall // EDGE] = extra
 
 
 def sin_cos(angle):
@@ -343,20 +346,22 @@
     spare_ref,
 ):
     z_hi, z_lo, x, yc = place_of()
-    width = lifted_ref.shape[2]
+    width = lifted_ref.shape[3]
     half_pulses = LANES // Z_HI
     main = Z_LO * LANES
     depth = main + LANES
-    blocks, columns = out_ref.shape[0], out_ref.shape[1] - EDGE
+    blocks, tiles = out_ref.shape[0], out_ref.shape[1] - 1
+    columns = tiles * EDGE
 
     zero = jnp.zeros((2 * EDGE, width), F32)
     pad_ref[: 2 * EDGE] = zero
     pad_ref[2 * EDGE + LANES :] = zero
     for i in range(Z_LO):
         for h in range(Z_HI):
-            pad_ref[pl.ds(2 * EDGE + h * half_pulses, half_pulses), :] = lifted_ref[
-                in_ring(h * Z_LO + i), :half_pulses, :
-            ].astype(F32)
+            part = lifted_ref[in_ring(h * Z_LO + i), : half_pulses // EDGE].astype(F32)
+            pad_ref[pl.ds(2 * EDGE + h * half_pulses, half_pulses), :] = part.reshape(
+                half_pulses, width
+            )
         blended = jnp.zeros((LANES + 2 * EDGE, width), F32)
         for t in range(2 * TAPS_K + 1):
             blended = blended + tap_rows_ref[t : t + 1, :] * pad_ref[
@@ -382,11 +387,13 @@
         for block in range(blocks // 2):
             part = total[block * columns : (block + 1) * columns]
             total_ref[side * (blocks // 2) + block] = part
-            out_ref[side * (blocks // 2) + block, :columns, :] = part.astype(BF16)
+            out_ref[side * (blocks // 2) + block, :tiles] = part.reshape(tiles, EDGE, width).astype(
+                BF16
+            )
     mine_ref[...] = total_ref[x]
 
     def came(half, z):
-        return joined(lifted_ref[in_ring(half * Z_LO + z % Z_LO), half_pulses:, :])
+        return joined(lifted_ref[in_ring(half * Z_LO + z % Z_LO), half_pulses // EDGE])
 
     first_band = (z_hi == 1) & (yc == 0)
     last_band = (z_hi == 0) & (yc == N_YC - 1)
@@ -402,11 +409,11 @@
     right = came(z_hi, z_lo + 1)
     right_fixed = with_corners(right, came(1 - z_hi, z_lo + 1), below)
     right = jnp.where(first_band, right_fixed, right)
-    out_ref[:, columns:, :] = jnp.zeros((blocks, EDGE, LANES), BF16)
+    out_ref[:, tiles] = jnp.zeros((blocks, EDGE, LANES), BF16)
     after = two_parts(jnp.where(x < N_X - 1, own, left), spare_ref)
     before = two_parts(jnp.where(x > 0, own, right), spare_ref)
-    out_ref[(x + 1) % N_X, columns:, :] = after
-    out_ref[(x + N_X - 1) % N_X, columns:, :] = before
+    out_ref[(x + 1) % N_X, tiles] = after
+    out_ref[(x + N_X - 1) % N_X, tiles] = before
 
 
 def finish(
@@ -418,13 +425,14 @@
     tall = pad_ref.shape[1]
     total = mine_ref[...]
     for k in range(1, N_X):
-        total = total + sums_ref[(x + k) % N_X, :columns, :].astype(F32)
+        part = sums_ref[(x + k) % N_X, : columns // EDGE].astype(F32)
+        total = total + part.reshape(total.shape)
     step, weight = rows_ref[STEP : STEP + 1, :1], rows_ref[STEP + 1 : STEP + 2, :1]
     total = (total * step).T.reshape(image_ref.shape)
 
     zero = jnp.zeros((2, LANES), F32)
-    left = joined(sums_ref[(x + N_X - 1) % N_X, columns:, :])[2:4]
-    right = joined(sums_ref[(x + 1) % N_X, columns:, :])[0:2]
+    left = joined(sums_ref[(x + N_X - 1) % N_X, columns // EDGE])[2:4]
+    right = joined(sums_ref[(x + 1) % N_X, columns // EDGE])[0:2]
     side_ref[...] = jnp.zeros_like(side_ref)
     side_ref[0:2, :] = jnp.where(group > 0, left, zero)
     side_ref[2:4, :] = jnp.where(group < Z_LO * N_X - 1, right, zero)
@@ -506,7 +514,7 @@
     for wanted in range(Z_HI):
         windows = pl.pallas_call(
             functools.partial(cut_windows, wanted),
-            out_shape=pltpu.HBM((N_YC, Z_HI * block + EDGE, LANES), BF16),
+            out_shape=pltpu.HBM((N_YC, Z_HI * block // EDGE + 1, EDGE, LANES), BF16),
             in_specs=[HBM] * (len(given) + len(windows)),
             out_specs=HBM,
             scratch_shapes=[
@@ -514,9 +522,9 @@
                 pltpu.SMEM(footprint.shape, jnp.int32),
                 pltpu.VMEM(pulse_data.shape, BF16),
                 pltpu.VMEM((2, comps, EDGE, columns), F32),
-                pltpu.VMEM((pulses * comps * (bins // LANES + 1), LANES), F32),
-                pltpu.VMEM((band_count * block, LANES), F32),
-                pltpu.VMEM((N_YC, Z_HI * block + EDGE, LANES), BF16),
+                pltpu.VMEM(((pulses + 1) * comps * (bins // LANES + 1), LANES), F32),
+                pltpu.VMEM((band_count * block + EDGE, LANES), F32),
+                pltpu.VMEM((N_YC, Z_HI * block // EDGE + 1, EDGE, LANES), BF16),
                 pltpu.VMEM((EDGE, LANES), F32),
                 pltpu.SemaphoreType.DMA((5,)),
                 pltpu.SemaphoreType.DMA((N_YC,)),
@@ -575,7 +583,7 @@
     lifted, edges = call(
         lift_windows,
         (
-            shape((N_Z, N_YC * pulses + EDGE, width), BF16),
+            shape((N_Z, N_YC * pulses // EDGE + 1, EDGE, width), BF16),
             shape((EDGE, LANES), F32),
         ),
         [VMEM] * 3 + [ANY],
@@ -586,7 +594,7 @@
     sums, mine, edges = call(
         sum_pulses,
         (
-            shape((N_X, columns + EDGE, width), BF16),
+            shape((N_X, columns // EDGE + 1, EDGE, width), BF16),
             shape((columns, width), F32),
             shape((EDGE, LANES), F32),
         ),

time: 64.1 us -> 64.1 us (level)
  no operation moved by 1% of the time
where the time goes in v8:
time: 64.1 us; the launch traced here: 63.6 us
  blocking collectives  36.2 us (56%)
  starting transfers between devices  14.2 us (22%)
  Pallas kernels  8.64 us (13%)
  waiting for transfers between devices  4.57 us (7%)
    all_to_all x1, blocking collectives, local(): lax.all_to_all(lifted, ('aper', 'band'), 0, 0, axis_index_groups=z_rings(...  25.3 us
    all_to_all x1, blocking collectives, local(): lax.all_to_all(sums, 'aper', 0, 0, axis_index_groups=along_x, tiled=True)  10.8 us
    ppermute x1, starting transfers between devices, local(): other_weight = lax.ppermute(weight, ('aper', 'band'), halves_swapped())  9.72 us
    pallas_call x5, Pallas kernels, call(): pl.pallas_call(kernel, out_shape=out_shape, in_specs=in_specs, out_specs=...  6.27 us
    all_to_all x1, waiting for transfers between devices, local(): lax.all_to_all(windows, 'band', 0, 0, axis_index_groups=in_plane, tiled=T...  4.57 us
    all_to_all x1, starting transfers between devices, local(): lax.all_to_all(windows, 'band', 0, 0, axis_index_groups=in_plane, tiled=T...  4.48 us
    pallas_call x2, Pallas kernels, local(): pl.pallas_call(functools.partial(cut_windows, wanted), out_shape=pltpu.HB...  2.37 us
  transfers between devices with their start and end apart: 2, of which 1 were waited for; matrix products, arithmetic and copies ran while one was open for 0% of the time, Pallas kernels for 5%

profile of v8, /device:TPU:32, one launch (start us, length us, event | category | flops | bytes accessed | tf_op | source)
XLA Modules:
  0.0 63.6 jit_solution(6579945450613086470)
XLA Ops:
  0.0 2.2 %shard_map.82.refs_0_ = bf16[8,17,8,128]{3,2,1,0:T(8,128)(2,1)} custom-call(s32[8,16]{1,0:T(8,128)} %start_hbm.3, s32[8,8]{1,0:T(8,128)} %foot_hbm.3, bf16[2,8,8192]{2,1,0:T(8,128)(2,1)} %pulse_hbm.3, f32[2,64,256]{2,1,0:T(8,128)} %image_ref.1), custom_call_target="tpu_custom_call" | custom-call | tf_op jit(solution)/shard_map/pallas_call | solution.py:515
  2.2 9.7 %collective-permute-start = (bf16[64,512]{1,0:T(8,128)(2,1)}, bf16[64,512]{1,0:T(8,128)(2,1)S(1)}, u32[]{:S(2)}, u32[]{:S(2)}) collective-permute-start(bf16[64,512]{1,0:T(8,128)(2,1)} %weight_hbm.1), channel_id=1, source_target_pairs={{0,264},{1,265},{2,266},{3,267},{4,268},{5,269},{6,270},{7,271},{1... | collective-permute-start | bytes 196616 | tf_op jit(solution)/shard_map/ppermute | solution.py:537
  12.0 0.1 shard_map.83.after_ref
  12.1 4.5 %all-to-all-start = ((bf16[8,17,8,128]{3,2,1,0:T(8,128)(2,1)}), bf16[8,17,8,128]{3,2,1,0:T(8,128)(2,1)S(1)}, u32[]{:S(2)}, u32[]{:S(2)}) async-start(bf16[8,17,8,128]{3,2,1,0:T(8,128)(2,1)} %shard_map.83.after_ref), calls=%async_computation | async-start | bytes 557056 | tf_op jit(solution)/shard_map/all_to_all | solution.py:569
  16.6 2.0 %shard_map.84 = (bf16[512,2304]{1,0:T(8,128)(2,1)S(1)}, f32[2,16,1152]{2,1,0:T(8,128)S(1)}, f32[2,32,1152]{2,1,0:T(8,128)S(1)}, f32[8,128]{1,0:T(8,128)S(1)}) custom-call(bf16[8,17,8,128]{3,2,1,0:T(8,128)(2,1)} %shard_map.83.after_ref, f32[32,128]{1,0:T(8,128)} %bitcast.1, f32[5]{0:T(128)} %taps_hbm.1, f32[2]{0:T(128)} %step_hbm.1), custom_call_target="tpu_custom_call" | custom-call | flops 16777216 | bytes 8388608 | tf_op jit(solution)/shard_map/pallas_call | solution.py:482
  18.7 0.0 collective-permute-done.other_ref
  18.7 1.1 %shard_map.85 = (f32[8,128]{1,0:T(8,128)S(1)}, bf16[2,64,512]{2,1,0:T(8,128)(2,1)S(1)}) custom-call(f32[2,64,256]{2,1,0:T(8,128)} %image_ref.1, bf16[64,512]{1,0:T(8,128)(2,1)} %weight_hbm.1, bf16[64,512]{1,0:T(8,128)(2,1)S(1)} %collective-permute-done.other_ref), custom_call_target="tpu_custom_call" | custom-call | flops 17179869184 | bytes 134217728 | tf_op jit(solution)/shard_map/pallas_call | solution.py:482
  19.7 0.0 copy-start
  19.7 4.6 %all-to-all-done.window_ref = bf16[8,17,8,128]{3,2,1,0:T(8,128)(2,1)S(1)} async-done(((bf16[8,17,8,128]{3,2,1,0:T(8,128)(2,1)}), bf16[8,17,8,128]{3,2,1,0:T(8,128)(2,1)S(1)}, u32[]{:S(2)}, u32[]{:S(2)}) %all-to-all-start) | async-done | bytes 278560 | tf_op jit(solution)/shard_map/all_to_all | solution.py:569
  24.3 0.3 shard_map.86
  24.6 25.3 %all_to_all.15.lifted_ref = bf16[16,9,8,128]{3,2,1,0:T(8,128)(2,1)S(1)} all-to-all(bf16[16,9,8,128]{3,2,1,0:T(8,128)(2,1)S(1)} %get-tuple-element.26), channel_id=1, replica_groups={{8,72,136,200,264,328,392,456,0,64,128,192,256,320,384,448},{9,73,137,2..., dimensions={0} | all-to-all | bytes 589824 | tf_op jit(solution)/shard_map/all_to_all | solution.py:593
  49.9 1.6 %shard_map.87 = (bf16[4,33,8,128]{3,2,1,0:T(8,128)(2,1)S(1)}, f32[256,128]{1,0:T(8,128)S(1)}, f32[8,128]{1,0:T(8,128)S(1)}) custom-call(f32[8,128]{1,0:T(8,128)S(1)} %get-tuple-element.19.after_ref.tap_rows_ref.rows_ref, bf16[512,2304]{1,0:T(8,128)(2,1)S(1)} %get-tuple-element.20.near_ref, f32[2,16,1152]{2,1,0:T(8,128)S(1)} %get-tuple-element.21.fine_ref, ...), custom_call_target="tpu_custom_call" | custom-call | tf_op jit(solution)/shard_map/pallas_call | solution.py:482
  51.6 10.8 %all_to_all.16.sums_ref = bf16[4,33,8,128]{3,2,1,0:T(8,128)(2,1)S(1)} all-to-all(bf16[4,33,8,128]{3,2,1,0:T(8,128)(2,1)S(1)} %get-tuple-element.28), channel_id=1, replica_groups={{0,16,32,48},{64,80,96,112},{128,144,160,176},{192,208,224,240},{256,27..., dimensions={0} | all-to-all | bytes 540672 | tf_op jit(solution)/shard_map/all_to_all | solution.py:612
  62.4 0.0 copy-done
  62.4 1.2 %shard_map.88 = f32[2,64,256]{2,1,0:T(8,128)} custom-call(f32[8,128]{1,0:T(8,128)S(1)} %get-tuple-element.19.after_ref.tap_rows_ref.rows_ref, bf16[4,33,8,128]{3,2,1,0:T(8,128)(2,1)S(1)} %all_to_all.16.sums_ref, f32[256,128]{1,0:T(8,128)S(1)} %get-tuple-element.29.mine_ref, f32[8,128]{1,0:T(8,128)S(1)} %get-tuple-element.30.edge_ref, f32[2,64,256]{2,1,0:T(8,128)S(1)} %copy-done), custom_call_target="tpu_custom_call" | custom-call | tf_op jit(solution)/shard_map/pallas_call | solution.py:482
Async XLA Ops:
  2.2 16.4 %collective-permute-start = (bf16[64,512]{1,0:T(8,128)(2,1)}, bf16[64,512]{1,0:T(8,128)(2,1)S(1)}, u32[]{:S(2)}, u32[]{:S(2)}) collective-permute-start(bf16[64,512]{1,0:T(8,128)(2,1)} %weight_hbm.1), channel_id=1, source_target_pairs={{0,264},{1,265},{2,266},{3,267},{4,268},{5,269},{6,270},{7,271},{1... | collective-permute-start | bytes 196616 | tf_op jit(solution)/shard_map/ppermute | solution.py:537
  12.1 12.2 %all-to-all-start = ((bf16[8,17,8,128]{3,2,1,0:T(8,128)(2,1)}), bf16[8,17,8,128]{3,2,1,0:T(8,128)(2,1)S(1)}, u32[]{:S(2)}, u32[]{:S(2)}) async-start(bf16[8,17,8,128]{3,2,1,0:T(8,128)(2,1)} %shard_map.83.after_ref), calls=%async_computation | async-start | bytes 557056 | tf_op jit(solution)/shard_map/all_to_all | solution.py:569
  19.7 42.7 %copy-start = (f32[2,64,256]{2,1,0:T(8,128)S(1)}, f32[2,64,256]{2,1,0:T(8,128)}, u32[]{:S(2)}) copy-start(f32[2,64,256]{2,1,0:T(8,128)} %image_ref.1) | copy-start | bytes 393220

commit v9 on v8

--- a/solution.py
+++ b/solution.py
@@ -14,6 +14,8 @@
 Z_HI, Z_LO, N_X, N_YC = 2, 8, 4, 8
 N_Z = Z_HI * Z_LO
 FIRST_Z = 8
+FIRST_YC = 4
+FIRST_X = 2
 smooth_eps = 0.05
 BF16, F32 = jnp.bfloat16, jnp.float32
 VMEM = pl.BlockSpec(memory_space=pltpu.VMEM)
@@ -33,6 +35,14 @@
         for x in range(N_X)
         for yc in range(N_YC)
     ]
+
+
+def in_plane(yc):
+    return (yc + N_YC - FIRST_YC) % N_YC
+
+
+def in_row(x):
+    return (x + N_X - FIRST_X) % N_X
 
 
 def in_ring(z):
@@ -132,7 +142,7 @@
                 following = flat_ref[pl.ds(row + comps, block // pulses), :]
                 both = jnp.where(lane >= shift, here, following)
                 both = pltpu.roll(both, (LANES - shift) & (LANES - 1), 1)
-                place = ((band & (N_YC - 1)) * Z_HI + (band >> 3)) * block + pulse
+                place = (((band + N_YC - FIRST_YC) & (N_YC - 1)) * Z_HI + (band >> 3)) * block + pulse
                 window_ref[pl.ds(place, block // pulses, stride=pulses), :] = both
         tall = Z_HI * block
         packed_ref[:, tall // EDGE] = jnp.zeros((N_YC, EDGE, LANES), BF16)
@@ -140,7 +150,7 @@
         for side, line, to in ((0, 0, yc + N_YC - 1), (1, EDGE - 1, yc + 1)):
             edge = [edge_ref[side, comp, line : line + 1, :] for comp in range(comps)]
             edge = [e[:, i * LANES : (i + 1) * LANES] for e in edge for i in range(2)]
-            packed_ref[to % N_YC, tall // EDGE] = two_parts(jnp.concatenate(edge, axis=0), spare_ref)
+            packed_ref[in_plane(to), tall // EDGE] = two_parts(jnp.concatenate(edge, axis=0), spare_ref)
         leaving = []
         for to in range(N_YC):
             part = window_ref[to * tall : (to + 1) * tall, :].reshape(tall // EDGE, EDGE, LANES)
@@ -187,8 +197,8 @@
     rows = tiles * EDGE
     tall = sources * rows // 2
 
-    above = joined(window_ref[(yc + N_YC - 1) % N_YC, height])
-    below = joined(window_ref[(yc + 1) % N_YC, height])
+    above = joined(window_ref[in_plane(yc + N_YC - 1), height])
+    below = joined(window_ref[in_plane(yc + 1), height])
     foreign = jnp.where(yc == 0, above, below)
     above = jnp.where(yc > 0, above, jnp.zeros_like(above))
     below = jnp.where(yc < N_YC - 1, below, jnp.zeros_like(below))
@@ -215,7 +225,8 @@
         both = both.reshape(tall // EDGE, EDGE, 2 * band_rows).astype(BF16)
         extra = two_parts(extra, spare_ref)
         for z in range(Z_LO):
-            out_ref[in_ring(z_half * Z_LO + z), : tall // EDGE] = both
+            for source in range(sources):
+                out_ref[in_ring(z_half * Z_LO + z), source] = both[in_plane(source)]
             out_ref[in_ring(z_half * Z_LO + z), tall // EDGE] = extra
 
 
@@ -387,7 +398,7 @@
         for block in range(blocks // 2):
             part = total[block * columns : (block + 1) * columns]
             total_ref[side * (blocks // 2) + block] = part
-            out_ref[side * (blocks // 2) + block, :tiles] = part.reshape(tiles, EDGE, width).astype(
+            out_ref[in_row(side * (blocks // 2) + block), :tiles] = part.reshape(tiles, EDGE, width).astype(
                 BF16
             )
     mine_ref[...] = total_ref[x]
@@ -412,8 +423,8 @@
     out_ref[:, tiles] = jnp.zeros((blocks, EDGE, LANES), BF16)
     after = two_parts(jnp.where(x < N_X - 1, own, left), spare_ref)
     before = two_parts(jnp.where(x > 0, own, right), spare_ref)
-    out_ref[(x + 1) % N_X, tiles] = after
-    out_ref[(x + N_X - 1) % N_X, tiles] = before
+    out_ref[in_row(x + 1), tiles] = after
+    out_ref[in_row(x + N_X - 1), tiles] = before
 
 
 def finish(
@@ -425,14 +436,14 @@
     tall = pad_ref.shape[1]
     total = mine_ref[...]
     for k in range(1, N_X):
-        part = sums_ref[(x + k) % N_X, : columns // EDGE].astype(F32)
+        part = sums_ref[in_row(x + k), : columns // EDGE].astype(F32)
         total = total + part.reshape(total.shape)
     step, weight = rows_ref[STEP : STEP + 1, :1], rows_ref[STEP + 1 : STEP + 2, :1]
     total = (total * step).T.reshape(image_ref.shape)
 
     zero = jnp.zeros((2, LANES), F32)
-    left = joined(sums_ref[(x + N_X - 1) % N_X, columns // EDGE])[2:4]
-    right = joined(sums_ref[(x + 1) % N_X, columns // EDGE])[0:2]
+    left = joined(sums_ref[in_row(x + N_X - 1), columns // EDGE])[2:4]
+    right = joined(sums_ref[in_row(x + 1), columns // EDGE])[0:2]
     side_ref[...] = jnp.zeros_like(side_ref)
     side_ref[0:2, :] = jnp.where(group > 0, left, zero)
     side_ref[2:4, :] = jnp.where(group < Z_LO * N_X - 1, right, zero)
@@ -565,8 +576,10 @@
         ],
         pl.CostEstimate(flops=1 << 24, bytes_accessed=1 << 23, transcendentals=0),
     )
-    in_plane = [[h * N_YC + i for i in range(N_YC)] for h in range(Z_HI)]
-    windows = lax.all_to_all(windows, "band", 0, 0, axis_index_groups=in_plane, tiled=True)
+    planes = [
+        [h * N_YC + (FIRST_YC + i) % N_YC for i in range(N_YC)] for h in range(Z_HI)
+    ]
+    windows = lax.all_to_all(windows, "band", 0, 0, axis_index_groups=planes, tiled=True)
     side, weights = call(
         side_columns,
         (shape((EDGE, LANES), F32), shape((Z_HI, band_rows, window_len), BF16)),
@@ -608,7 +621,9 @@
             pltpu.VMEM((EDGE, LANES), F32),
         ],
     )
-    along_x = [[z * N_X + x for x in range(N_X)] for z in range(Z_LO)]
+    along_x = [
+        [z * N_X + (FIRST_X + k) % N_X for k in range(N_X)] for z in range(Z_LO)
+    ]
     sums = lax.all_to_all(sums, "aper", 0, 0, axis_index_groups=along_x, tiled=True)
     return call(
         finish,

time: 64.1 us -> 62.2 us (0.970)
  the two profiles are of different devices: /device:TPU:32 before, /device:TPU:2 now
where the time goes in v9:
time: 62.2 us; the launch traced here: 61.8 us
  blocking collectives  34.5 us (55%)
  starting transfers between devices  17.2 us (28%)
  Pallas kernels  8.65 us (14%)
  waiting for transfers between devices  1.38 us (2%)
    all_to_all x1, blocking collectives, local(): lax.all_to_all(lifted, ('aper', 'band'), 0, 0, axis_index_groups=z_rings(...  25.4 us
    ppermute x1, starting transfers between devices, local(): other_weight = lax.ppermute(weight, ('aper', 'band'), halves_swapped())  10.6 us
    all_to_all x1, blocking collectives, local(): lax.all_to_all(sums, 'aper', 0, 0, axis_index_groups=along_x, tiled=True)  9.12 us
    all_to_all x1, starting transfers between devices, local(): lax.all_to_all(windows, 'band', 0, 0, axis_index_groups=planes, tiled=True)  6.54 us
    pallas_call x5, Pallas kernels, call(): pl.pallas_call(kernel, out_shape=out_shape, in_specs=in_specs, out_specs=...  6.27 us
    pallas_call x2, Pallas kernels, local(): pl.pallas_call(functools.partial(cut_windows, wanted), out_shape=pltpu.HB...  2.38 us
    all_to_all x1, waiting for transfers between devices, local(): lax.all_to_all(windows, 'band', 0, 0, axis_index_groups=planes, tiled=True)  1.38 us
  transfers between devices with their start and end apart: 2, of which 1 were waited for; matrix products, arithmetic and copies ran while one was open for 0% of the time, Pallas kernels for 5%

profile of v9, /device:TPU:2, one launch (start us, length us, event | category | flops | bytes accessed | tf_op | source)
XLA Modules:
  0.0 61.8 jit_solution(7977259925359507187)
XLA Ops:
  0.0 2.2 %shard_map.82.refs_0_ = bf16[8,17,8,128]{3,2,1,0:T(8,128)(2,1)} custom-call(s32[8,16]{1,0:T(8,128)} %start_hbm.3, s32[8,8]{1,0:T(8,128)} %foot_hbm.3, bf16[2,8,8192]{2,1,0:T(8,128)(2,1)} %pulse_hbm.3, f32[2,64,256]{2,1,0:T(8,128)} %image_ref.1), custom_call_target="tpu_custom_call" | custom-call | tf_op jit(solution)/shard_map/pallas_call | solution.py:526
  2.3 10.6 %collective-permute-start = (bf16[64,512]{1,0:T(8,128)(2,1)}, bf16[64,512]{1,0:T(8,128)(2,1)S(1)}, u32[]{:S(2)}, u32[]{:S(2)}) collective-permute-start(bf16[64,512]{1,0:T(8,128)(2,1)} %weight_hbm.1), channel_id=1, source_target_pairs={{0,264},{1,265},{2,266},{3,267},{4,268},{5,269},{6,270},{7,271},{1... | collective-permute-start | bytes 196616 | tf_op jit(solution)/shard_map/ppermute | solution.py:548
  12.9 0.1 shard_map.83.after_ref
  13.0 6.5 %all-to-all-start = ((bf16[8,17,8,128]{3,2,1,0:T(8,128)(2,1)}), bf16[8,17,8,128]{3,2,1,0:T(8,128)(2,1)S(1)}, u32[]{:S(2)}, u32[]{:S(2)}) async-start(bf16[8,17,8,128]{3,2,1,0:T(8,128)(2,1)} %shard_map.83.after_ref), calls=%async_computation | async-start | bytes 557056 | tf_op jit(solution)/shard_map/all_to_all | solution.py:582
  19.6 2.0 %shard_map.84 = (bf16[512,2304]{1,0:T(8,128)(2,1)S(1)}, f32[2,16,1152]{2,1,0:T(8,128)S(1)}, f32[2,32,1152]{2,1,0:T(8,128)S(1)}, f32[8,128]{1,0:T(8,128)S(1)}) custom-call(bf16[8,17,8,128]{3,2,1,0:T(8,128)(2,1)} %shard_map.83.after_ref, f32[32,128]{1,0:T(8,128)} %bitcast.1, f32[5]{0:T(128)} %taps_hbm.1, f32[2]{0:T(128)} %step_hbm.1), custom_call_target="tpu_custom_call" | custom-call | flops 16777216 | bytes 8388608 | tf_op jit(solution)/shard_map/pallas_call | solution.py:493
  21.6 0.0 collective-permute-done.other_ref
  21.6 1.1 %shard_map.85 = (f32[8,128]{1,0:T(8,128)S(1)}, bf16[2,64,512]{2,1,0:T(8,128)(2,1)S(1)}) custom-call(f32[2,64,256]{2,1,0:T(8,128)} %image_ref.1, bf16[64,512]{1,0:T(8,128)(2,1)} %weight_hbm.1, bf16[64,512]{1,0:T(8,128)(2,1)S(1)} %collective-permute-done.other_ref), custom_call_target="tpu_custom_call" | custom-call | flops 17179869184 | bytes 134217728 | tf_op jit(solution)/shard_map/pallas_call | solution.py:493
  22.7 0.0 copy-start
  22.7 1.4 %all-to-all-done.window_ref = bf16[8,17,8,128]{3,2,1,0:T(8,128)(2,1)S(1)} async-done(((bf16[8,17,8,128]{3,2,1,0:T(8,128)(2,1)}), bf16[8,17,8,128]{3,2,1,0:T(8,128)(2,1)S(1)}, u32[]{:S(2)}, u32[]{:S(2)}) %all-to-all-start) | async-done | bytes 278560 | tf_op jit(solution)/shard_map/all_to_all | solution.py:582
  24.1 0.3 shard_map.86
  24.4 25.4 %all_to_all.15.lifted_ref = bf16[16,9,8,128]{3,2,1,0:T(8,128)(2,1)S(1)} all-to-all(bf16[16,9,8,128]{3,2,1,0:T(8,128)(2,1)S(1)} %get-tuple-element.26), channel_id=1, replica_groups={{8,72,136,200,264,328,392,456,0,64,128,192,256,320,384,448},{9,73,137,2..., dimensions={0} | all-to-all | bytes 589824 | tf_op jit(solution)/shard_map/all_to_all | solution.py:606
  49.8 1.6 %shard_map.87 = (bf16[4,33,8,128]{3,2,1,0:T(8,128)(2,1)S(1)}, f32[256,128]{1,0:T(8,128)S(1)}, f32[8,128]{1,0:T(8,128)S(1)}) custom-call(f32[8,128]{1,0:T(8,128)S(1)} %get-tuple-element.19.after_ref.tap_rows_ref.rows_ref, bf16[512,2304]{1,0:T(8,128)(2,1)S(1)} %get-tuple-element.20.near_ref, f32[2,16,1152]{2,1,0:T(8,128)S(1)} %get-tuple-element.21.fine_ref, ...), custom_call_target="tpu_custom_call" | custom-call | tf_op jit(solution)/shard_map/pallas_call | solution.py:493
  51.4 9.1 %all_to_all.16.sums_ref = bf16[4,33,8,128]{3,2,1,0:T(8,128)(2,1)S(1)} all-to-all(bf16[4,33,8,128]{3,2,1,0:T(8,128)(2,1)S(1)} %get-tuple-element.28), channel_id=1, replica_groups={{32,48,0,16},{96,112,64,80},{160,176,128,144},{224,240,192,208},{288,30..., dimensions={0} | all-to-all | bytes 540672 | tf_op jit(solution)/shard_map/all_to_all | solution.py:627
  60.5 0.0 copy-done
  60.5 1.2 %shard_map.88 = f32[2,64,256]{2,1,0:T(8,128)} custom-call(f32[8,128]{1,0:T(8,128)S(1)} %get-tuple-element.19.after_ref.tap_rows_ref.rows_ref, bf16[4,33,8,128]{3,2,1,0:T(8,128)(2,1)S(1)} %all_to_all.16.sums_ref, f32[256,128]{1,0:T(8,128)S(1)} %get-tuple-element.29.mine_ref, f32[8,128]{1,0:T(8,128)S(1)} %get-tuple-element.30.edge_ref, f32[2,64,256]{2,1,0:T(8,128)S(1)} %copy-done), custom_call_target="tpu_custom_call" | custom-call | tf_op jit(solution)/shard_map/pallas_call | solution.py:493
Async XLA Ops:
  2.3 19.4 %collective-permute-start = (bf16[64,512]{1,0:T(8,128)(2,1)}, bf16[64,512]{1,0:T(8,128)(2,1)S(1)}, u32[]{:S(2)}, u32[]{:S(2)}) collective-permute-start(bf16[64,512]{1,0:T(8,128)(2,1)} %weight_hbm.1), channel_id=1, source_target_pairs={{0,264},{1,265},{2,266},{3,267},{4,268},{5,269},{6,270},{7,271},{1... | collective-permute-start | bytes 196616 | tf_op jit(solution)/shard_map/ppermute | solution.py:548
  13.0 11.1 %all-to-all-start = ((bf16[8,17,8,128]{3,2,1,0:T(8,128)(2,1)}), bf16[8,17,8,128]{3,2,1,0:T(8,128)(2,1)S(1)}, u32[]{:S(2)}, u32[]{:S(2)}) async-start(bf16[8,17,8,128]{3,2,1,0:T(8,128)(2,1)} %shard_map.83.after_ref), calls=%async_computation | async-start | bytes 557056 | tf_op jit(solution)/shard_map/all_to_all | solution.py:582
  22.7 37.8 %copy-start = (f32[2,64,256]{2,1,0:T(8,128)S(1)}, f32[2,64,256]{2,1,0:T(8,128)}, u32[]{:S(2)}) copy-start(f32[2,64,256]{2,1,0:T(8,128)} %image_ref.1) | copy-start | bytes 393220

commit v10 on v9

--- a/solution.py
+++ b/solution.py
@@ -14,7 +14,7 @@
 Z_HI, Z_LO, N_X, N_YC = 2, 8, 4, 8
 N_Z = Z_HI * Z_LO
 FIRST_Z = 8
-FIRST_YC = 4
+FIRST_YC = 5
 FIRST_X = 2
 smooth_eps = 0.05
 BF16, F32 = jnp.bfloat16, jnp.float32

time: 62.2 us -> 60.9 us (0.979)
  the two profiles are of different devices: /device:TPU:2 before, /device:TPU:18 now
where the time goes in v10:
time: 60.9 us; the launch traced here: 60.5 us
  blocking collectives  34.1 us (56%)
  starting transfers between devices  14 us (23%)
  Pallas kernels  8.64 us (14%)
  waiting for transfers between devices  3.71 us (6%)
    all_to_all x1, blocking collectives, local(): lax.all_to_all(lifted, ('aper', 'band'), 0, 0, axis_index_groups=z_rings(...  25 us
    ppermute x1, starting transfers between devices, local(): other_weight = lax.ppermute(weight, ('aper', 'band'), halves_swapped())  10.6 us
    all_to_all x1, blocking collectives, local(): lax.all_to_all(sums, 'aper', 0, 0, axis_index_groups=along_x, tiled=True)  9.12 us
    pallas_call x5, Pallas kernels, call(): pl.pallas_call(kernel, out_shape=out_shape, in_specs=in_specs, out_specs=...  6.26 us
    all_to_all x1, waiting for transfers between devices, local(): lax.all_to_all(windows, 'band', 0, 0, axis_index_groups=planes, tiled=True)  3.4 us
    all_to_all x1, starting transfers between devices, local(): lax.all_to_all(windows, 'band', 0, 0, axis_index_groups=planes, tiled=True)  3.38 us
    pallas_call x2, Pallas kernels, local(): pl.pallas_call(functools.partial(cut_windows, wanted), out_shape=pltpu.HB...  2.38 us
  transfers between devices with their start and end apart: 2, of which 2 were waited for; matrix products, arithmetic and copies ran while one was open for 0% of the time, Pallas kernels for 5%

profile of v10, /device:TPU:18, one launch (start us, length us, event | category | flops | bytes accessed | tf_op | source)
XLA Modules:
  0.0 60.5 jit_solution(4493161397089603141)
XLA Ops:
  0.0 2.2 %shard_map.82.refs_0_ = bf16[8,17,8,128]{3,2,1,0:T(8,128)(2,1)} custom-call(s32[8,16]{1,0:T(8,128)} %start_hbm.3, s32[8,8]{1,0:T(8,128)} %foot_hbm.3, bf16[2,8,8192]{2,1,0:T(8,128)(2,1)} %pulse_hbm.3, f32[2,64,256]{2,1,0:T(8,128)} %image_ref.1), custom_call_target="tpu_custom_call" | custom-call | tf_op jit(solution)/shard_map/pallas_call | solution.py:526
  2.3 10.6 %collective-permute-start = (bf16[64,512]{1,0:T(8,128)(2,1)}, bf16[64,512]{1,0:T(8,128)(2,1)S(1)}, u32[]{:S(2)}, u32[]{:S(2)}) collective-permute-start(bf16[64,512]{1,0:T(8,128)(2,1)} %weight_hbm.1), channel_id=1, source_target_pairs={{0,264},{1,265},{2,266},{3,267},{4,268},{5,269},{6,270},{7,271},{1... | collective-permute-start | bytes 196616 | tf_op jit(solution)/shard_map/ppermute | solution.py:548
  12.9 0.1 shard_map.83.after_ref
  13.0 3.4 %all-to-all-start = ((bf16[8,17,8,128]{3,2,1,0:T(8,128)(2,1)}), bf16[8,17,8,128]{3,2,1,0:T(8,128)(2,1)S(1)}, u32[]{:S(2)}, u32[]{:S(2)}) async-start(bf16[8,17,8,128]{3,2,1,0:T(8,128)(2,1)} %shard_map.83.after_ref), calls=%async_computation | async-start | bytes 557056 | tf_op jit(solution)/shard_map/all_to_all | solution.py:582
  16.4 2.1 %shard_map.84 = (bf16[512,2304]{1,0:T(8,128)(2,1)S(1)}, f32[2,16,1152]{2,1,0:T(8,128)S(1)}, f32[2,32,1152]{2,1,0:T(8,128)S(1)}, f32[8,128]{1,0:T(8,128)S(1)}) custom-call(bf16[8,17,8,128]{3,2,1,0:T(8,128)(2,1)} %shard_map.83.after_ref, f32[32,128]{1,0:T(8,128)} %bitcast.1, f32[5]{0:T(128)} %taps_hbm.1, f32[2]{0:T(128)} %step_hbm.1), custom_call_target="tpu_custom_call" | custom-call | flops 16777216 | bytes 8388608 | tf_op jit(solution)/shard_map/pallas_call | solution.py:493
  18.5 0.3 collective-permute-done.other_ref
  18.8 1.1 %shard_map.85 = (f32[8,128]{1,0:T(8,128)S(1)}, bf16[2,64,512]{2,1,0:T(8,128)(2,1)S(1)}) custom-call(f32[2,64,256]{2,1,0:T(8,128)} %image_ref.1, bf16[64,512]{1,0:T(8,128)(2,1)} %weight_hbm.1, bf16[64,512]{1,0:T(8,128)(2,1)S(1)} %collective-permute-done.other_ref), custom_call_target="tpu_custom_call" | custom-call | flops 17179869184 | bytes 134217728 | tf_op jit(solution)/shard_map/pallas_call | solution.py:493
  19.8 0.0 copy-start
  19.8 3.4 %all-to-all-done.window_ref = bf16[8,17,8,128]{3,2,1,0:T(8,128)(2,1)S(1)} async-done(((bf16[8,17,8,128]{3,2,1,0:T(8,128)(2,1)}), bf16[8,17,8,128]{3,2,1,0:T(8,128)(2,1)S(1)}, u32[]{:S(2)}, u32[]{:S(2)}) %all-to-all-start) | async-done | bytes 278560 | tf_op jit(solution)/shard_map/all_to_all | solution.py:582
  23.2 0.3 shard_map.86
  23.5 25.0 %all_to_all.15.lifted_ref = bf16[16,9,8,128]{3,2,1,0:T(8,128)(2,1)S(1)} all-to-all(bf16[16,9,8,128]{3,2,1,0:T(8,128)(2,1)S(1)} %get-tuple-element.26), channel_id=1, replica_groups={{8,72,136,200,264,328,392,456,0,64,128,192,256,320,384,448},{9,73,137,2..., dimensions={0} | all-to-all | bytes 589824 | tf_op jit(solution)/shard_map/all_to_all | solution.py:606
  48.5 1.6 %shard_map.87 = (bf16[4,33,8,128]{3,2,1,0:T(8,128)(2,1)S(1)}, f32[256,128]{1,0:T(8,128)S(1)}, f32[8,128]{1,0:T(8,128)S(1)}) custom-call(f32[8,128]{1,0:T(8,128)S(1)} %get-tuple-element.19.after_ref.tap_rows_ref.rows_ref, bf16[512,2304]{1,0:T(8,128)(2,1)S(1)} %get-tuple-element.20.near_ref, f32[2,16,1152]{2,1,0:T(8,128)S(1)} %get-tuple-element.21.fine_ref, ...), custom_call_target="tpu_custom_call" | custom-call | tf_op jit(solution)/shard_map/pallas_call | solution.py:493
  50.1 9.1 %all_to_all.16.sums_ref = bf16[4,33,8,128]{3,2,1,0:T(8,128)(2,1)S(1)} all-to-all(bf16[4,33,8,128]{3,2,1,0:T(8,128)(2,1)S(1)} %get-tuple-element.28), channel_id=1, replica_groups={{32,48,0,16},{96,112,64,80},{160,176,128,144},{224,240,192,208},{288,30..., dimensions={0} | all-to-all | bytes 540672 | tf_op jit(solution)/shard_map/all_to_all | solution.py:627
  59.3 0.0 copy-done
  59.3 1.2 %shard_map.88 = f32[2,64,256]{2,1,0:T(8,128)} custom-call(f32[8,128]{1,0:T(8,128)S(1)} %get-tuple-element.19.after_ref.tap_rows_ref.rows_ref, bf16[4,33,8,128]{3,2,1,0:T(8,128)(2,1)S(1)} %all_to_all.16.sums_ref, f32[256,128]{1,0:T(8,128)S(1)} %get-tuple-element.29.mine_ref, f32[8,128]{1,0:T(8,128)S(1)} %get-tuple-element.30.edge_ref, f32[2,64,256]{2,1,0:T(8,128)S(1)} %copy-done), custom_call_target="tpu_custom_call" | custom-call | tf_op jit(solution)/shard_map/pallas_call | solution.py:493
Async XLA Ops:
  2.3 16.5 %collective-permute-start = (bf16[64,512]{1,0:T(8,128)(2,1)}, bf16[64,512]{1,0:T(8,128)(2,1)S(1)}, u32[]{:S(2)}, u32[]{:S(2)}) collective-permute-start(bf16[64,512]{1,0:T(8,128)(2,1)} %weight_hbm.1), channel_id=1, source_target_pairs={{0,264},{1,265},{2,266},{3,267},{4,268},{5,269},{6,270},{7,271},{1... | collective-permute-start | bytes 196616 | tf_op jit(solution)/shard_map/ppermute | solution.py:548
  13.0 10.2 %all-to-all-start = ((bf16[8,17,8,128]{3,2,1,0:T(8,128)(2,1)}), bf16[8,17,8,128]{3,2,1,0:T(8,128)(2,1)S(1)}, u32[]{:S(2)}, u32[]{:S(2)}) async-start(bf16[8,17,8,128]{3,2,1,0:T(8,128)(2,1)} %shard_map.83.after_ref), calls=%async_computation | async-start | bytes 557056 | tf_op jit(solution)/shard_map/all_to_all | solution.py:582
  19.8 39.4 %copy-start = (f32[2,64,256]{2,1,0:T(8,128)S(1)}, f32[2,64,256]{2,1,0:T(8,128)}, u32[]{:S(2)}) copy-start(f32[2,64,256]{2,1,0:T(8,128)} %image_ref.1) | copy-start | bytes 393220
